TPU v7x, 128 devices: a whole 4x4x4 slice. The times are simulated.
128 devices in a mesh: samp: 4 (over y_hi, core), row: 32 (over y_lo, x, z).
Axes of the slice: x: 4, y: 4 (y_hi: 2, y_lo: 2; y = y_hi * 2 + y_lo), z: 4, core: 2. Of those that a mesh axis runs over, the one named last changes fastest.
Arguments:
- queries: bfloat16 [8, 2048, 768], P('samp', 'row'), may hold values from -6 to 6
- keys: bfloat16 [8, 2048, 768], P('samp', 'row'), may hold values from -6 to 6
- values: bfloat16 [8, 2048, 768], P('samp', 'row'), may hold values from -6 to 6
- out_grad: bfloat16 [8, 2048, 768], P('samp', 'row'), may hold values from -6 to 6
- pair_repr: bfloat16 [2048, 2048, 128], P('row', 'samp'), may hold values from -6 to 6
- norm_gain: float32 [128], replicated, may hold values from 0.25 to 1.75
- bias_weight: bfloat16 [128, 16], replicated, may hold values from -0.5 to 0.5
- token_mask: int32 [2048], replicated, may hold values 0 or 1
Outputs:
- grad_queries: bfloat16 [8, 2048, 768], P('samp', 'row')
- grad_keys: bfloat16 [8, 2048, 768], P('samp', 'row')
- grad_values: bfloat16 [8, 2048, 768], P('samp', 'row')
- grad_pair: bfloat16 [2048, 2048, 128], P('row', 'samp')
- grad_weight: float32 [128, 16], replicated
- grad_gain: float32 [128], replicated
All inputs are finite; a program needn't handle non-finite values.
Results may differ from a plain program's by a relative error of at most 0.03.
Values may be sent and summed in bfloat16 or wider, within the bound.
A program may use at most 320 MiB of HBM per device.

v0:
```python
import math

import jax
import jax.numpy as jnp
from jax import lax
from jax.sharding import PartitionSpec as P


def layer_stats(pair_rows, norm_gain):
    entries = pair_rows.astype(jnp.float32)
    average = jnp.mean(entries, -1, keepdims=True)
    centred = entries - average
    variance = jnp.mean(centred * centred, -1, keepdims=True)
    inverse = lax.rsqrt(variance + 1e-05)
    standard = centred * inverse
    normed = (standard * norm_gain).astype(jnp.bfloat16)
    return (standard, inverse, normed)


def project_bias(normed, bias_weight):
    return jnp.einsum(
        "rjc,ch->hrj", normed, bias_weight, preferred_element_type=jnp.float32
    ).astype(jnp.bfloat16)


def attend(query_block, keys_all, values_all, grad_block, pair_bias, key_keep, inv_root):
    samp_count, row_count, model_width = query_block.shape
    head_count = pair_bias.shape[0]
    head_size = model_width // head_count
    query_heads = query_block.reshape(samp_count, row_count, head_count, head_size)
    grad_heads = grad_block.reshape(samp_count, row_count, head_count, head_size)
    key_heads = keys_all.reshape(samp_count, -1, head_count, head_size)
    value_heads = values_all.reshape(samp_count, -1, head_count, head_size)
    scores = (
        jnp.einsum("srhe,sjhe->shrj", query_heads, key_heads, preferred_element_type=jnp.float32)
        * inv_root
    )
    scores = scores + pair_bias.astype(jnp.float32)[None]
    scores = jnp.where(key_keep[None, None, None, :], scores, -1000000000.0)
    row_top = jnp.max(scores, -1, keepdims=True)
    raised = jnp.exp(scores - row_top)
    probs = raised / jnp.sum(raised, -1, keepdims=True)
    probs_low = probs.astype(jnp.bfloat16)
    grad_prob = jnp.einsum(
        "srhe,sjhe->shrj", grad_heads, value_heads, preferred_element_type=jnp.float32
    )
    row_along = jnp.sum(probs * grad_prob, -1, keepdims=True)
    grad_score = probs * (grad_prob - row_along)
    score_low = grad_score.astype(jnp.bfloat16)
    grad_query = (
        jnp.einsum("shrj,sjhe->srhe", score_low, key_heads, preferred_element_type=jnp.float32)
        * inv_root
    )
    grad_query = grad_query.astype(jnp.bfloat16).reshape(samp_count, row_count, model_width)
    return (grad_query, probs_low, score_low, jnp.sum(grad_score, 0))


def key_terms(score_low, probs_low, query_block, grad_block, inv_root, row_total):
    samp_count, row_count, model_width = query_block.shape
    head_count = score_low.shape[1]
    query_heads = query_block.reshape(samp_count, row_count, head_count, model_width // head_count)
    grad_heads = grad_block.reshape(samp_count, row_count, head_count, model_width // head_count)
    grad_key = (
        jnp.einsum("shrj,srhe->jshe", score_low, query_heads, preferred_element_type=jnp.float32)
        * inv_root
    )
    grad_value = jnp.einsum(
        "shrj,srhe->jshe", probs_low, grad_heads, preferred_element_type=jnp.float32
    )
    stacked = jnp.stack((grad_key, grad_value), axis=2)
    return stacked.reshape(row_total, -1)


def split_grads(summed, samp_count, model_width):
    shaped = summed.reshape(summed.shape[0], samp_count, 2, model_width)
    grad_key = shaped[:, :, 0, :].transpose(1, 0, 2).astype(jnp.bfloat16)
    grad_value = shaped[:, :, 1, :].transpose(1, 0, 2).astype(jnp.bfloat16)
    return (grad_key, grad_value)


def on_device(queries, keys, values, out_grad, pair_repr, norm_gain, bias_weight, token_mask):
    samp_count, row_count, model_width = queries.shape
    head_count = bias_weight.shape[1]
    inv_root = 1.0 / math.sqrt(model_width // head_count)
    key_keep = token_mask > 0
    standard, inverse, normed = layer_stats(pair_repr, norm_gain)
    pair_bias = lax.all_gather(project_bias(normed, bias_weight), "samp", axis=2, tiled=True)
    keys_all, values_all = (
        lax.all_gather(keys, "row", axis=1, tiled=True),
        lax.all_gather(values, "row", axis=1, tiled=True),
    )
    grad_queries, probs_low, score_low, grad_bias = attend(
        queries, keys_all, values_all, out_grad, pair_bias, key_keep, inv_root
    )
    summed = lax.psum_scatter(
        key_terms(
            score_low, probs_low, queries, out_grad, inv_root, row_count * lax.axis_size("row")
        ).astype(jnp.bfloat16),
        "row",
        scatter_dimension=0,
        tiled=True,
    ).astype(jnp.float32)
    grad_keys, grad_values = split_grads(summed, samp_count, model_width)
    bias_low = grad_bias.astype(jnp.bfloat16)
    bias_own = (
        lax.psum_scatter(bias_low, "samp", scatter_dimension=2, tiled=True)
        .astype(jnp.float32)
        .astype(jnp.bfloat16)
    )
    grad_normed = jnp.einsum(
        "hrj,ch->rjc", bias_own, bias_weight, preferred_element_type=jnp.float32
    )
    grad_weight = jnp.einsum("rjc,hrj->ch", normed, bias_own, preferred_element_type=jnp.float32)
    grad_gain = jnp.sum(grad_normed * standard, (0, 1))
    scaled = grad_normed * norm_gain
    grad_pair = inverse * (
        scaled
        - jnp.mean(scaled, -1, keepdims=True)
        - standard * jnp.mean(scaled * standard, -1, keepdims=True)
    )
    grad_weight, grad_gain = lax.psum((grad_weight, grad_gain), ("samp", "row"))
    return (
        grad_queries,
        grad_keys,
        grad_values,
        grad_pair.astype(jnp.bfloat16),
        grad_weight,
        grad_gain,
    )


def solution(mesh):
    placed = (
        P("samp", "row", None),
        P("samp", "row", None),
        P("samp", "row", None),
        P("samp", "row", None),
        P("row", "samp", None),
        P(),
        P(),
        P(),
    )
    return jax.shard_map(
        on_device,
        mesh=mesh,
        in_specs=placed,
        out_specs=(
            P("samp", "row", None),
            P("samp", "row", None),
            P("samp", "row", None),
            P("row", "samp", None),
            P(),
            P(),
        ),
        check_vma=False,
    )
```

profile of v0, /device:TPU:10, one launch (start us, length us, event | category | flops | bytes accessed | tf_op | source)
XLA Modules:
  0.0 692.0 jit_solution(569014779296191123)
XLA Ops:
  7.2 0.0 copy-start
  7.2 0.0 copy-start.4
  7.2 0.0 all-gather.6.cloned.1.call-start
  7.2 11.9 %copy.60 = bf16[64,512,128]{1,2,0:T(8,128)(2,1)} copy(bf16[64,512,128]{2,1,0:T(8,128)(2,1)} %param.12) | data formatting | bytes 16777216 | tf_op args[4]
  19.2 5.6 convert_reduce_fusion
  24.8 0.0 slice-start.1
  24.8 6.8 fusion.13
  31.7 0.0 copy-done
  31.7 0.0 copy-done.4
  31.7 3.6 fusion.28
  35.3 0.0 all-gather.6.cloned.1.call-update
  35.3 0.0 all-gather.4.cloned.1.call-start
  35.3 0.7 all-gather.4.cloned.1.call-update
  36.0 0.0 all-gather.8.cloned.1.call-start
  36.1 0.7 all-gather.8.cloned.1.call-update
  36.8 0.2 reduce-scatter.5.cloned.1.call-start
  37.0 0.2 copy.81
  37.3 0.2 copy.82
  37.5 37.8 %all-gather.6.cloned.1.call-done = bf16[16,64,2048]{2,0,1:T(8,128)(2,1)} async-done(((bf16[16,64,512]{2,0,1:T(8,128)(2,1)}), bf16[16,64,2048]{2,0,1:T(8,128)(2,1)}) %all-gather.6.cloned.1.call-update) | async-done | bytes 4194320 | tf_op jit(solution)/shard_map/all_gather | solution.py:87
  75.3 8.0 %copy.62 = f32[16,64,2048]{2,1,0:T(8,128)} copy(bf16[16,64,2048]{2,0,1:T(8,128)(2,1)} %all-gather.6.cloned.1.call-done) | data formatting | bytes 12582912 | tf_op jit(solution)/shard_map/convert_element_type | solution.py:38
  83.4 151.0 %all-gather.4.cloned.1.call-done = bf16[2,2048,768]{2,1,0:T(8,128)(2,1)} async-done(((bf16[2,64,768]{2,1,0:T(8,128)(2,1)}), bf16[2,2048,768]{2,1,0:T(8,128)(2,1)}) %all-gather.4.cloned.1.call-update) | async-done | bytes 6291472 | tf_op jit(solution)/shard_map/all_gather | solution.py:89
  234.3 8.7 %copy.58 = bf16[2,2048,768]{1,2,0:T(8,128)(2,1)} copy(bf16[2,2048,768]{2,1,0:T(8,128)(2,1)} %all-gather.4.cloned.1.call-done) | data formatting | bytes 12582912 | tf_op jit(solution)/shard_map/all_gather | solution.py:89
  243.1 12.8 %fusion.44 = (f32[2,16,64]{2,1,0:T(8,128)S(1)}, f32[2,16,64,2048]{3,2,1,0:T(8,128)}) fusion(f32[16,64,2048]{2,1,0:T(8,128)} %copy.62, pred[2048]{0:T(1024)(128)(4,1)S(1)} %broadcast_compare_fusion, bf16[2,64,16,48]{1,3,2,0:T(8,128)(2,1)S(1)} %bitcast.52, bf16[2,2048,16,48]{1,3,2,0:T(8,128)(2,1)} %bitcast.49), kind=kOutput, calls=%fused_computation.55 | convolution fusion | flops 423626752 | bytes 31664128 | tf_op jit(solution)/shard_map/sub | solution.py:41
  255.8 144.1 %all-gather.8.cloned.1.call-done = bf16[2,2048,768]{2,1,0:T(8,128)(2,1)} async-done(((bf16[2,64,768]{2,1,0:T(8,128)(2,1)}), bf16[2,2048,768]{2,1,0:T(8,128)(2,1)}) %all-gather.8.cloned.1.call-update) | async-done | bytes 6291472 | tf_op jit(solution)/shard_map/all_gather | solution.py:90
  400.0 8.6 %copy.63 = bf16[2,2048,768]{1,2,0:T(8,128)(2,1)} copy(bf16[2,2048,768]{2,1,0:T(8,128)(2,1)} %all-gather.8.cloned.1.call-done) | data formatting | bytes 12582912 | tf_op jit(solution)/shard_map/all_gather | solution.py:90
  408.6 14.3 %multiply_reduce_fusion = (f32[2,16,64]{2,1,0:T(8,128)S(1)}, f32[2,16,64,2048]{3,2,1,0:T(8,128)}) fusion(f32[2,16,64,2048]{3,2,1,0:T(8,128)} %get-tuple-element.40, f32[2,16,64]{2,1,0:T(8,128)S(1)} %get-tuple-element.39, bf16[2,64,16,48]{1,3,2,0:T(8,128)(2,1)S(1)} %bitcast.55, bf16[2,2048,16,48]{1,3,2,0:T(8,128)(2,1)} %bitcast.51), kind=kOutput, calls=%fused_computation.17 | convolution fusion | flops 415234048 | bytes 40058880 | tf_op jit(solution)/shard_map/srhe,sjhe->shrj/dot_general | solution.py:44
  422.9 18.1 %fusion.21 = (bf16[16,64,2048]{2,1,0:T(8,128)(2,1)}, bf16[2,16,64,2048]{3,2,1,0:T(8,128)(2,1)}) fusion(f32[2,16,64,2048]{3,2,1,0:T(8,128)} %get-tuple-element.42, f32[2,16,64]{2,1,0:T(8,128)S(1)} %get-tuple-element.41, f32[2,16,64,2048]{3,2,1,0:T(8,128)} %get-tuple-element.40, f32[2,16,64]{2,1,0:T(8,128)S(1)} %get-tuple-element.39), kind=kLoop, calls=%fused_computation.31 | loop fusion | flops 18874368 | bytes 46153728 | tf_op jit(solution)/shard_map/reduce_sum | solution.py:55
  441.0 0.0 reduce-scatter.5.cloned.1.call-update
  441.0 0.0 reduce-scatter.7.cloned.1.call-start
  441.1 5.2 fusion.23
  446.2 10.5 %convert_bitcast_fusion = bf16[2048,2,1,16,48]{0,4,3,1,2:T(8,128)(2,1)} fusion(bf16[2,64,16,48]{1,3,2,0:T(8,128)(2,1)S(1)} %bitcast.56, f32[2,16,64,2048]{3,2,1,0:T(8,128)} %get-tuple-element.40, f32[2,16,64]{2,1,0:T(8,128)S(1)} %get-tuple-element.39), kind=kOutput, calls=%fused_computation.34 | convolution fusion | flops 414187520 | bytes 23273472 | tf_op jit(solution)/shard_map/shrj,srhe->jshe/dot_general | solution.py:67
  456.7 5.3 pad_maximum_fusion
  462.0 5.2 copy.67
  467.2 15.7 %copy.79 = bf16[2048,3072]{1,0:T(8,128)(2,1)} copy(bf16[2048,3072]{0,1:T(8,128)(2,1)} %bitcast.48) | data formatting | bytes 25165824
  482.9 0.0 reduce-scatter.7.cloned.1.call-update
  483.0 7.6 %fusion.32 = bf16[2,16,64,48]{2,3,1,0:T(8,128)(2,1)S(1)} fusion(bf16[2,16,64,2048]{3,2,1,0:T(8,128)(2,1)} %get-tuple-element.36, bf16[2,2048,16,48]{1,3,2,0:T(8,128)(2,1)} %bitcast.50), kind=kOutput, calls=%fused_computation.40 | convolution fusion | flops 402849792 | bytes 14876672 | tf_op jit(solution)/shard_map/shrj,sjhe->srhe/dot_general | solution.py:51
  490.6 0.9 copy.74
  491.4 7.0 %reduce-scatter.5.cloned.1.call-done = bf16[16,64,512]{2,1,0:T(8,128)(2,1)} async-done(((bf16[16,64,2048]{2,1,0:T(8,128)(2,1)}), bf16[16,64,512]{2,1,0:T(8,128)(2,1)}) %reduce-scatter.5.cloned.1.call-update) | async-done | bytes 1048592 | tf_op jit(solution)/shard_map/reduce_scatter | solution.py:106
  498.4 9.7 %fusion.12 = (f32[128]{0:T(128)S(1)}, f32[64,512]{1,0:T(8,128)S(1)}, f32[64,512]{1,0:T(8,128)S(1)}, f32[64,512,128]{1,2,0:T(8,128)S(1)}) fusion(bf16[64,512,128]{1,2,0:T(8,128)(2,1)} %copy.60, f32[64,512]{1,0:T(8,128)S(1)} %add_rsqrt_fusion, f32[64,512]{1,0:T(8,128)S(1)} %broadcast_multiply_fusion.2, f32[128]{0:T(128)S(1)} %copy-done.4, ...), kind=kOutput, calls=%fused_computation.14 | convolution fusion | flops 171900800 | bytes 26743808 | tf_op jit(solution)/shard_map/hrj,ch->rjc/dot_general | solution.py:110
  508.1 10.1 %fusion.11 = bf16[64,512,128]{1,2,0:T(8,128)(2,1)} fusion(bf16[64,512,128]{1,2,0:T(8,128)(2,1)} %copy.60, f32[64,512,128]{1,2,0:T(8,128)S(1)} %get-tuple-element.43, f32[64,512]{1,0:T(8,128)S(1)} %get-tuple-element.44, f32[64,512]{1,0:T(8,128)S(1)} %get-tuple-element.45, f32[128]{0:T(128)S(1)} %copy-done.4, f32[64,512]{1,0:T(8,128)S(1)} %add_rsqrt_fusion, ...), kind=kLoop, calls=%fused_computation.13 | loop fusion | flops 37748736 | bytes 34079232 | tf_op jit(solution)/shard_map/convert_element_type | solution.py:126
  518.2 12.0 %copy.75 = bf16[64,512,128]{2,1,0:T(8,128)(2,1)} copy(bf16[64,512,128]{1,2,0:T(8,128)(2,1)} %fusion.11) | data formatting | bytes 16777216
  530.2 5.8 fusion.33
  536.0 71.3 %all-reduce = (f32[128,16]{0,1:T(8,128)}, f32[128]{0:T(128)}) all-reduce(f32[128,16]{0,1:T(8,128)S(1)} %fusion.33, f32[128]{0:T(128)S(1)} %get-tuple-element.30), channel_id=1, replica_groups=mesh['samp'=4,'row'=32] {'samp','row'}, use_global_device_ids=true, to_apply=%region_10.11 | all-reduce | flops 2176 | bytes 17408 | tf_op jit(solution)/shard_map/psum | solution.py:121
  607.4 75.0 %reduce-scatter.7.cloned.1.call-done = bf16[64,3072]{1,0:T(8,128)(2,1)} async-done(((bf16[2048,3072]{1,0:T(8,128)(2,1)}), bf16[64,3072]{1,0:T(8,128)(2,1)}) %reduce-scatter.7.cloned.1.call-update) | async-done | bytes 393232
  682.4 1.4 copy.80
  683.8 0.1 fusion.43
  683.8 0.9 copy.69
  684.7 0.8 copy.70
  (16 shorter events, 0.1 us)
Async XLA Ops:
  7.2 24.5 %copy-start = (bf16[128,16]{0,1:T(8,128)(2,1)S(1)}, bf16[128,16]{0,1:T(8,128)(2,1)}, u32[]{:S(2)}) copy-start(bf16[128,16]{0,1:T(8,128)(2,1)} %param.14) | copy-start | bytes 12292
  7.2 24.5 %copy-start.4 = (f32[128]{0:T(128)S(1)}, f32[128]{0:T(128)}, u32[]{:S(2)}) copy-start(f32[128]{0:T(128)} %param.13) | copy-start | bytes 1540
  7.2 68.2 %all-gather.6.cloned.1.call-start = ((), (), s32[]{:S(2)}) async-start(), calls=%async_computation.3 | async-start | bytes 5242880 | tf_op jit(solution)/shard_map/all_gather | solution.py:87
  19.2 12.5 %slice-start = ((s8[8388608]{0:T(1024)(128)(4,1)}), s8[4194304]{0:T(1024)(128)(4,1)S(1)}, s32[]{:S(2)}) async-start(s8[8388608]{0:T(1024)(128)(4,1)} %bitcast.46), calls=%async_computation.7 | async-start | bytes 8388608
  19.2 17.8 %copy-start.1 = (bf16[2,64,768]{2,1,0:T(8,128)(2,1)S(1)}, bf16[2,64,768]{2,1,0:T(8,128)(2,1)}, u32[]{:S(2)}) copy-start(bf16[2,64,768]{2,1,0:T(8,128)(2,1)} %param.8) | copy-start | bytes 589828
  19.2 18.1 %copy-start.2 = (bf16[2,64,768]{2,1,0:T(8,128)(2,1)S(1)}, bf16[2,64,768]{2,1,0:T(8,128)(2,1)}, u32[]{:S(2)}) copy-start(bf16[2,64,768]{2,1,0:T(8,128)(2,1)} %param.11) | copy-start | bytes 589828
  19.2 18.3 %copy-start.3 = (s32[2048]{0:T(1024)S(1)}, s32[2048]{0:T(1024)}, u32[]{:S(2)}) copy-start(s32[2048]{0:T(1024)} %param.15) | copy-start | bytes 24580
  24.8 6.9 slice-start.1
  35.3 199.0 %all-gather.4.cloned.1.call-start = ((), (), s32[]{:S(2)}) async-start(), calls=%async_computation.2 | async-start | bytes 6488064 | tf_op jit(solution)/shard_map/all_gather | solution.py:89
  36.0 363.9 %all-gather.8.cloned.1.call-start = ((), (), s32[]{:S(2)}) async-start(), calls=%async_computation.4 | async-start | bytes 6488064 | tf_op jit(solution)/shard_map/all_gather | solution.py:90
  36.8 461.6 %reduce-scatter.5.cloned.1.call-start = ((), (), s32[]{:S(2)}) async-start(), calls=%async_computation.5 | async-start | bytes 5242880 | tf_op jit(solution)/shard_map/reduce_scatter | solution.py:106
  441.0 241.4 %reduce-scatter.7.cloned.1.call-start = ((), (), s32[]{:S(2)}) async-start(), calls=%async_computation.6 | async-start | bytes 12976128
  518.2 12.0 %copy-start.5 = (bf16[16,64,512]{2,1,0:T(8,128)(2,1)S(1)}, bf16[16,64,512]{2,1,0:T(8,128)(2,1)}, u32[]{:S(2)}) copy-start(bf16[16,64,512]{2,1,0:T(8,128)(2,1)} %reduce-scatter.5.cloned.1.call-done) | copy-start | bytes 3145732
Sparse Core Ops, SparseCore 0:
  35.4 39.8 all-gather.5
  77.0 157.2 all-gather.3
  236.0 163.9 all-gather.7
  441.1 57.2 reduce-scatter.4
  500.8 181.5 reduce-scatter.6
where the time goes:
time: 702 us; the launch traced here: 692 us
  waiting for transfers between devices  416 us (59%)
  local copies, waits for them, and re-layouts  74.7 us (11%)
  blocking collectives  71.3 us (10%)
  matrix products  69.4 us (10%)
  other arithmetic  45.9 us (7%)
  between operations  14 us (2%)
    all_gather x1, waiting for transfers between devices, on_device(): lax.all_gather(keys, 'row', axis=1, tiled=True)  151 us
    all_gather x1, waiting for transfers between devices, on_device(): lax.all_gather(values, 'row', axis=1, tiled=True)  144 us
    unnamed x6, waiting for transfers between devices  76.4 us
    psum x1, blocking collectives, on_device(): grad_weight, grad_gain = lax.psum((grad_weight, grad_gain), ('samp', 'row'))  71.3 us
    unnamed x21, local copies, waits for them, and re-layouts  42 us
    all_gather x1, waiting for transfers between devices, on_device(): lax.all_gather(project_bias(normed, bias_weight), 'samp', axis=2, tiled=T...  37.8 us
    reduce_sum x1, other arithmetic, attend(): return (grad_query, probs_low, score_low, jnp.sum(grad_score, 0))  18.1 us
    dot_general x1, matrix products, attend(): jnp.einsum('srhe,sjhe->shrj', grad_heads, value_heads, preferred_element_...  14.3 us
  transfers between devices with their start and end apart: 5, of which 5 were waited for; matrix products, arithmetic and copies ran while one was open for 17% of the time, Pallas kernels for 0%

commit v1 on v0

v1 whole, which is shorter than its diff:
```python
import functools
import math

import jax
import jax.numpy as jnp
from jax import lax
from jax.experimental import pallas as pl
from jax.experimental.pallas import tpu as pltpu
from jax.sharding import PartitionSpec as P

MESH = pl.DeviceIdType.MESH
F32 = jnp.float32
BF16 = jnp.bfloat16
LOG2E = math.log2(math.e)
MASKED = -1e9 * LOG2E
HEADS = 16
SIZE = 48
ANY = pl.BlockSpec(memory_space=pl.ANY)
WHOLE = pl.BlockSpec(memory_space=pltpu.VMEM)
MIB = 1024 * 1024


def shape(dims, dtype=BF16):
    return jax.ShapeDtypeStruct(dims, dtype)


def place():
    samp, row = lax.axis_index("samp"), lax.axis_index("row")
    return samp, row // HEADS, lax.rem(row, HEADS)


def remote(src, dst, send, recv, samp, half, head):
    return pltpu.make_async_remote_copy(
        src_ref=src,
        dst_ref=dst,
        send_sem=send,
        recv_sem=recv,
        device_id=(samp, half * HEADS + head),
        device_id_type=MESH,
    )


def greet(samp, half, head, plane, group):
    barrier = pltpu.get_barrier_semaphore()
    count = 0
    if plane:
        def signal(step, _):
            peer = lax.rem(head + step, HEADS)
            pl.semaphore_signal(
                barrier, inc=1, device_id=(samp, half * HEADS + peer), device_id_type=MESH
            )
            return 0

        lax.fori_loop(1, HEADS, signal, 0)
        count += HEADS - 1
    for apart in range(1, 8):
        if apart >= 4 and group < 7:
            break
        other = lax.rem(samp + apart, 4)
        side = half if apart < 4 else 1 - half
        pl.semaphore_signal(
            barrier, inc=1, device_id=(other, side * HEADS + head), device_id_type=MESH
        )
        count += 1
    pl.semaphore_wait(barrier, count)


def pack_kernel(q_ref, o_ref, k_ref, v_ref, out_ref):
    for part, ref in enumerate((q_ref, o_ref, k_ref, v_ref)):
        turned = ref[...].T
        for head in range(HEADS):
            out_ref[head, part * SIZE : (part + 1) * SIZE, :] = turned[
                head * SIZE : (head + 1) * SIZE
            ]


def normalise(entries):
    wide = entries.astype(F32)
    average = jnp.sum(wide, -1, keepdims=True) * (1.0 / 128)
    centred = wide - average
    variance = jnp.sum(centred * centred, -1, keepdims=True) * (1.0 / 128)
    inverse = lax.rsqrt(variance + 1e-05)
    return centred * inverse, inverse


def bias_kernel(pair_ref, gain_ref, spread_ref, bias_ref, normed_ref):
    gain = gain_ref[...]

    def each(i, _):
        lanes = pl.ds(pl.multiple_of(i * 128, 128), 128)
        for part in range(4):
            rows = pl.ds(part * 128, 128)
            standard, _ = normalise(pair_ref[i, rows, :])
            normed_ref[rows, lanes] = (standard * gain).astype(BF16)
        return 0

    lax.fori_loop(0, 16, each, 0)
    bias = jnp.dot(normed_ref[...], spread_ref[...], preferred_element_type=F32)
    bias_ref[...] = bias.T.reshape(HEADS, 16, 512).astype(BF16)


def spread_kernel(
    pack_ref, bias_ref, qo_ref, kv_ref, all_bias_ref, kv_near, out_sem, in_sem, own_sem, out2_sem, in2_sem
):
    samp, half, head = place()
    greet(samp, half, head, True, 7)
    chunk = pl.multiple_of(head * 64, 64)

    def copy_pack(step, which):
        peer = lax.rem(head + step, HEADS)
        land = kv_near if which else qo_ref.at[samp]
        return remote(
            pack_ref.at[peer, pl.ds(which * 96, 96)], land.at[head],
            out_sem.at[which, step], in_sem.at[which, step], samp, half, peer,
        )

    def copy_bias(step):
        peer = lax.rem(head + step, HEADS)
        return remote(
            bias_ref.at[peer], all_bias_ref.at[pl.ds(chunk, 64)],
            out_sem.at[2, step], in_sem.at[2, step], samp, half, peer,
        )

    def start_pack(step, _):
        copy_pack(step, 0).start()
        copy_pack(step, 1).start()
        return 0

    def start_bias(step, _):
        copy_bias(step).start()
        return 0

    def wait_pack(step, _):
        copy_pack(step, 0).wait()
        copy_pack(step, 1).wait()
        return 0

    def wait_bias(step, _):
        copy_bias(step).wait()
        return 0

    lax.fori_loop(1, HEADS, start_pack, 0)
    own = (
        pltpu.make_async_copy(pack_ref.at[head, pl.ds(0, 96)], qo_ref.at[samp, head], own_sem.at[0]),
        pltpu.make_async_copy(pack_ref.at[head, pl.ds(96, 96)], kv_near.at[head], own_sem.at[1]),
        pltpu.make_async_copy(bias_ref.at[head], all_bias_ref.at[pl.ds(chunk, 64)], own_sem.at[2]),
    )
    for copy in own:
        copy.start()
    lax.fori_loop(1, HEADS, start_bias, 0)
    lax.fori_loop(1, HEADS, wait_pack, 0)
    own[0].wait()
    own[1].wait()

    def send_qo(apart):
        return remote(
            qo_ref.at[samp], qo_ref.at[samp], out2_sem.at[apart], in2_sem.at[apart], lax.rem(samp + apart, 4), half, head
        )

    def send_kv(part, across):
        side = half if across == 0 else 1 - half
        return remote(
            kv_near.at[pl.ds(part * 8, 8)],
            kv_ref.at[samp],
            out2_sem.at[4 + part * 2 + across],
            in2_sem.at[4 + samp],
            2 * half + part,
            side,
            head,
        )

    def keep_kv(part):
        return pltpu.make_async_copy(kv_near.at[pl.ds(part * 8, 8)], kv_ref.at[samp], own_sem.at[3])

    for apart in (2, 3, 1):
        send_qo(apart).start()
    for part in range(2):
        send_kv(part, 1).start()
        mine = samp == 2 * half + part

        @pl.when(mine)
        def _():
            keep_kv(part).start()

        @pl.when(jnp.logical_not(mine))
        def _():
            send_kv(part, 0).start()

    source = samp // 2
    for other in range(4):
        @pl.when(jnp.logical_not((source == half) & (samp == other)))
        def _():
            pltpu.make_async_remote_copy(
                src_ref=kv_near.at[pl.ds(0, 8)],
                dst_ref=kv_ref.at[other],
                send_sem=out2_sem.at[4],
                recv_sem=in2_sem.at[4 + other],
                device_id=(other, source * HEADS + head),
                device_id_type=MESH,
            ).wait_recv()

    for part in range(2):
        send_kv(part, 1).wait_send()
        mine = samp == 2 * half + part

        @pl.when(mine)
        def _():
            keep_kv(part).wait()

        @pl.when(jnp.logical_not(mine))
        def _():
            send_kv(part, 0).wait_send()

    for apart in range(1, 4):
        send_qo(apart).wait_send()
        other = lax.rem(samp + 4 - apart, 4)
        pltpu.make_async_remote_copy(
            src_ref=qo_ref.at[other],
            dst_ref=qo_ref.at[other],
            send_sem=out2_sem.at[apart],
            recv_sem=in2_sem.at[apart],
            device_id=(other, half * HEADS + head),
            device_id_type=MESH,
        ).wait_recv()
    own[2].wait()
    lax.fori_loop(1, HEADS, wait_bias, 0)


def untangle(first, second):
    first, second = first.astype(F32), second.astype(F32)
    low = lax.broadcasted_iota(jnp.int32, first.shape, 1) < 64
    return (
        jnp.where(low, first, pltpu.roll(second, 64, 1)),
        jnp.where(low, pltpu.roll(first, 64, 1), second),
    )


def attend_kernel(
    qo_ref, kv_ref, bias_ref, keep_ref, dq_ref, dkv_ref, dbias_ref,
    raised_ref, along_ref, bias_t, dbias_t, qo_t, qo_rows, kv_t, kv_rows,
    probs_low, score_low, tops, stats, out_sem, in_sem,
):
    samp, half, head = place()
    greet(samp, half, head, False, 3)
    inv_root = 1.0 / math.sqrt(SIZE)

    def turn_bias(block, _):
        at = pl.ds(pl.multiple_of(block * 128, 128), 128)
        turned = bias_ref[at, :].astype(F32).T * LOG2E
        bias_t[:, at] = jnp.where(keep_ref[...] > 0, turned, MASKED)
        return 0

    lax.fori_loop(0, 8, turn_bias, 0)
    filler = jnp.zeros((32, 128), F32)

    def unpack(source, turned_ref, rows_ref, pairs):
        def body(index, _):
            owner, pair = index // pairs, lax.rem(index, pairs)
            at = pl.ds(pl.multiple_of(pair * 128, 128), 128)
            both = untangle(source[owner, 2 * pair], source[owner, 2 * pair + 1])
            for which in range(2):
                filled = jnp.concatenate([both[which], filler], 0)
                turned_ref[2 * owner + which, :, at] = filled.astype(BF16)
                rows_ref[2 * owner + which, at, :] = filled.T.astype(BF16)
            return 0

        lax.fori_loop(0, 4 * pairs, body, 0)

    unpack(qo_ref, qo_t, qo_rows, 8)
    unpack(kv_ref, kv_t, kv_rows, 4)

    def stat_copy(sample, apart):
        return remote(
            stats.at[samp, sample], stats.at[samp, sample],
            out_sem.at[sample, apart], in_sem.at[sample, apart],
            lax.rem(samp + apart, 4), half, head,
        )

    lane = lax.broadcasted_iota(jnp.int32, (128, 128), 1)

    def first_pass(sample, _):
        def block_body(block, _):
            at = pl.ds(pl.multiple_of(block * 256, 256), 256)
            right = qo_t[sample, :, at]
            partial = []
            for part in range(4):
                rows = pl.ds(part * 128, 128)
                kv = kv_rows[sample, rows, :]
                kept = jnp.where((lane < SIZE) & (keep_ref[rows, :] > 0), kv, 0).astype(BF16)
                vals = jnp.where(lane >= SIZE, kv, 0).astype(BF16)
                score = jnp.dot(kept, right, preferred_element_type=F32)
                score = score * (inv_root * LOG2E) + bias_t[rows, at]
                top = jnp.max(score, 0, keepdims=True)
                raised = jnp.exp2(score - top)
                along = jnp.dot(vals, right, preferred_element_type=F32)
                raised_ref[sample, rows, at] = raised
                along_ref[sample, rows, at] = along
                total = jnp.sum(raised, 0, keepdims=True)
                mixed = jnp.sum(raised * along, 0, keepdims=True)
                tops[sample, part : part + 1, at] = top
                partial.append((top, total, mixed))
            peak = functools.reduce(jnp.maximum, [p[0] for p in partial])
            scale = [jnp.exp2(p[0] - peak) for p in partial]
            stats[samp, sample, 0:1, at] = peak
            stats[samp, sample, 1:2, at] = sum(p[1] * w for p, w in zip(partial, scale))
            stats[samp, sample, 2:3, at] = sum(p[2] * w for p, w in zip(partial, scale))
            return 0

        lax.fori_loop(0, 4, block_body, 0)
        for apart in range(1, 4):
            stat_copy(sample, apart).start()
        return 0

    stats[samp] = jnp.zeros((8, 8, 1024), F32)
    lax.fori_loop(0, 8, first_pass, 0)
    dbias_t[...] = jnp.zeros((512, 1024), F32)

    def second_pass(sample, _):
        for apart in range(1, 4):
            stat_copy(sample, apart).wait_recv()

        def block_body(block, _):
            at = pl.ds(pl.multiple_of(block * 256, 256), 256)
            peaks = [stats[other, sample, 0:1, at] for other in range(4)]
            peak = functools.reduce(jnp.maximum, peaks)
            scale = [jnp.exp2(p - peak) for p in peaks]
            total = sum(stats[other, sample, 1:2, at] * scale[other] for other in range(4))
            mixed = sum(stats[other, sample, 2:3, at] * scale[other] for other in range(4))
            share = 1.0 / total
            mean = mixed * share
            for part in range(4):
                rows = pl.ds(part * 128, 128)
                factor = jnp.exp2(tops[sample, part : part + 1, at] - peak) * share
                probs = raised_ref[sample, rows, at] * factor
                grad = probs * (along_ref[sample, rows, at] - mean)
                dbias_t[rows, at] += grad
                probs_low[rows, at] = probs.astype(BF16)
                score_low[rows, at] = grad.astype(BF16)
            return 0

        lax.fori_loop(0, 4, block_body, 0)
        right = qo_rows[sample]
        dk = jnp.dot(score_low[...], right, preferred_element_type=F32)
        dv = jnp.dot(probs_low[...], right, preferred_element_type=F32)
        wide = lax.broadcasted_iota(jnp.int32, (512, 128), 1)
        both = jnp.where(wide < SIZE, dk * inv_root, dv).T
        dkv_ref[sample] = both[:96].astype(BF16)
        dq = jnp.dot(kv_t[sample, :SIZE, :], score_low[...], preferred_element_type=F32)
        dq_ref[sample] = (dq * inv_root).astype(BF16)
        return 0

    lax.fori_loop(0, 8, second_pass, 0)

    def turn_back(block, _):
        at = pl.ds(pl.multiple_of(block * 128, 128), 128)
        dbias_ref[at, :] = dbias_t[:, at].T.astype(BF16)
        return 0

    lax.fori_loop(0, 8, turn_back, 0)

    def sent(sample, _):
        for apart in range(1, 4):
            stat_copy(sample, apart).wait_send()
        return 0

    lax.fori_loop(0, 8, sent, 0)


def collect_kernel(
    dq_ref, dkv_ref, dbias_ref, own_bias, own_dq, own_dkv,
    dq_parts, dkv_parts, dq_sum, dkv_sum, out_sem, in_sem, own_sem, out2_sem, in2_sem,
):
    samp, half, head = place()
    greet(samp, half, head, True, 7)
    owner = samp // 2
    part = lax.rem(samp, 2)

    def send_dq(apart):
        other = lax.rem(samp + apart, 4)
        return remote(
            dq_ref.at[pl.ds(2 * other, 2)], dq_parts.at[apart], out2_sem.at[apart], in2_sem.at[apart], other, half, head
        )

    def send_dkv(other):
        return remote(
            dkv_ref.at[pl.ds(2 * other, 2)], dkv_parts.at[part, half],
            out2_sem.at[4 + other], in2_sem.at[4 + 2 * part + half], other, owner, head,
        )

    keep_dkv = pltpu.make_async_copy(dkv_ref.at[pl.ds(2 * samp, 2)], dkv_parts.at[part, half], own_sem.at[0])
    keep_dq = pltpu.make_async_copy(dq_ref.at[pl.ds(2 * samp, 2)], dq_parts.at[0], own_sem.at[1])
    keep_bias = pltpu.make_async_copy(
        dbias_ref.at[pl.ds(pl.multiple_of(head * 64, 64), 64)], own_bias.at[head], own_sem.at[2]
    )
    for apart in (2, 3, 1):
        send_dq(apart).start()
    for other in range(4):
        mine = (owner == half) & (samp == other)

        @pl.when(mine)
        def _():
            keep_dkv.start()

        @pl.when(jnp.logical_not(mine))
        def _():
            send_dkv(other).start()

    keep_dq.start()
    keep_bias.start()

    def send_bias(step):
        peer = lax.rem(head + step, HEADS)
        return remote(
            dbias_ref.at[pl.ds(pl.multiple_of(peer * 64, 64), 64)], own_bias.at[head],
            out_sem.at[0, step], in_sem.at[0, step], samp, half, peer,
        )

    def start_bias(step, _):
        send_bias(step).start()
        return 0

    lax.fori_loop(1, HEADS, start_bias, 0)

    keep_dq.wait()
    for apart in range(1, 4):
        send_dq(apart).wait()
    for block in range(8):
        at = pl.ds(block * 128, 128)
        total = sum(dq_parts[apart, :, :, at].astype(F32) for apart in range(4))
        dq_sum[block] = total.astype(BF16)

    for other in range(4):
        mine = (owner == half) & (samp == other)

        @pl.when(mine)
        def _():
            keep_dkv.wait()

        @pl.when(jnp.logical_not(mine))
        def _():
            send_dkv(other).wait_send()

    for piece in range(2):
        for side in range(2):
            from_samp = 2 * half + piece

            @pl.when(jnp.logical_not((from_samp == samp) & (side == half)))
            def _():
                pltpu.make_async_remote_copy(
                    src_ref=dkv_ref.at[pl.ds(0, 2)],
                    dst_ref=dkv_parts.at[piece, side],
                    send_sem=out2_sem.at[4],
                    recv_sem=in2_sem.at[4 + 2 * piece + side],
                    device_id=(from_samp, side * HEADS + head),
                    device_id_type=MESH,
                ).wait_recv()

    for block in range(8):
        at = pl.ds((block % 4) * 128, 128)
        total = dkv_parts[block // 4, 0, :, :, at].astype(F32) + dkv_parts[block // 4, 1, :, :, at].astype(F32)
        dkv_sum[block] = total.astype(BF16)

    def send_out(step):
        peer = lax.rem(head + step, HEADS)
        to = (samp, half, peer)
        return (
            remote(dq_sum.at[peer // 2], own_dq.at[head], out_sem.at[1, step], in_sem.at[1, step], *to),
            remote(dkv_sum.at[peer // 2], own_dkv.at[head], out_sem.at[2, step], in_sem.at[2, step], *to),
        )

    def start_out(step, _):
        for copy in send_out(step):
            copy.start()
        return 0

    lax.fori_loop(1, HEADS, start_out, 0)
    keep_q = pltpu.make_async_copy(dq_sum.at[head // 2], own_dq.at[head], own_sem.at[3])
    keep_kv = pltpu.make_async_copy(dkv_sum.at[head // 2], own_dkv.at[head], own_sem.at[4])
    keep_q.start()
    keep_kv.start()
    keep_q.wait()
    keep_kv.wait()
    keep_bias.wait()

    def finish(step, _):
        send_bias(step).wait()
        for copy in send_out(step):
            copy.wait()
        return 0

    lax.fori_loop(1, HEADS, finish, 0)


def unpack_kernel(dq_ref, dkv_ref, q_out, k_out, v_out):
    odd = lax.rem(lax.axis_index("row"), 2) == 1
    for which in range(2):
        for out, source in (
            (q_out, dq_ref[:, which]),
            (k_out, dkv_ref[:, which, :SIZE]),
            (v_out, dkv_ref[:, which, SIZE:]),
        ):
            turned = source.reshape(HEADS * SIZE, 128).astype(F32).T
            out[which] = jnp.where(odd, turned[64:], turned[:64]).astype(BF16)


def pair_kernel(pair_ref, dbias_ref, back_ref, out_ref, mixed_ref, turned_ref, wide_ref, scaled_ref, standard_ref):
    dbias = dbias_ref[...].reshape(256, 512).astype(F32)
    for part in range(4):
        wide_ref[part] = dbias[:, part * 128 : (part + 1) * 128]
    turned_ref[...] = dbias.T.astype(BF16)

    @pl.when(pl.program_id(0) == 0)
    def _():
        mixed_ref[...] = jnp.zeros_like(mixed_ref)

    def each(couple, _):
        scaled_ref[...] = jnp.dot(turned_ref[...], back_ref[couple], preferred_element_type=F32)
        for which in range(2):
            lanes = pl.ds(which * 128, 128)
            for part in range(4):
                rows = pl.ds(part * 128, 128)
                standard, inverse = normalise(pair_ref[2 * couple + which, rows, :])
                scaled = scaled_ref[rows, lanes]
                along = jnp.sum(scaled * standard, -1, keepdims=True) * (1.0 / 128)
                out_ref[2 * couple + which, rows, :] = (inverse * (scaled - standard * along)).astype(BF16)
                standard_ref[rows, lanes] = standard.astype(BF16)
        left = jnp.concatenate(
            [
                jnp.concatenate(
                    [wide_ref[part, pl.ds(2 * couple + which, 16, stride=16), :] for part in range(4)], 1
                )
                for which in range(2)
            ],
            0,
        )
        mixed_ref[...] += jnp.dot(left.astype(BF16), standard_ref[...], preferred_element_type=F32)
        return 0

    lax.fori_loop(0, 8, each, 0)


def on_device(queries, keys, values, out_grad, pair_repr, norm_gain, bias_weight, token_mask):
    samp = lax.axis_index("samp")
    flat = [array.reshape(128, 768) for array in (queries, out_grad, keys, values)]
    packed = pl.pallas_call(
        pack_kernel,
        out_shape=shape((HEADS, 4 * SIZE, 128)),
        in_specs=[WHOLE] * 4,
        out_specs=WHOLE,
    )(*flat)

    eye = jnp.eye(16, dtype=F32)
    weight = bias_weight.astype(F32)
    spread = (weight[None, :, :, None] * eye[:, None, None, :]).reshape(16 * 128, 256).astype(BF16)
    bias = pl.pallas_call(
        bias_kernel,
        grid=(4,),
        out_shape=shape((HEADS, 64, 512)),
        in_specs=[
            pl.BlockSpec((16, 512, 128), lambda i: (i, 0, 0)),
            pl.BlockSpec((1, 128), lambda i: (0, 0)),
            pl.BlockSpec((2048, 256), lambda i: (0, 0)),
        ],
        out_specs=pl.BlockSpec((HEADS, 16, 512), lambda i: (0, i, 0)),
        scratch_shapes=[pltpu.VMEM((512, 2048), BF16)],
        compiler_params=pltpu.CompilerParams(vmem_limit_bytes=32 * MIB),
    )(pair_repr, norm_gain.reshape(1, 128), spread)

    qo, kv, all_bias, _ = pl.pallas_call(
        spread_kernel,
        out_shape=(
            shape((4, 16, 96, 128)),
            shape((4, 8, 96, 128)),
            shape((1024, 512)),
            shape((16, 96, 128)),
        ),
        in_specs=[ANY] * 2,
        out_specs=[ANY] * 4,
        scratch_shapes=[
            pltpu.SemaphoreType.DMA((3, 16)),
            pltpu.SemaphoreType.DMA((3, 16)),
            pltpu.SemaphoreType.DMA((4,)),
            pltpu.SemaphoreType.DMA((8,)),
            pltpu.SemaphoreType.DMA((8,)),
        ],
        compiler_params=pltpu.CompilerParams(collective_id=0, has_side_effects=True),
    )(packed, bias)

    keep = lax.dynamic_slice_in_dim((token_mask > 0).astype(F32), samp * 512, 512)
    keep = jnp.broadcast_to(keep[:, None], (512, 128))
    dq, dkv, dbias = pl.pallas_call(
        attend_kernel,
        out_shape=(shape((8, SIZE, 1024)), shape((8, 96, 512)), shape((1024, 512))),
        in_specs=[WHOLE] * 4,
        out_specs=[WHOLE] * 3,
        scratch_shapes=[
            pltpu.VMEM((8, 512, 1024), F32),
            pltpu.VMEM((8, 512, 1024), F32),
            pltpu.VMEM((512, 1024), F32),
            pltpu.VMEM((512, 1024), F32),
            pltpu.VMEM((8, 128, 1024), BF16),
            pltpu.VMEM((8, 1024, 128), BF16),
            pltpu.VMEM((8, 128, 512), BF16),
            pltpu.VMEM((8, 512, 128), BF16),
            pltpu.VMEM((512, 1024), BF16),
            pltpu.VMEM((512, 1024), BF16),
            pltpu.VMEM((8, 8, 1024), F32),
            pltpu.VMEM((4, 8, 8, 1024), F32),
            pltpu.SemaphoreType.DMA((8, 4)),
            pltpu.SemaphoreType.DMA((8, 4)),
        ],
        compiler_params=pltpu.CompilerParams(
            collective_id=1, has_side_effects=True, vmem_limit_bytes=60 * MIB
        ),
    )(qo, kv, all_bias, keep)

    own_bias, own_dq, own_dkv = pl.pallas_call(
        collect_kernel,
        out_shape=(shape((HEADS, 64, 512)), shape((HEADS, 2, SIZE, 128)), shape((HEADS, 2, 96, 128))),
        in_specs=[ANY] * 3,
        out_specs=[ANY] * 3,
        scratch_shapes=[
            pltpu.VMEM((4, 2, SIZE, 1024), BF16),
            pltpu.VMEM((2, 2, 2, 96, 512), BF16),
            pltpu.VMEM((8, 2, SIZE, 128), BF16),
            pltpu.VMEM((8, 2, 96, 128), BF16),
            pltpu.SemaphoreType.DMA((3, 16)),
            pltpu.SemaphoreType.DMA((3, 16)),
            pltpu.SemaphoreType.DMA((5,)),
            pltpu.SemaphoreType.DMA((8,)),
            pltpu.SemaphoreType.DMA((8,)),
        ],
        compiler_params=pltpu.CompilerParams(
            collective_id=2, has_side_effects=True, vmem_limit_bytes=32 * MIB
        ),
    )(dq, dkv, dbias)

    grad_queries, grad_keys, grad_values = pl.pallas_call(
        unpack_kernel,
        out_shape=(shape((2, 64, 768)),) * 3,
        in_specs=[WHOLE] * 2,
        out_specs=[WHOLE] * 3,
    )(own_dq, own_dkv)

    scaled = weight * norm_gain[:, None]
    scaled = scaled - jnp.mean(scaled, 0, keepdims=True)
    picks = eye.reshape(8, 2, 16)
    back = jnp.einsum("ch,ktj->khjtc", scaled, picks).reshape(8, 256, 256).astype(BF16)
    grad_pair, mixed = pl.pallas_call(
        pair_kernel,
        grid=(4,),
        out_shape=(shape((64, 512, 128)), shape((32, 256), F32)),
        in_specs=[
            pl.BlockSpec((16, 512, 128), lambda i: (i, 0, 0)),
            pl.BlockSpec((HEADS, 16, 512), lambda i: (0, i, 0)),
            pl.BlockSpec((8, 256, 256), lambda i: (0, 0, 0)),
        ],
        out_specs=(
            pl.BlockSpec((16, 512, 128), lambda i: (i, 0, 0)),
            pl.BlockSpec((32, 256), lambda i: (0, 0)),
        ),
        scratch_shapes=[
            pltpu.VMEM((512, 256), BF16),
            pltpu.VMEM((4, 256, 128), F32),
            pltpu.VMEM((512, 256), F32),
            pltpu.VMEM((512, 256), BF16),
        ],
        compiler_params=pltpu.CompilerParams(vmem_limit_bytes=32 * MIB),
    )(pair_repr, own_bias, back)
    mixed = (mixed[:16, :128] + mixed[16:, 128:]).T
    mixed = lax.psum(mixed, ("samp", "row"))
    grad_weight = mixed * norm_gain[:, None]
    grad_gain = jnp.sum(mixed * weight, 1)
    return grad_queries, grad_keys, grad_values, grad_pair, grad_weight, grad_gain


def solution(mesh):
    tokens = P("samp", "row", None)
    pairs = P("row", "samp", None)
    return jax.shard_map(
        on_device,
        mesh=mesh,
        in_specs=(tokens, tokens, tokens, tokens, pairs, P(), P(), P()),
        out_specs=(tokens, tokens, tokens, pairs, P(), P()),
        check_vma=False,
    )
```

time: 702 us -> 283 us (0.40); the launches traced: 692 us -> 280 us
  waiting for transfers between devices: 416 us -> 0 us
  Pallas kernels: 0 us -> 192 us
  matrix products: 69.4 us -> 0 us
  local copies, waits for them, and re-layouts: 74.7 us -> 15.2 us
  other arithmetic: 45.9 us -> 5.18 us
  between operations: 14 us -> 0.77 us
    all_gather x3 -> x0, waiting for transfers between devices: 333 us -> none  [the longest x1 151 us: on_device(): lax.all_gather(keys, 'row', axis=1, tiled=True)]
    pallas_call x0 -> x7, Pallas kernels: none -> 192 us  [the longest x1 54.6 us: on_device(): pl.pallas_call(spread_kernel, out_shape=(shape((4, 16, 96, 128)), shape((...]
    unnamed x6 -> x0, waiting for transfers between devices: 76.4 us -> none
    dot_general x7 -> x0, matrix products: 56.6 us -> none  [the longest x1 14.3 us: attend(): jnp.einsum('srhe,sjhe->shrj', grad_heads, value_heads, preferred_element_...]
    unnamed x21, local copies, waits for them, and re-layouts: 42 us -> 13.1 us
    reduce_sum x3 -> x2, other arithmetic: 30.4 us -> 1.92 us  [the longest x1 1.11 us: on_device(): grad_gain = jnp.sum(mixed * weight, 1)]
    all_gather x2 -> x0, local copies, waits for them, and re-layouts: 17.3 us -> none  [the longest x1 8.73 us: on_device(): lax.all_gather(keys, 'row', axis=1, tiled=True)]
    sub x1 -> x0, matrix products: 12.8 us -> none  [attend(): raised = jnp.exp(scores - row_top)]
  transfers between devices with their start and end apart: 5 -> 0, of which waited for: 5 -> 0; matrix products, arithmetic and copies ran while one was open for 17% -> 0% of each run, Pallas kernels for 0% -> 0%
where the time goes in v1:
time: 283 us; the launch traced here: 280 us
  Pallas kernels  192 us (68%)
  blocking collectives  67 us (24%)
  local copies, waits for them, and re-layouts  15.2 us (5%)
  other arithmetic  5.18 us (2%)
    psum x1, blocking collectives, on_device(): mixed = lax.psum(mixed, ('samp', 'row'))  67 us
    pallas_call x1, Pallas kernels, on_device(): pl.pallas_call(spread_kernel, out_shape=(shape((4, 16, 96, 128)), shape((...  54.6 us
    pallas_call x1, Pallas kernels, on_device(): pl.pallas_call(collect_kernel, out_shape=(shape((HEADS, 64, 512)), shape(...  46.2 us
    pallas_call x1, Pallas kernels, on_device(): pl.pallas_call(attend_kernel, out_shape=(shape((8, SIZE, 1024)), shape((8...  43.2 us
    pallas_call x1, Pallas kernels, on_device(): pl.pallas_call(pair_kernel, grid=(4,), out_shape=(shape((64, 512, 128)),...  23.5 us
    pallas_call x1, Pallas kernels, on_device(): pl.pallas_call(bias_kernel, grid=(4,), out_shape=shape((HEADS, 64, 512)),...  20 us
    unnamed x21, local copies, waits for them, and re-layouts  13.1 us

profile of v1, /device:TPU:10, one launch (start us, length us, event | category | flops | bytes accessed | tf_op | source)
XLA Modules:
  0.0 280.4 jit_solution(7272992481123411537)
XLA Ops:
  0.6 0.8 multiply_reduce_fusion.1
  1.4 0.8 fusion.3
  2.2 0.8 multiply_subtract_fusion
  3.0 0.7 convert_element_type.25
  3.7 0.8 broadcast_in_dim.2.keep_ref
  4.5 2.4 shard_map.127.pack_ref
  6.9 0.7 fusion
  7.6 0.7 convert_element_type.32.back_ref
  8.3 0.3 multiply_convert_fusion.1
  8.6 0.0 copy-start.8
  8.6 0.3 copy.18
  8.9 0.5 copy.15.spread_ref
  9.5 0.0 copy-done.8
  9.5 0.0 copy-start
  9.5 3.4 %copy-done = bf16[64,512,128]{2,1,0:T(8,128)(2,1)S(1)} copy-done((bf16[64,512,128]{2,1,0:T(8,128)(2,1)S(1)}, bf16[64,512,128]{2,1,0:T(8,128)(2,1)}, u32[]{:S(2)}) %copy-start) | copy-done | bytes 8388632
  12.9 20.0 %shard_map.128.bias_ref = bf16[16,64,512]{2,1,0:T(8,128)(2,1)S(1)} custom-call(bf16[64,512,128]{2,1,0:T(8,128)(2,1)S(1)} %copy-done, f32[1,128]{1,0:T(1,128)S(1)} %bitcast.16, bf16[2048,256]{1,0:T(8,128)(2,1)S(1)} %copy.15.spread_ref), custom_call_target="tpu_custom_call" | custom-call | tf_op jit(solution)/shard_map/pallas_call | solution.py:555
  32.9 0.0 copy-start.2
  32.9 1.0 copy-done.2
  33.9 54.6 %shard_map.129 = (bf16[4,16,96,128]{3,2,1,0:T(8,128)(2,1)}, bf16[4,8,96,128]{3,2,1,0:T(8,128)(2,1)}, bf16[1024,512]{1,0:T(8,128)(2,1)}, bf16[16,96,128]{2,1,0:T(8,128)(2,1)}) custom-call(bf16[16,192,128]{2,1,0:T(8,128)(2,1)} %shard_map.127.pack_ref, bf16[16,64,512]{2,1,0:T(8,128)(2,1)} %copy-done.2), custom_call_target="tpu_custom_call" | custom-call | tf_op jit(solution)/shard_map/pallas_call | solution.py:569
  88.5 43.2 %shard_map.130 = (bf16[8,48,1024]{2,1,0:T(8,128)(2,1)}, bf16[8,96,512]{2,1,0:T(8,128)(2,1)}, bf16[1024,512]{1,0:T(8,128)(2,1)}) custom-call(bf16[4,16,96,128]{3,2,1,0:T(8,128)(2,1)} %get-tuple-element.20.qo_ref, bf16[4,8,96,128]{3,2,1,0:T(8,128)(2,1)} %get-tuple-element.21.kv_ref, bf16[1024,512]{1,0:T(8,128)(2,1)} %get-tuple-element.22.bias_ref, ...), custom_call_target="tpu_custom_call" | custom-call | tf_op jit(solution)/shard_map/pallas_call | solution.py:591
  131.7 0.0 copy-start.3
  131.8 1.2 copy-done.3
  133.0 0.0 copy-start.5
  133.0 1.1 copy-done.5
  134.1 0.0 copy-start.6
  134.1 1.1 copy-done.6
  135.2 46.2 %shard_map.131 = (bf16[16,64,512]{2,1,0:T(8,128)(2,1)S(1)}, bf16[16,2,48,128]{3,2,1,0:T(8,128)(2,1)S(1)}, bf16[16,2,96,128]{3,2,1,0:T(8,128)(2,1)S(1)}) custom-call(bf16[8,48,1024]{2,1,0:T(8,128)(2,1)S(1)} %copy-done.5, bf16[8,96,512]{2,1,0:T(8,128)(2,1)S(1)} %copy-done.6, bf16[1024,512]{1,0:T(8,128)(2,1)S(1)} %copy-done.3), custom_call_target="tpu_custom_call" | custom-call | tf_op jit(solution)/shard_map/pallas_call | solution.py:617
  181.4 0.0 copy-start.4
  181.5 0.9 copy-done.4
  182.3 0.0 copy-start.7
  182.3 0.7 copy-done.7
  183.1 2.3 shard_map.132
  185.4 0.0 copy-start.1
  185.4 3.4 %copy-done.1 = bf16[64,512,128]{2,1,0:T(8,128)(2,1)S(1)} copy-done((bf16[64,512,128]{2,1,0:T(8,128)(2,1)S(1)}, bf16[64,512,128]{2,1,0:T(8,128)(2,1)}, u32[]{:S(2)}) %copy-start.1) | copy-done | bytes 8388632
  188.8 0.0 copy-start.9
  188.8 23.5 %shard_map.133 = (bf16[64,512,128]{2,1,0:T(8,128)(2,1)}, f32[32,256]{1,0:T(8,128)S(1)}) custom-call(bf16[64,512,128]{2,1,0:T(8,128)(2,1)S(1)} %copy-done.1, bf16[16,64,512]{2,1,0:T(8,128)(2,1)S(1)} %get-tuple-element.31.dbias_ref, bf16[8,256,256]{2,1,0:T(8,128)(2,1)S(1)} %convert_element_type.32.back_ref), custom_call_target="tpu_custom_call" | custom-call | tf_op jit(solution)/shard_map/pallas_call | solution.py:649
  212.3 67.0 %psum.7 = f32[128,16]{0,1:T(8,128)S(1)} all-reduce(f32[128,16]{0,1:T(8,128)S(1)} %add_bitcast_fusion), channel_id=1, replica_groups=mesh['samp'=4,'row'=32] {'samp','row'}, use_global_device_ids=true, to_apply=%region_1.0 | all-reduce | flops 2048 | bytes 16384 | tf_op jit(solution)/shard_map/psum | solution.py:671
  279.3 0.0 copy-done.9
  279.3 1.1 multiply_reduce_fusion
  (5 shorter events, 0.0 us)
Async XLA Ops:
  8.6 0.8 copy-start.8
  9.5 3.4 %copy-start = (bf16[64,512,128]{2,1,0:T(8,128)(2,1)S(1)}, bf16[64,512,128]{2,1,0:T(8,128)(2,1)}, u32[]{:S(2)}) copy-start(bf16[64,512,128]{2,1,0:T(8,128)(2,1)} %pair_ref.3) | copy-start | bytes 25165828
  32.9 1.0 copy-start.2
  131.7 1.2 copy-start.3
  133.0 1.1 copy-start.5
  134.1 1.1 copy-start.6
  181.4 0.9 copy-start.4
  182.3 0.7 copy-start.7
  185.4 3.4 %copy-start.1 = (bf16[64,512,128]{2,1,0:T(8,128)(2,1)S(1)}, bf16[64,512,128]{2,1,0:T(8,128)(2,1)}, u32[]{:S(2)}) copy-start(bf16[64,512,128]{2,1,0:T(8,128)(2,1)} %pair_ref.3) | copy-start | bytes 25165828
  188.8 90.5 %copy-start.9 = (bf16[128,16]{0,1:T(8,128)(2,1)S(1)}, bf16[128,16]{0,1:T(8,128)(2,1)}, u32[]{:S(2)}) copy-start(bf16[128,16]{0,1:T(8,128)(2,1)} %param.14) | copy-start | bytes 12292

commit v2 on v1

--- a/solution.py
+++ b/solution.py
@@ -367,8 +367,8 @@
 
 
 def collect_kernel(
-    dq_ref, dkv_ref, dbias_ref, own_bias, own_dq, own_dkv,
-    dq_parts, dkv_parts, dq_sum, dkv_sum, out_sem, in_sem, own_sem, out2_sem, in2_sem,
+    dq_ref, dkv_ref, dbias_ref, own_bias, dq_sum, dkv_sum,
+    dq_parts, dkv_parts, out_sem, in_sem, own_sem, out2_sem, in2_sem,
 ):
     samp, half, head = place()
     greet(samp, half, head, True, 7)
@@ -460,50 +460,97 @@
         total = dkv_parts[block // 4, 0, :, :, at].astype(F32) + dkv_parts[block // 4, 1, :, :, at].astype(F32)
         dkv_sum[block] = total.astype(BF16)
 
-    def send_out(step):
-        peer = lax.rem(head + step, HEADS)
-        to = (samp, half, peer)
-        return (
-            remote(dq_sum.at[peer // 2], own_dq.at[head], out_sem.at[1, step], in_sem.at[1, step], *to),
-            remote(dkv_sum.at[peer // 2], own_dkv.at[head], out_sem.at[2, step], in_sem.at[2, step], *to),
-        )
-
-    def start_out(step, _):
-        for copy in send_out(step):
-            copy.start()
-        return 0
-
-    lax.fori_loop(1, HEADS, start_out, 0)
-    keep_q = pltpu.make_async_copy(dq_sum.at[head // 2], own_dq.at[head], own_sem.at[3])
-    keep_kv = pltpu.make_async_copy(dkv_sum.at[head // 2], own_dkv.at[head], own_sem.at[4])
-    keep_q.start()
-    keep_kv.start()
-    keep_q.wait()
-    keep_kv.wait()
     keep_bias.wait()
 
     def finish(step, _):
         send_bias(step).wait()
-        for copy in send_out(step):
-            copy.wait()
         return 0
 
     lax.fori_loop(1, HEADS, finish, 0)
 
 
-def unpack_kernel(dq_ref, dkv_ref, q_out, k_out, v_out):
-    odd = lax.rem(lax.axis_index("row"), 2) == 1
+def finish_kernel(
+    mixed_ref, gain_ref, weight_ref, dq_ref, dkv_ref, q_out, k_out, v_out, weight_out, gain_out,
+    plane_parts, group_parts, own_dq, own_dkv, out_sem, in_sem, out2_sem, in2_sem, own_sem,
+):
+    samp, half, head = place()
+    greet(samp, half, head, True, 7)
+
+    def share(step):
+        return remote(
+            mixed_ref, plane_parts.at[head], out_sem.at[0, step], in_sem.at[0, step],
+            samp, half, lax.rem(head + step, HEADS),
+        )
+
+    def send_dq(step):
+        peer = lax.rem(head + step, HEADS)
+        return remote(
+            dq_ref.at[peer // 2], own_dq.at[head], out_sem.at[1, step], in_sem.at[1, step], samp, half, peer
+        )
+
+    def send_dkv(step):
+        peer = lax.rem(head + step, HEADS)
+        return remote(
+            dkv_ref.at[peer // 2], own_dkv.at[head], out_sem.at[2, step], in_sem.at[2, step], samp, half, peer
+        )
+
+    def start_share(step, _):
+        share(step).start()
+        return 0
+
+    def start_grads(step, _):
+        send_dq(step).start()
+        send_dkv(step).start()
+        return 0
+
+    def wait_share(step, _):
+        share(step).wait()
+        return 0
+
+    def wait_grads(step, _):
+        send_dq(step).wait()
+        send_dkv(step).wait()
+        return 0
+
+    lax.fori_loop(1, HEADS, start_share, 0)
+    lax.fori_loop(1, HEADS, start_grads, 0)
+    keep_dq = pltpu.make_async_copy(dq_ref.at[head // 2], own_dq.at[head], own_sem.at[0])
+    keep_dkv = pltpu.make_async_copy(dkv_ref.at[head // 2], own_dkv.at[head], own_sem.at[1])
+    keep_dq.start()
+    keep_dkv.start()
+    plane_parts[head] = mixed_ref[...]
+    lax.fori_loop(1, HEADS, wait_share, 0)
+    spot = samp * 2 + half
+    group_parts[spot] = sum(plane_parts[other] for other in range(HEADS))
+
+    def share_group(apart):
+        return remote(
+            group_parts.at[spot], group_parts.at[spot], out2_sem.at[apart], in2_sem.at[apart],
+            lax.rem(samp + apart % 4, 4), half if apart < 4 else 1 - half, head,
+        )
+
+    for apart in range(1, 8):
+        share_group(apart).start()
+    keep_dq.wait()
+    keep_dkv.wait()
+    lax.fori_loop(1, HEADS, wait_grads, 0)
+    odd = lax.rem(head, 2) == 1
     for which in range(2):
         for out, source in (
-            (q_out, dq_ref[:, which]),
-            (k_out, dkv_ref[:, which, :SIZE]),
-            (v_out, dkv_ref[:, which, SIZE:]),
+            (q_out, own_dq[:, which]),
+            (k_out, own_dkv[:, which, :SIZE]),
+            (v_out, own_dkv[:, which, SIZE:]),
         ):
             turned = source.reshape(HEADS * SIZE, 128).astype(F32).T
             out[which] = jnp.where(odd, turned[64:], turned[:64]).astype(BF16)
-
-
-def pair_kernel(pair_ref, dbias_ref, back_ref, out_ref, mixed_ref, turned_ref, wide_ref, scaled_ref, standard_ref):
+    for apart in range(1, 8):
+        share_group(apart).wait()
+    total = sum(group_parts[other] for other in range(8))
+    gain_out[...] = jnp.sum(total * weight_ref[...], 0, keepdims=True)
+    weight_out[...] = (total * gain_ref[...]).T
+
+
+def pair_kernel(pair_ref, dbias_ref, back_ref, out_ref, total_ref, mixed_ref, turned_ref, wide_ref, scaled_ref, standard_ref):
     dbias = dbias_ref[...].reshape(256, 512).astype(F32)
     for part in range(4):
         wide_ref[part] = dbias[:, part * 128 : (part + 1) * 128]
@@ -537,6 +584,10 @@
         return 0
 
     lax.fori_loop(0, 8, each, 0)
+
+    @pl.when(pl.program_id(0) == 3)
+    def _():
+        total_ref[...] = mixed_ref[:16, :128] + mixed_ref[16:, 128:]
 
 
 def on_device(queries, keys, values, out_grad, pair_repr, norm_gain, bias_weight, token_mask):
@@ -614,19 +665,17 @@
         ),
     )(qo, kv, all_bias, keep)
 
-    own_bias, own_dq, own_dkv = pl.pallas_call(
+    own_bias, dq_sum, dkv_sum = pl.pallas_call(
         collect_kernel,
-        out_shape=(shape((HEADS, 64, 512)), shape((HEADS, 2, SIZE, 128)), shape((HEADS, 2, 96, 128))),
+        out_shape=(shape((HEADS, 64, 512)), shape((8, 2, SIZE, 128)), shape((8, 2, 96, 128))),
         in_specs=[ANY] * 3,
-        out_specs=[ANY] * 3,
+        out_specs=[ANY, WHOLE, WHOLE],
         scratch_shapes=[
             pltpu.VMEM((4, 2, SIZE, 1024), BF16),
             pltpu.VMEM((2, 2, 2, 96, 512), BF16),
-            pltpu.VMEM((8, 2, SIZE, 128), BF16),
-            pltpu.VMEM((8, 2, 96, 128), BF16),
-            pltpu.SemaphoreType.DMA((3, 16)),
-            pltpu.SemaphoreType.DMA((3, 16)),
-            pltpu.SemaphoreType.DMA((5,)),
+            pltpu.SemaphoreType.DMA((1, 16)),
+            pltpu.SemaphoreType.DMA((1, 16)),
+            pltpu.SemaphoreType.DMA((3,)),
             pltpu.SemaphoreType.DMA((8,)),
             pltpu.SemaphoreType.DMA((8,)),
         ],
@@ -635,13 +684,6 @@
         ),
     )(dq, dkv, dbias)
 
-    grad_queries, grad_keys, grad_values = pl.pallas_call(
-        unpack_kernel,
-        out_shape=(shape((2, 64, 768)),) * 3,
-        in_specs=[WHOLE] * 2,
-        out_specs=[WHOLE] * 3,
-    )(own_dq, own_dkv)
-
     scaled = weight * norm_gain[:, None]
     scaled = scaled - jnp.mean(scaled, 0, keepdims=True)
     picks = eye.reshape(8, 2, 16)
@@ -649,7 +691,7 @@
     grad_pair, mixed = pl.pallas_call(
         pair_kernel,
         grid=(4,),
-        out_shape=(shape((64, 512, 128)), shape((32, 256), F32)),
+        out_shape=(shape((64, 512, 128)), shape((HEADS, 128), F32)),
         in_specs=[
             pl.BlockSpec((16, 512, 128), lambda i: (i, 0, 0)),
             pl.BlockSpec((HEADS, 16, 512), lambda i: (0, i, 0)),
@@ -657,9 +699,10 @@
         ],
         out_specs=(
             pl.BlockSpec((16, 512, 128), lambda i: (i, 0, 0)),
-            pl.BlockSpec((32, 256), lambda i: (0, 0)),
+            pl.BlockSpec((HEADS, 128), lambda i: (0, 0)),
         ),
         scratch_shapes=[
+            pltpu.VMEM((32, 256), F32),
             pltpu.VMEM((512, 256), BF16),
             pltpu.VMEM((4, 256, 128), F32),
             pltpu.VMEM((512, 256), F32),
@@ -667,11 +710,27 @@
         ],
         compiler_params=pltpu.CompilerParams(vmem_limit_bytes=32 * MIB),
     )(pair_repr, own_bias, back)
-    mixed = (mixed[:16, :128] + mixed[16:, 128:]).T
-    mixed = lax.psum(mixed, ("samp", "row"))
-    grad_weight = mixed * norm_gain[:, None]
-    grad_gain = jnp.sum(mixed * weight, 1)
-    return grad_queries, grad_keys, grad_values, grad_pair, grad_weight, grad_gain
+    grad_queries, grad_keys, grad_values, grad_weight, grad_gain = pl.pallas_call(
+        finish_kernel,
+        out_shape=(shape((2, 64, 768)),) * 3 + (shape((128, HEADS), F32), shape((1, 128), F32)),
+        in_specs=[WHOLE] * 5,
+        out_specs=[WHOLE] * 5,
+        scratch_shapes=[
+            pltpu.VMEM((HEADS, HEADS, 128), F32),
+            pltpu.VMEM((8, HEADS, 128), F32),
+            pltpu.VMEM((HEADS, 2, SIZE, 128), BF16),
+            pltpu.VMEM((HEADS, 2, 96, 128), BF16),
+            pltpu.SemaphoreType.DMA((3, 16)),
+            pltpu.SemaphoreType.DMA((3, 16)),
+            pltpu.SemaphoreType.DMA((8,)),
+            pltpu.SemaphoreType.DMA((8,)),
+            pltpu.SemaphoreType.DMA((2,)),
+        ],
+        compiler_params=pltpu.CompilerParams(
+            collective_id=3, has_side_effects=True, vmem_limit_bytes=32 * MIB
+        ),
+    )(mixed, norm_gain.reshape(1, 128), weight.T, dq_sum, dkv_sum)
+    return grad_queries, grad_keys, grad_values, grad_pair, grad_weight, grad_gain.reshape(128)
 
 
 def solution(mesh):

time: 283 us -> 223 us (0.79)
  blocking collectives: 67 us -> 0 us
  Pallas kernels: 192 us -> 199 us
    psum x1 -> x0, blocking collectives: 67 us -> none  [on_device(): mixed = lax.psum(mixed, ('samp', 'row'))]
    pallas_call x1, Pallas kernels: 2.34 us -> 25.8 us  [on_device(): pl.pallas_call(finish_kernel, out_shape=(shape((2, 64, 768)),) * 3 + (sha...]
    pallas_call x1, Pallas kernels: 46.2 us -> 29.2 us  [on_device(): pl.pallas_call(collect_kernel, out_shape=(shape((HEADS, 64, 512)), shape(...]
    unnamed x21 -> x20, local copies, waits for them, and re-layouts: 13.1 us -> 14.7 us
where the time goes in v2:
time: 223 us; the launch traced here: 220 us
  Pallas kernels  199 us (89%)
  local copies, waits for them, and re-layouts  16.8 us (8%)
  other arithmetic  4.07 us (2%)
    pallas_call x1, Pallas kernels, on_device(): pl.pallas_call(spread_kernel, out_shape=(shape((4, 16, 96, 128)), shape((...  54.6 us
    pallas_call x1, Pallas kernels, on_device(): pl.pallas_call(attend_kernel, out_shape=(shape((8, SIZE, 1024)), shape((8...  43.3 us
    pallas_call x1, Pallas kernels, on_device(): pl.pallas_call(collect_kernel, out_shape=(shape((HEADS, 64, 512)), shape(...  29.2 us
    pallas_call x1, Pallas kernels, on_device(): pl.pallas_call(finish_kernel, out_shape=(shape((2, 64, 768)),) * 3 + (sha...  25.8 us
    pallas_call x1, Pallas kernels, on_device(): pl.pallas_call(pair_kernel, grid=(4,), out_shape=(shape((64, 512, 128)),...  23.5 us
    pallas_call x1, Pallas kernels, on_device(): pl.pallas_call(bias_kernel, grid=(4,), out_shape=shape((HEADS, 64, 512)),...  20 us
    unnamed x20, local copies, waits for them, and re-layouts  14.7 us

profile of v2, /device:TPU:10, one launch (start us, length us, event | category | flops | bytes accessed | tf_op | source)
XLA Modules:
  0.0 220.4 jit_solution(564642322226331024)
XLA Ops:
  0.6 0.8 multiply_reduce_fusion
  1.4 0.8 fusion.3
  2.2 0.8 multiply_subtract_fusion
  3.0 0.7 convert_bitcast_fusion
  3.7 0.8 broadcast_in_dim.2.keep_ref
  4.5 2.4 %shard_map.127.pack_ref = bf16[16,192,128]{2,1,0:T(8,128)(2,1)} custom-call(bf16[128,768]{1,0:T(8,128)(2,1)} %bitcast.22, bf16[128,768]{1,0:T(8,128)(2,1)} %bitcast.23, bf16[128,768]{1,0:T(8,128)(2,1)} %bitcast.24, bf16[128,768]{1,0:T(8,128)(2,1)} %bitcast.25), custom_call_target="tpu_custom_call" | custom-call | tf_op jit(solution)/shard_map/pallas_call | solution.py:596
  6.9 0.7 fusion
  7.6 0.7 convert_element_type.32.back_ref
  8.3 0.3 multiply_convert_fusion.1
  8.6 0.0 copy-start.6
  8.7 0.3 copy.20
  8.9 0.5 copy.16.spread_ref
  9.5 0.0 copy-done.6
  9.5 0.0 copy-start
  9.5 3.4 %copy-done = bf16[64,512,128]{2,1,0:T(8,128)(2,1)S(1)} copy-done((bf16[64,512,128]{2,1,0:T(8,128)(2,1)S(1)}, bf16[64,512,128]{2,1,0:T(8,128)(2,1)}, u32[]{:S(2)}) %copy-start) | copy-done | bytes 8388632
  12.9 20.0 %shard_map.128.bias_ref = bf16[16,64,512]{2,1,0:T(8,128)(2,1)S(1)} custom-call(bf16[64,512,128]{2,1,0:T(8,128)(2,1)S(1)} %copy-done, f32[1,128]{1,0:T(1,128)S(1)} %bitcast.17, bf16[2048,256]{1,0:T(8,128)(2,1)S(1)} %copy.16.spread_ref), custom_call_target="tpu_custom_call" | custom-call | tf_op jit(solution)/shard_map/pallas_call | solution.py:606
  32.9 0.0 copy-start.2
  32.9 1.0 copy-done.2
  33.9 54.6 %shard_map.129 = (bf16[4,16,96,128]{3,2,1,0:T(8,128)(2,1)}, bf16[4,8,96,128]{3,2,1,0:T(8,128)(2,1)}, bf16[1024,512]{1,0:T(8,128)(2,1)}, bf16[16,96,128]{2,1,0:T(8,128)(2,1)}) custom-call(bf16[16,192,128]{2,1,0:T(8,128)(2,1)} %shard_map.127.pack_ref, bf16[16,64,512]{2,1,0:T(8,128)(2,1)} %copy-done.2), custom_call_target="tpu_custom_call" | custom-call | tf_op jit(solution)/shard_map/pallas_call | solution.py:620
  88.5 43.3 %shard_map.130 = (bf16[8,48,1024]{2,1,0:T(8,128)(2,1)}, bf16[8,96,512]{2,1,0:T(8,128)(2,1)}, bf16[1024,512]{1,0:T(8,128)(2,1)}) custom-call(bf16[4,16,96,128]{3,2,1,0:T(8,128)(2,1)} %get-tuple-element.22.qo_ref, bf16[4,8,96,128]{3,2,1,0:T(8,128)(2,1)} %get-tuple-element.23.kv_ref, bf16[1024,512]{1,0:T(8,128)(2,1)} %get-tuple-element.24.bias_ref, ...), custom_call_target="tpu_custom_call" | custom-call | tf_op jit(solution)/shard_map/pallas_call | solution.py:642
  131.8 0.0 copy-start.3
  131.8 1.2 copy-done.3
  133.0 0.0 copy-start.4
  133.0 1.1 copy-done.4
  134.1 0.0 copy-start.5
  134.1 1.1 copy-done.5
  135.3 29.2 %shard_map.131 = (bf16[16,64,512]{2,1,0:T(8,128)(2,1)S(1)}, bf16[8,2,48,128]{3,2,1,0:T(8,128)(2,1)S(1)}, bf16[8,2,96,128]{3,2,1,0:T(8,128)(2,1)S(1)}) custom-call(bf16[8,48,1024]{2,1,0:T(8,128)(2,1)S(1)} %copy-done.4, bf16[8,96,512]{2,1,0:T(8,128)(2,1)S(1)} %copy-done.5, bf16[1024,512]{1,0:T(8,128)(2,1)S(1)} %copy-done.3), custom_call_target="tpu_custom_call" | custom-call | tf_op jit(solution)/shard_map/pallas_call | solution.py:668
  164.5 0.0 copy-start.1
  164.5 3.4 %copy-done.1 = bf16[64,512,128]{2,1,0:T(8,128)(2,1)S(1)} copy-done((bf16[64,512,128]{2,1,0:T(8,128)(2,1)S(1)}, bf16[64,512,128]{2,1,0:T(8,128)(2,1)}, u32[]{:S(2)}) %copy-start.1) | copy-done | bytes 8388632
  167.9 23.5 %shard_map.132 = (bf16[64,512,128]{2,1,0:T(8,128)(2,1)}, f32[16,128]{1,0:T(8,128)S(1)}) custom-call(bf16[64,512,128]{2,1,0:T(8,128)(2,1)S(1)} %copy-done.1, bf16[16,64,512]{2,1,0:T(8,128)(2,1)S(1)} %get-tuple-element.28.dbias_ref, bf16[8,256,256]{2,1,0:T(8,128)(2,1)S(1)} %convert_element_type.32.back_ref), custom_call_target="tpu_custom_call" | custom-call | tf_op jit(solution)/shard_map/pallas_call | solution.py:691
  191.4 25.8 %shard_map.133 = (bf16[2,64,768]{2,1,0:T(8,128)(2,1)S(1)}, bf16[2,64,768]{2,1,0:T(8,128)(2,1)S(1)}, bf16[2,64,768]{2,1,0:T(8,128)(2,1)S(1)}, f32[128,16]{1,0:T(8,128)S(1)}, f32[1,128]{1,0:T(1,128)S(1)}) custom-call(f32[16,128]{1,0:T(8,128)S(1)} %get-tuple-element.29.mixed_ref, f32[1,128]{1,0:T(1,128)S(1)} %bitcast.18, ...), custom_call_target="tpu_custom_call" | custom-call | tf_op jit(solution)/shard_map/pallas_call | solution.py:713
  217.2 0.7 copy.17
  217.8 0.7 copy.25
  218.5 0.7 copy.26
  219.2 0.7 copy.27
  219.9 0.5 copy.28
  (4 shorter events, 0.0 us)
Async XLA Ops:
  8.6 0.8 copy-start.6
  9.5 3.4 %copy-start = (bf16[64,512,128]{2,1,0:T(8,128)(2,1)S(1)}, bf16[64,512,128]{2,1,0:T(8,128)(2,1)}, u32[]{:S(2)}) copy-start(bf16[64,512,128]{2,1,0:T(8,128)(2,1)} %pair_ref.3) | copy-start | bytes 25165828
  32.9 1.0 copy-start.2
  131.8 1.2 copy-start.3
  133.0 1.1 copy-start.4
  134.1 1.1 copy-start.5
  164.5 3.4 %copy-start.1 = (bf16[64,512,128]{2,1,0:T(8,128)(2,1)S(1)}, bf16[64,512,128]{2,1,0:T(8,128)(2,1)}, u32[]{:S(2)}) copy-start(bf16[64,512,128]{2,1,0:T(8,128)(2,1)} %pair_ref.3) | copy-start | bytes 25165828

commit v3 on v0

v3 whole, which is shorter than its diff:
```python
import functools
import math

import jax
import jax.numpy as jnp
import numpy as np
from jax import lax
from jax.experimental import pallas as pl
from jax.experimental.pallas import tpu as pltpu
from jax.sharding import PartitionSpec as P

MESH = pl.DeviceIdType.MESH
F32 = jnp.float32
BF16 = jnp.bfloat16
LOG2E = math.log2(math.e)
MASKED = -1e9 * LOG2E
HEADS = 16
SIZE = 48
ANY = pl.BlockSpec(memory_space=pl.ANY)
WHOLE = pl.BlockSpec(memory_space=pltpu.VMEM)
MIB = 1024 * 1024


def shape(dims, dtype=BF16):
    return jax.ShapeDtypeStruct(dims, dtype)


def place():
    samp, row = lax.axis_index("samp"), lax.axis_index("row")
    return samp, row // HEADS, lax.rem(row, HEADS)


def remote(src, dst, send, recv, samp, half, head):
    return pltpu.make_async_remote_copy(
        src_ref=src,
        dst_ref=dst,
        send_sem=send,
        recv_sem=recv,
        device_id=(samp, half * HEADS + head),
        device_id_type=MESH,
    )


def greet(samp, half, head, plane, group):
    barrier = pltpu.get_barrier_semaphore()
    count = 0
    if plane:
        def signal(step, _):
            peer = lax.rem(head + step, HEADS)
            pl.semaphore_signal(
                barrier, inc=1, device_id=(samp, half * HEADS + peer), device_id_type=MESH
            )
            return 0

        lax.fori_loop(1, HEADS, signal, 0)
        count += HEADS - 1
    for apart in range(1, 8):
        if apart >= 4 and group < 7:
            break
        other = lax.rem(samp + apart, 4)
        side = half if apart < 4 else 1 - half
        pl.semaphore_signal(
            barrier, inc=1, device_id=(other, side * HEADS + head), device_id_type=MESH
        )
        count += 1
    pl.semaphore_wait(barrier, count)


def dot(left, right):
    return jnp.dot(left, right, preferred_element_type=F32)


def untangle(first, second):
    first, second = first.astype(F32), second.astype(F32)
    low = lax.broadcasted_iota(jnp.int32, first.shape, 1) < 64
    return (
        jnp.where(low, first, pltpu.roll(second, 64, 1)),
        jnp.where(low, pltpu.roll(first, 64, 1), second),
    )


def main_kernel(
    q_ref, o_ref, k_ref, v_ref, pair_ref, gain_ref, spread_ref, centre_ref, mean_ref, keep_ref,
    standard_out, inverse_out, own_bias, dq_sum, dkv_sum,
    packed, qo, kv, kv_near, all_bias, bias, pairs, inverse_wide,
    raised_ref, along_ref, bias_t, qo_t, qo_rows, kv_t, kv_rows, kept_ref, vals_ref,
    low_ref, tops, stats, dq_ref, dkv_ref, dq_parts, dkv_parts,
    load_sem, store_sem, own_sem, plane_out, plane_in, bias_out, bias_in, group_out, group_in,
    stat_out, stat_in, part_out, part_in, back_out, back_in,
):
    samp, half, head = place()
    core, high = lax.rem(samp, 2), samp // 2
    kin = (samp, high * 2 + 1 - core, (1 - high) * 2 + core, (1 - high) * 2 + 1 - core)
    inv_root = 1.0 / math.sqrt(SIZE)

    def load(block):
        return pltpu.make_async_copy(
            pair_ref.at[pl.ds(block * 16, 16)], pairs.at[block % 3], load_sem.at[block]
        )

    def store(block):
        return pltpu.make_async_copy(
            pairs.at[block % 3], standard_out.at[pl.ds(block * 16, 16)], store_sem.at[block]
        )

    load(0).start()
    load(1).start()
    for part, ref in enumerate((q_ref, o_ref, k_ref, v_ref)):
        turned = ref[...].T
        for each in range(HEADS):
            packed[each, part * SIZE : (part + 1) * SIZE, :] = turned[each * SIZE : (each + 1) * SIZE]
    greet(samp, half, head, True, 7)

    def copy_pack(step, which):
        peer = lax.rem(head + step, HEADS)
        land = kv_near if which else qo.at[samp]
        return remote(
            packed.at[peer, pl.ds(which * 96, 96)], land.at[head],
            plane_out.at[which, step], plane_in.at[which, step], samp, half, peer,
        )

    def start_pack(which):
        def body(step, _):
            copy_pack(step, which).start()
            return 0

        lax.fori_loop(1, HEADS, body, 0)

    def wait_pack(which):
        def body(step, _):
            copy_pack(step, which).wait()
            return 0

        lax.fori_loop(1, HEADS, body, 0)

    start_pack(1)
    start_pack(0)
    own_kv = pltpu.make_async_copy(packed.at[head, pl.ds(96, 96)], kv_near.at[head], own_sem.at[0])
    own_qo = pltpu.make_async_copy(packed.at[head, pl.ds(0, 96)], qo.at[samp, head], own_sem.at[1])
    own_kv.start()
    own_qo.start()

    gain = gain_ref[...]
    narrow = lax.broadcasted_iota(jnp.int32, (128, 128), 1)

    def norm_block(block):
        slot = block % 3
        load(block).wait()

        def couple(index, _):
            lanes = pl.ds(pl.multiple_of(index * 256, 256), 256)
            for part in range(4):
                rows = pl.ds(part * 128, 128)
                both = jnp.concatenate(
                    [pairs[slot, 2 * index, rows, :], pairs[slot, 2 * index + 1, rows, :]], 1
                )
                centred = dot(both, centre_ref[...])
                variance = dot((centred * centred).astype(BF16), mean_ref[...])
                inverse = lax.rsqrt(variance + 1e-05)
                standard = centred * inverse
                low = standard.astype(BF16)
                pairs[slot, 2 * index, rows, :] = low[:, :128]
                pairs[slot, 2 * index + 1, rows, :] = low[:, 128:]
                low_ref[rows, lanes] = (standard * gain).astype(BF16)
                old = jnp.where(narrow == 2 * index, inverse[:, :128], inverse_wide[rows, :])
                inverse_wide[rows, :] = jnp.where(narrow == 2 * index + 1, inverse[:, 128:], old)
            return 0

        lax.fori_loop(0, 8, couple, 0, unroll=2)
        store(block).start()
        rows = pl.ds(block * 16, 16)
        bias[:, rows, :] = dot(low_ref[...], spread_ref[...]).T.reshape(HEADS, 16, 512).astype(BF16)
        inverse_out[rows, :] = inverse_wide[...].T[:16]

    def copy_bias(block, step):
        peer = lax.rem(head + step, HEADS)
        start = pl.multiple_of(head * 64 + block * 16, 16)
        return remote(
            bias.at[peer, pl.ds(block * 16, 16)], all_bias.at[pl.ds(start, 16)],
            bias_out.at[block, step], bias_in.at[block, step], samp, half, peer,
        )

    def start_bias(block):
        def body(step, _):
            copy_bias(block, step).start()
            return 0

        lax.fori_loop(1, HEADS, body, 0)

    def send_kv(part, across):
        return remote(
            kv_near.at[pl.ds(part * 8, 8)], kv.at[samp],
            group_out.at[4 + part * 2 + across], group_in.at[4 + samp],
            2 * half + part, 1 - half if across else half, head,
        )

    def keep_kv(part):
        return pltpu.make_async_copy(kv_near.at[pl.ds(part * 8, 8)], kv.at[samp], own_sem.at[2])

    def send_qo(which):
        slot = kin[2] if which == 3 else samp
        to = kin[1] if which == 3 else kin[which]
        return remote(qo.at[slot], qo.at[slot], group_out.at[which], group_in.at[which], to, half, head)

    def wait_qo(which):
        slot = kin[which]
        remote(
            qo.at[slot], qo.at[slot], group_out.at[which], group_in.at[which],
            kin[1] if which == 3 else kin[which], half, head,
        ).wait_recv()

    norm_block(0)
    start_bias(0)
    load(2).start()
    norm_block(1)
    start_bias(1)
    store(0).wait()
    load(3).start()
    wait_pack(1)
    own_kv.wait()
    for part in range(2):
        send_kv(part, 1).start()
        mine = samp == 2 * half + part

        @pl.when(mine)
        def _():
            keep_kv(part).start()

        @pl.when(jnp.logical_not(mine))
        def _():
            send_kv(part, 0).start()

    norm_block(2)
    start_bias(2)
    wait_pack(0)
    own_qo.wait()
    send_qo(2).start()
    send_qo(1).start()
    norm_block(3)
    start_bias(3)
    own_rows = pl.ds(pl.multiple_of(head * 64, 64), 64)
    own_move = pltpu.make_async_copy(bias.at[head], all_bias.at[own_rows], own_sem.at[3])
    own_move.start()

    filler = jnp.zeros((32, 128), F32)

    def unpack(source, turned_ref, rows_ref, owner, count):
        def body(pair, _):
            at = pl.ds(pl.multiple_of(pair * 128, 128), 128)
            both = untangle(source[owner, 2 * pair], source[owner, 2 * pair + 1])
            for which in range(2):
                filled = jnp.concatenate([both[which], filler], 0)
                turned_ref[2 * owner + which, :, at] = filled.astype(BF16)
                rows_ref[2 * owner + which, at, :] = filled.T.astype(BF16)
            return 0

        lax.fori_loop(0, count, body, 0, unroll=2)

    unpack(qo, qo_t, qo_rows, samp, 8)
    wait_qo(2)
    send_qo(3).start()

    for other in range(4):
        @pl.when(jnp.logical_not((high == half) & (samp == other)))
        def _():
            pltpu.make_async_remote_copy(
                src_ref=kv_near.at[pl.ds(0, 8)],
                dst_ref=kv.at[other],
                send_sem=group_out.at[4],
                recv_sem=group_in.at[4 + other],
                device_id=(other, high * HEADS + head),
                device_id_type=MESH,
            ).wait_recv()

    for part in range(2):
        @pl.when(samp == 2 * half + part)
        def _():
            keep_kv(part).wait()

    def unpack_kv(owner, _):
        unpack(kv, kv_t, kv_rows, owner, 4)
        return 0

    lax.fori_loop(0, 4, unpack_kv, 0)

    own_move.wait()
    for block in range(4):
        def wait_bias(step, _):
            copy_bias(block, step).wait()
            return 0

        lax.fori_loop(1, HEADS, wait_bias, 0)

    def turn_bias(block, _):
        at = pl.ds(pl.multiple_of(block * 128, 128), 128)
        turned = all_bias[at, :].astype(F32).T * LOG2E
        bias_t[:, at] = jnp.where(keep_ref[...] > 0, turned, MASKED)
        return 0

    lax.fori_loop(0, 8, turn_bias, 0)

    def stat_copy(sample, apart):
        return remote(
            stats.at[samp, sample], stats.at[samp, sample],
            stat_out.at[sample, apart], stat_in.at[sample, apart],
            lax.rem(samp + apart, 4), half, head,
        )

    wide = lax.broadcasted_iota(jnp.int32, (512, 128), 1)

    def first_pass(owner):
        def sample_body(which, _):
            sample = 2 * owner + which
            both = kv_rows[sample]
            kept_ref[...] = jnp.where((wide < SIZE) & (keep_ref[...] > 0), both, 0).astype(BF16)
            vals_ref[...] = jnp.where(wide >= SIZE, both, 0).astype(BF16)

            def block_body(block, _):
                at = pl.ds(pl.multiple_of(block * 512, 512), 512)
                right = qo_t[sample, :, at]
                partial = []
                for part in range(4):
                    rows = pl.ds(part * 128, 128)
                    score = dot(kept_ref[rows, :], right)
                    along = dot(vals_ref[rows, :], right)
                    score = score * (inv_root * LOG2E) + bias_t[rows, at]
                    top = jnp.max(score, 0, keepdims=True)
                    raised = jnp.exp2(score - top)
                    raised_ref[sample, rows, at] = raised
                    along_ref[sample, rows, at] = along
                    tops[sample, part : part + 1, at] = top
                    partial.append(
                        (top, jnp.sum(raised, 0, keepdims=True), jnp.sum(raised * along, 0, keepdims=True))
                    )
                peak = functools.reduce(jnp.maximum, [p[0] for p in partial])
                scale = [jnp.exp2(p[0] - peak) for p in partial]
                stats[samp, sample, 0:1, at] = peak
                stats[samp, sample, 1:2, at] = sum(p[1] * w for p, w in zip(partial, scale))
                stats[samp, sample, 2:3, at] = sum(p[2] * w for p, w in zip(partial, scale))
                return 0

            lax.fori_loop(0, 2, block_body, 0)
            for apart in range(1, 4):
                stat_copy(sample, apart).start()
            return 0

        lax.fori_loop(0, 2, sample_body, 0)

    stats[samp] = jnp.zeros((8, 8, 1024), F32)
    first_pass(samp)
    for which in range(1, 4):
        if which != 2:
            wait_qo(which)
        unpack(qo, qo_t, qo_rows, kin[which], 8)
        first_pass(kin[which])

    dbias_t = bias_t
    dbias_t[...] = jnp.zeros((512, 1024), F32)

    def second_pass(owner):
        def sample_body(which, _):
            sample = 2 * owner + which
            for apart in range(1, 4):
                stat_copy(sample, apart).wait_recv()

            def block_body(block, _):
                at = pl.ds(pl.multiple_of(block * 256, 256), 256)
                after = pl.ds(pl.multiple_of(block * 256 + 1024, 256), 256)
                peaks = [stats[other, sample, 0:1, at] for other in range(4)]
                peak = functools.reduce(jnp.maximum, peaks)
                scale = [jnp.exp2(p - peak) for p in peaks]
                total = sum(stats[other, sample, 1:2, at] * scale[other] for other in range(4))
                mixed = sum(stats[other, sample, 2:3, at] * scale[other] for other in range(4))
                share = 1.0 / total
                mean = mixed * share
                for part in range(4):
                    rows = pl.ds(part * 128, 128)
                    factor = jnp.exp2(tops[sample, part : part + 1, at] - peak) * share
                    probs = raised_ref[sample, rows, at] * factor
                    grad = probs * (along_ref[sample, rows, at] - mean)
                    dbias_t[rows, at] += grad
                    low_ref[rows, at] = probs.astype(BF16)
                    low_ref[rows, after] = grad.astype(BF16)
                return 0

            lax.fori_loop(0, 4, block_body, 0)
            right = qo_rows[sample]
            dv = dot(low_ref[:, :1024], right)
            dk = dot(low_ref[:, 1024:], right)
            turned = jnp.where(wide < SIZE, dk * inv_root, dv).T
            dkv_ref[sample] = turned[:96].astype(BF16)
            dq = dot(kv_t[sample, :SIZE, :], low_ref[:, 1024:])
            dq_ref[sample] = (dq * inv_root).astype(BF16)
            return 0

        lax.fori_loop(0, 2, sample_body, 0)

    def send_dq(which):
        return remote(
            dq_ref.at[pl.ds(2 * kin[which], 2)], dq_parts.at[which - 1],
            part_out.at[which], part_in.at[which], kin[which], half, head,
        )

    def send_dkv(which):
        return remote(
            dkv_ref.at[pl.ds(2 * kin[which], 2)], dkv_parts.at[core, half],
            part_out.at[4 + which], part_in.at[4 + 2 * core + half], kin[which], high, head,
        )

    keep_dkv = pltpu.make_async_copy(dkv_ref.at[pl.ds(2 * samp, 2)], dkv_parts.at[core, half], own_sem.at[4])
    for which in (2, 3, 1):
        second_pass(kin[which])
        send_dq(which).start()
        send_dkv(which).start()
    second_pass(samp)

    @pl.when(high == half)
    def _():
        keep_dkv.start()

    @pl.when(high != half)
    def _():
        send_dkv(0).start()

    def send_back(peer):
        at = pl.ds(pl.multiple_of(peer * 64, 64), 64)
        return remote(
            all_bias.at[at], own_bias.at[head], back_out.at[peer], back_in.at[head], samp, half, peer
        )

    keep_back = pltpu.make_async_copy(all_bias.at[own_rows], own_bias.at[head], own_sem.at[5])

    def turn_back(step, _):
        block = lax.rem(head // 2 + step, 8)
        at = pl.ds(pl.multiple_of(block * 128, 128), 128)
        all_bias[at, :] = dbias_t[:, at].T.astype(BF16)
        for odd in range(2):
            peer = 2 * block + odd

            @pl.when(peer == head)
            def _():
                keep_back.start()

            @pl.when(peer != head)
            def _():
                send_back(peer).start()

        return 0

    lax.fori_loop(0, 8, turn_back, 0)

    for which in range(1, 4):
        send_dq(which).wait()
    for block in range(8):
        at = pl.ds(block * 128, 128)
        total = dq_ref[pl.ds(2 * samp, 2), :, at].astype(F32)
        for which in range(3):
            total = total + dq_parts[which, :, :, at].astype(F32)
        dq_sum[block] = total.astype(BF16)

    @pl.when(high == half)
    def _():
        keep_dkv.wait()

    @pl.when(high != half)
    def _():
        send_dkv(0).wait_send()

    for which in range(1, 4):
        send_dkv(which).wait_send()
    for piece in range(2):
        for side in range(2):
            source = 2 * half + piece

            @pl.when(jnp.logical_not((source == samp) & (half == side)))
            def _():
                pltpu.make_async_remote_copy(
                    src_ref=dkv_ref.at[pl.ds(0, 2)],
                    dst_ref=dkv_parts.at[piece, side],
                    send_sem=part_out.at[4],
                    recv_sem=part_in.at[4 + 2 * piece + side],
                    device_id=(source, side * HEADS + head),
                    device_id_type=MESH,
                ).wait_recv()

    for block in range(8):
        at = pl.ds((block % 4) * 128, 128)
        total = dkv_parts[block // 4, 0, :, :, at].astype(F32) + dkv_parts[block // 4, 1, :, :, at].astype(F32)
        dkv_sum[block] = total.astype(BF16)

    for part in range(2):
        send_kv(part, 1).wait_send()

        @pl.when(samp != 2 * half + part)
        def _():
            send_kv(part, 0).wait_send()

    for which in range(1, 4):
        send_qo(which).wait_send()

    def sent(sample, _):
        for apart in range(1, 4):
            stat_copy(sample, apart).wait_send()
        return 0

    lax.fori_loop(0, 8, sent, 0)
    for block in range(1, 4):
        store(block).wait()
    keep_back.wait()

    def arrived(step, _):
        other = lax.rem(head + step, HEADS)
        at = pl.ds(pl.multiple_of(other * 64, 64), 64)
        remote(
            all_bias.at[at], own_bias.at[other], back_out.at[other], back_in.at[other], samp, half, other
        ).wait()
        return 0

    lax.fori_loop(1, HEADS, arrived, 0)


def pair_kernel(
    standard_ref, dbias_ref, inverse_ref, back_ref, out_ref, total_ref, mixed_ref, turned_ref, wide_ref
):
    dbias = dbias_ref[...].reshape(256, 512).astype(F32)
    for part in range(4):
        wide_ref[part] = dbias[:, part * 128 : (part + 1) * 128]
    shrunk = dbias.reshape(HEADS, 16, 512) * inverse_ref[...][None]
    turned_ref[...] = shrunk.reshape(256, 512).T.astype(BF16)

    @pl.when(pl.program_id(0) == 0)
    def _():
        mixed_ref[...] = jnp.zeros_like(mixed_ref)

    def couple(index, _):
        left = jnp.concatenate(
            [
                jnp.concatenate(
                    [wide_ref[part, pl.ds(2 * index + which, 16, stride=16), :] for part in range(4)], 1
                )
                for which in range(2)
            ],
            0,
        ).astype(BF16)
        mixed = mixed_ref[...]
        for part in range(4):
            rows = pl.ds(part * 128, 128)
            low = jnp.concatenate([standard_ref[2 * index, rows, :], standard_ref[2 * index + 1, rows, :]], 1)
            standard = low.astype(F32)
            scaled = dot(turned_ref[rows, :], back_ref[index])
            for which in range(2):
                lanes = slice(which * 128, which * 128 + 128)
                mine = standard[:, lanes]
                along = jnp.sum(scaled[:, lanes] * mine, -1, keepdims=True) * (1.0 / 128)
                out_ref[2 * index + which, rows, :] = (scaled[:, lanes] - mine * along).astype(BF16)
            mixed = mixed + dot(left[:, part * 128 : (part + 1) * 128], low)
        mixed_ref[...] = mixed
        return 0

    lax.fori_loop(0, 8, couple, 0)

    @pl.when(pl.program_id(0) == 3)
    def _():
        total_ref[...] = mixed_ref[:16, :128] + mixed_ref[16:, 128:]


def finish_kernel(
    mixed_ref, gain_ref, weight_ref, dq_ref, dkv_ref, q_out, k_out, v_out, weight_out, gain_out,
    plane_parts, group_parts, own_dq, own_dkv, out_sem, in_sem, out2_sem, in2_sem, own_sem,
):
    samp, half, head = place()
    greet(samp, half, head, True, 7)

    def share(step):
        return remote(
            mixed_ref, plane_parts.at[head], out_sem.at[0, step], in_sem.at[0, step],
            samp, half, lax.rem(head + step, HEADS),
        )

    def send_dq(step):
        peer = lax.rem(head + step, HEADS)
        return remote(
            dq_ref.at[peer // 2], own_dq.at[head], out_sem.at[1, step], in_sem.at[1, step], samp, half, peer
        )

    def send_dkv(step):
        peer = lax.rem(head + step, HEADS)
        return remote(
            dkv_ref.at[peer // 2], own_dkv.at[head], out_sem.at[2, step], in_sem.at[2, step], samp, half, peer
        )

    def start_share(step, _):
        share(step).start()
        return 0

    def start_grads(step, _):
        send_dq(step).start()
        send_dkv(step).start()
        return 0

    def wait_share(step, _):
        share(step).wait()
        return 0

    def wait_grads(step, _):
        send_dq(step).wait()
        send_dkv(step).wait()
        return 0

    lax.fori_loop(1, HEADS, start_share, 0)
    lax.fori_loop(1, HEADS, start_grads, 0)
    keep_dq = pltpu.make_async_copy(dq_ref.at[head // 2], own_dq.at[head], own_sem.at[0])
    keep_dkv = pltpu.make_async_copy(dkv_ref.at[head // 2], own_dkv.at[head], own_sem.at[1])
    keep_dq.start()
    keep_dkv.start()
    plane_parts[head] = mixed_ref[...]
    lax.fori_loop(1, HEADS, wait_share, 0)
    spot = samp * 2 + half
    group_parts[spot] = sum(plane_parts[other] for other in range(HEADS))

    def share_group(apart):
        return remote(
            group_parts.at[spot], group_parts.at[spot], out2_sem.at[apart], in2_sem.at[apart],
            lax.rem(samp + apart % 4, 4), half if apart < 4 else 1 - half, head,
        )

    for apart in range(1, 8):
        share_group(apart).start()
    keep_dq.wait()
    keep_dkv.wait()
    lax.fori_loop(1, HEADS, wait_grads, 0)
    odd = lax.rem(head, 2) == 1
    for which in range(2):
        for out, source in (
            (q_out, own_dq[:, which]),
            (k_out, own_dkv[:, which, :SIZE]),
            (v_out, own_dkv[:, which, SIZE:]),
        ):
            turned = source.reshape(HEADS * SIZE, 128).astype(F32).T
            out[which] = jnp.where(odd, turned[64:], turned[:64]).astype(BF16)
    for apart in range(1, 8):
        share_group(apart).wait()
    total = sum(group_parts[other] for other in range(8))
    gain_out[...] = jnp.sum(total * weight_ref[...], 0, keepdims=True)
    weight_out[...] = (total * gain_ref[...]).T


def on_device(queries, keys, values, out_grad, pair_repr, norm_gain, bias_weight, token_mask):
    samp = lax.axis_index("samp")
    flat = [array.reshape(128, 768) for array in (queries, out_grad, keys, values)]
    eye = jnp.eye(16, dtype=F32)
    weight = bias_weight.astype(F32)
    spread = (weight[None, :, :, None] * eye[:, None, None, :]).reshape(16 * 128, 256).astype(BF16)
    mean = np.kron(np.eye(2), np.full((128, 128), 1.0 / 128))
    centre = jnp.asarray(np.eye(256) - mean, BF16)
    mean = jnp.asarray(mean, BF16)
    keep = lax.dynamic_slice_in_dim((token_mask > 0).astype(F32), samp * 512, 512)
    keep = jnp.broadcast_to(keep[:, None], (512, 128))
    sems = pltpu.SemaphoreType.DMA
    standard, inverse, own_bias, dq_sum, dkv_sum = pl.pallas_call(
        main_kernel,
        out_shape=(
            shape((64, 512, 128)),
            shape((64, 512), F32),
            shape((HEADS, 64, 512)),
            shape((8, 2, SIZE, 128)),
            shape((8, 2, 96, 128)),
        ),
        in_specs=[WHOLE] * 4 + [ANY] + [WHOLE] * 5,
        out_specs=[ANY, WHOLE, ANY, WHOLE, WHOLE],
        scratch_shapes=[
            pltpu.VMEM((HEADS, 4 * SIZE, 128), BF16),
            pltpu.VMEM((4, HEADS, 96, 128), BF16),
            pltpu.VMEM((4, 8, 96, 128), BF16),
            pltpu.VMEM((HEADS, 96, 128), BF16),
            pltpu.VMEM((1024, 512), BF16),
            pltpu.VMEM((HEADS, 64, 512), BF16),
            pltpu.VMEM((3, 16, 512, 128), BF16),
            pltpu.VMEM((512, 128), F32),
            pltpu.VMEM((8, 512, 1024), F32),
            pltpu.VMEM((8, 512, 1024), F32),
            pltpu.VMEM((512, 1024), F32),
            pltpu.VMEM((8, 128, 1024), BF16),
            pltpu.VMEM((8, 1024, 128), BF16),
            pltpu.VMEM((8, 128, 512), BF16),
            pltpu.VMEM((8, 512, 128), BF16),
            pltpu.VMEM((512, 128), BF16),
            pltpu.VMEM((512, 128), BF16),
            pltpu.VMEM((512, 2048), BF16),
            pltpu.VMEM((8, 8, 1024), F32),
            pltpu.VMEM((4, 8, 8, 1024), F32),
            pltpu.VMEM((8, SIZE, 1024), BF16),
            pltpu.VMEM((8, 96, 512), BF16),
            pltpu.VMEM((3, 2, SIZE, 1024), BF16),
            pltpu.VMEM((2, 2, 2, 96, 512), BF16),
            sems((4,)),
            sems((4,)),
            sems((6,)),
            sems((2, 16)),
            sems((2, 16)),
            sems((4, 16)),
            sems((4, 16)),
            sems((8,)),
            sems((8,)),
            sems((8, 4)),
            sems((8, 4)),
            sems((8,)),
            sems((8,)),
            sems((16,)),
            sems((16,)),
        ],
        compiler_params=pltpu.CompilerParams(
            collective_id=0, has_side_effects=True, vmem_limit_bytes=63 * MIB
        ),
    )(*flat, pair_repr, jnp.tile(norm_gain.reshape(1, 128), (1, 2)), spread, centre, mean, keep)

    scaled = weight * norm_gain[:, None]
    scaled = scaled - jnp.mean(scaled, 0, keepdims=True)
    back = jnp.einsum("ch,ktj->khjtc", scaled, eye.reshape(8, 2, 16)).reshape(8, 256, 256).astype(BF16)
    grad_pair, mixed = pl.pallas_call(
        pair_kernel,
        grid=(4,),
        out_shape=(shape((64, 512, 128)), shape((HEADS, 128), F32)),
        in_specs=[
            pl.BlockSpec((16, 512, 128), lambda i: (i, 0, 0)),
            pl.BlockSpec((HEADS, 16, 512), lambda i: (0, i, 0)),
            pl.BlockSpec((16, 512), lambda i: (i, 0)),
            pl.BlockSpec((8, 256, 256), lambda i: (0, 0, 0)),
        ],
        out_specs=(
            pl.BlockSpec((16, 512, 128), lambda i: (i, 0, 0)),
            pl.BlockSpec((HEADS, 128), lambda i: (0, 0)),
        ),
        scratch_shapes=[
            pltpu.VMEM((32, 256), F32),
            pltpu.VMEM((512, 256), BF16),
            pltpu.VMEM((4, 256, 128), F32),
        ],
        compiler_params=pltpu.CompilerParams(vmem_limit_bytes=32 * MIB),
    )(standard, own_bias, inverse, back)
    grad_queries, grad_keys, grad_values, grad_weight, grad_gain = pl.pallas_call(
        finish_kernel,
        out_shape=(shape((2, 64, 768)),) * 3 + (shape((128, HEADS), F32), shape((1, 128), F32)),
        in_specs=[WHOLE] * 5,
        out_specs=[WHOLE] * 5,
        scratch_shapes=[
            pltpu.VMEM((HEADS, HEADS, 128), F32),
            pltpu.VMEM((8, HEADS, 128), F32),
            pltpu.VMEM((HEADS, 2, SIZE, 128), BF16),
            pltpu.VMEM((HEADS, 2, 96, 128), BF16),
            pltpu.SemaphoreType.DMA((3, 16)),
            pltpu.SemaphoreType.DMA((3, 16)),
            pltpu.SemaphoreType.DMA((8,)),
            pltpu.SemaphoreType.DMA((8,)),
            pltpu.SemaphoreType.DMA((2,)),
        ],
        compiler_params=pltpu.CompilerParams(
            collective_id=3, has_side_effects=True, vmem_limit_bytes=32 * MIB
        ),
    )(mixed, norm_gain.reshape(1, 128), weight.T, dq_sum, dkv_sum)
    return grad_queries, grad_keys, grad_values, grad_pair, grad_weight, grad_gain.reshape(128)


def solution(mesh):
    tokens = P("samp", "row", None)
    pairs = P("row", "samp", None)
    return jax.shard_map(
        on_device,
        mesh=mesh,
        in_specs=(tokens, tokens, tokens, tokens, pairs, P(), P(), P()),
        out_specs=(tokens, tokens, tokens, pairs, P(), P()),
        check_vma=False,
    )
```

time: 702 us -> 146 us (0.21); the launches traced: 692 us -> 146 us
  waiting for transfers between devices: 416 us -> 0 us
  Pallas kernels: 0 us -> 126 us
  blocking collectives: 71.3 us -> 0 us
  matrix products: 69.4 us -> 0 us
  local copies, waits for them, and re-layouts: 74.7 us -> 15.1 us
  other arithmetic: 45.9 us -> 4.06 us
  between operations: 14 us -> 0.7 us
    all_gather x3 -> x0, waiting for transfers between devices: 333 us -> none  [the longest x1 151 us: on_device(): lax.all_gather(keys, 'row', axis=1, tiled=True)]
    pallas_call x0 -> x3, Pallas kernels: none -> 126 us  [the longest x1 85.8 us: on_device(): pl.pallas_call(main_kernel, out_shape=(shape((64, 512, 128)), shape((64,...]
    unnamed x6 -> x0, waiting for transfers between devices: 76.4 us -> none
    psum x1 -> x0, blocking collectives: 71.3 us -> none  [on_device(): grad_weight, grad_gain = lax.psum((grad_weight, grad_gain), ('samp', 'row'))]
    dot_general x7 -> x0, matrix products: 56.6 us -> none  [the longest x1 14.3 us: attend(): jnp.einsum('srhe,sjhe->shrj', grad_heads, value_heads, preferred_element_...]
    unnamed x21 -> x20, local copies, waits for them, and re-layouts: 42 us -> 10.2 us
    reduce_sum x3 -> x1, other arithmetic: 30.4 us -> 0.8 us  [on_device(): scaled = scaled - jnp.mean(scaled, 0, keepdims=True)]
    all_gather x2 -> x0, local copies, waits for them, and re-layouts: 17.3 us -> none  [the longest x1 8.73 us: on_device(): lax.all_gather(keys, 'row', axis=1, tiled=True)]
  transfers between devices with their start and end apart: 5 -> 0, of which waited for: 5 -> 0; matrix products, arithmetic and copies ran while one was open for 17% -> 0% of each run, Pallas kernels for 0% -> 0%
where the time goes in v3:
time: 146 us
  Pallas kernels  126 us (86%)
  local copies, waits for them, and re-layouts  15.1 us (10%)
  other arithmetic  4.06 us (3%)
    pallas_call x1, Pallas kernels, on_device(): pl.pallas_call(main_kernel, out_shape=(shape((64, 512, 128)), shape((64,...  85.8 us
    pallas_call x1, Pallas kernels, on_device(): pl.pallas_call(finish_kernel, out_shape=(shape((2, 64, 768)),) * 3 + (sha...  25.8 us
    pallas_call x1, Pallas kernels, on_device(): pl.pallas_call(pair_kernel, grid=(4,), out_shape=(shape((64, 512, 128)),...  14.1 us
    unnamed x20, local copies, waits for them, and re-layouts  10.2 us

profile of v3, /device:TPU:10, one launch (start us, length us, event | category | flops | bytes accessed | tf_op | source)
XLA Modules:
  0.0 145.6 jit_solution(10776199685972638318)
XLA Ops:
  0.6 0.8 multiply_reduce_fusion
  1.4 1.2 tile.8
  2.7 0.8 fusion.3
  3.4 0.8 multiply_subtract_fusion
  4.2 0.7 convert_bitcast_fusion
  4.9 0.8 broadcast_in_dim.2.keep_ref
  5.8 0.7 fusion
  6.5 1.5 %convert_element_type.32.back_ref = bf16[8,256,256]{2,1,0:T(8,128)(2,1)} reshape(bf16[8,16,16,2,128]{4,3,2,1,0:T(2,128)(2,1)S(1)} %fusion) | data formatting | bytes 2097152 | tf_op jit(solution)/shard_map/convert_element_type | solution.py:719
  8.0 0.3 multiply_convert_fusion.1
  8.3 0.3 copy.22
  8.6 1.3 copy.18.spread_ref
  9.9 85.8 %shard_map.145 = (bf16[64,512,128]{2,1,0:T(8,128)(2,1)}, f32[64,512]{1,0:T(8,128)}, bf16[16,64,512]{2,1,0:T(8,128)(2,1)}, bf16[8,2,48,128]{3,2,1,0:T(8,128)(2,1)}, bf16[8,2,96,128]{3,2,1,0:T(8,128)(2,1)}) custom-call(bf16[128,768]{1,0:T(8,128)(2,1)} %bitcast.22, bf16[128,768]{1,0:T(8,128)(2,1)} %bitcast.23, bf16[128,768]{1,0:T(8,128)(2,1)} %bitcast.24, ...), custom_call_target="tpu_custom_call" | custom-call | tf_op jit(solution)/shard_map/pallas_call | solution.py:660
  95.7 0.0 copy-start
  95.7 3.4 %copy-done = bf16[64,512,128]{2,1,0:T(8,128)(2,1)S(1)} copy-done((bf16[64,512,128]{2,1,0:T(8,128)(2,1)S(1)}, bf16[64,512,128]{2,1,0:T(8,128)(2,1)}, u32[]{:S(2)}) %copy-start) | copy-done | bytes 8388632
  99.1 0.0 copy-start.1
  99.1 1.2 copy-done.1
  100.3 0.0 copy-start.2
  100.3 1.2 copy-done.2
  101.5 0.0 copy-start.5
  101.5 0.9 copy-done.5
  102.4 0.0 copy-start.3
  102.5 0.0 copy-start.4
  102.5 0.0 copy-start.6
  102.5 14.1 %shard_map.146 = (bf16[64,512,128]{2,1,0:T(8,128)(2,1)}, f32[16,128]{1,0:T(8,128)S(1)}) custom-call(bf16[64,512,128]{2,1,0:T(8,128)(2,1)S(1)} %copy-done, bf16[16,64,512]{2,1,0:T(8,128)(2,1)S(1)} %copy-done.2, f32[64,512]{1,0:T(8,128)S(1)} %copy-done.5, bf16[8,256,256]{2,1,0:T(8,128)(2,1)S(1)} %copy-done.1), custom_call_target="tpu_custom_call" | custom-call | tf_op jit(solution)/shard_map/pallas_call | solution.py:720
  116.5 0.0 copy-done.3
  116.5 0.0 copy-done.4
  116.5 0.0 copy-done.6
  116.5 25.8 %shard_map.147 = (bf16[2,64,768]{2,1,0:T(8,128)(2,1)S(1)}, bf16[2,64,768]{2,1,0:T(8,128)(2,1)S(1)}, bf16[2,64,768]{2,1,0:T(8,128)(2,1)S(1)}, f32[128,16]{1,0:T(8,128)S(1)}, f32[1,128]{1,0:T(1,128)S(1)}) custom-call(f32[16,128]{1,0:T(8,128)S(1)} %get-tuple-element.21.mixed_ref, f32[1,128]{1,0:T(1,128)S(1)} %bitcast.18, ...), custom_call_target="tpu_custom_call" | custom-call | tf_op jit(solution)/shard_map/pallas_call | solution.py:741
  142.4 0.7 copy.19
  143.1 0.7 copy.27
  143.7 0.7 copy.28
  144.4 0.7 copy.29
  145.1 0.5 copy.30
  (4 shorter events, 0.0 us)
Async XLA Ops:
  95.7 3.4 %copy-start = (bf16[64,512,128]{2,1,0:T(8,128)(2,1)S(1)}, bf16[64,512,128]{2,1,0:T(8,128)(2,1)}, u32[]{:S(2)}) copy-start(bf16[64,512,128]{2,1,0:T(8,128)(2,1)} %get-tuple-element.18.standard_ref) | copy-start | bytes 25165828
  99.1 1.2 copy-start.1
  100.3 1.2 copy-start.2
  101.5 0.9 copy-start.5
  102.4 14.1 %copy-start.3 = (bf16[8,2,96,128]{3,2,1,0:T(8,128)(2,1)S(1)}, bf16[8,2,96,128]{3,2,1,0:T(8,128)(2,1)}, u32[]{:S(2)}) copy-start(bf16[8,2,96,128]{3,2,1,0:T(8,128)(2,1)} %get-tuple-element.23.dkv_ref) | copy-start | bytes 1179652
  102.5 14.1 %copy-start.4 = (bf16[8,2,48,128]{3,2,1,0:T(8,128)(2,1)S(1)}, bf16[8,2,48,128]{3,2,1,0:T(8,128)(2,1)}, u32[]{:S(2)}) copy-start(bf16[8,2,48,128]{3,2,1,0:T(8,128)(2,1)} %get-tuple-element.22.dq_ref) | copy-start | bytes 589828
  102.5 14.1 %copy-start.6 = (f32[128]{0:T(128)S(1)}, f32[128]{0:T(128)}, u32[]{:S(2)}) copy-start(f32[128]{0:T(128)} %param.15) | copy-start | bytes 1540

commit v4 on v0

v4 whole, which is shorter than its diff:
```python
import functools
import math

import jax
import jax.numpy as jnp
from jax import lax
from jax.experimental import pallas as pl
from jax.experimental.pallas import tpu as pltpu
from jax.sharding import PartitionSpec as P

MESH = pl.DeviceIdType.MESH
F32 = jnp.float32
BF16 = jnp.bfloat16
LOG2E = math.log2(math.e)
MASKED = -1e9 * LOG2E
HEADS = 16
SIZE = 48
ANY = pl.BlockSpec(memory_space=pl.ANY)
WHOLE = pl.BlockSpec(memory_space=pltpu.VMEM)
MIB = 1024 * 1024


def shape(dims, dtype=BF16):
    return jax.ShapeDtypeStruct(dims, dtype)


def place():
    samp, row = lax.axis_index("samp"), lax.axis_index("row")
    return samp, row // HEADS, lax.rem(row, HEADS)


def remote(src, dst, send, recv, samp, half, head):
    return pltpu.make_async_remote_copy(
        src_ref=src,
        dst_ref=dst,
        send_sem=send,
        recv_sem=recv,
        device_id=(samp, half * HEADS + head),
        device_id_type=MESH,
    )


def dot(left, right):
    return jnp.dot(left, right, preferred_element_type=F32)


def untangle(first, second):
    first, second = first.astype(F32), second.astype(F32)
    low = lax.broadcasted_iota(jnp.int32, first.shape, 1) < 64
    return (
        jnp.where(low, first, pltpu.roll(second, 64, 1)),
        jnp.where(low, pltpu.roll(first, 64, 1), second),
    )


def steps(count, body, start=0, unroll=1):
    def wrapped(index, _):
        body(index)
        return 0

    lax.fori_loop(start, count, wrapped, 0, unroll=unroll)


def kernel(
    q_ref, o_ref, k_ref, v_ref, pair_ref, gain_ref, weight_ref, mask_ref,
    grad_pair, q_out, k_out, v_out, weight_out, gain_out, spilled,
    packed, qo, kv, kv_near, all_bias, bias, pairs, inverse_wide, inverse_ref,
    raised_ref, along_ref, bias_t, qo_rows, kv_t, kv_rows, kept_ref, vals_ref,
    low_ref, tops, stats, dq_parts, dkv_parts, own_bias, weights, turned_ref, wide_ref, mixed_ref,
    centre_ref, mean_ref, keep_ref, dq_sum, dkv_sum, own_dq, own_dkv, mine_ref, plane_parts, group_parts,
    load_sem, store_sem, own_sem, plane_out, plane_in, bias_out, bias_in, group_out, group_in,
    stat_out, stat_in, part_out, part_in, back_out, back_in, last_out, last_in, share_out, share_in,
):
    samp, half, head = place()
    core, high = lax.rem(samp, 2), samp // 2
    kin = (samp, high * 2 + 1 - core, (1 - high) * 2 + core, (1 - high) * 2 + 1 - core)
    inv_root = 1.0 / math.sqrt(SIZE)

    barrier = pltpu.get_barrier_semaphore()

    def hello(step):
        peer = lax.rem(head + step, HEADS)
        pl.semaphore_signal(barrier, inc=1, device_id=(samp, half * HEADS + peer), device_id_type=MESH)

    steps(HEADS, hello, 1)
    for apart in range(1, 8):
        side = half if apart < 4 else 1 - half
        pl.semaphore_signal(
            barrier, inc=1, device_id=(lax.rem(samp + apart, 4), side * HEADS + head), device_id_type=MESH
        )

    def load(block):
        return pltpu.make_async_copy(
            pair_ref.at[pl.ds(block * 16, 16)], pairs.at[min(block, 2)], load_sem.at[block]
        )

    spill = pltpu.make_async_copy(pairs.at[2], spilled, store_sem.at[0])
    reload = pltpu.make_async_copy(spilled, pairs.at[0], store_sem.at[1])

    for block in range(3):
        load(block).start()
    for part, ref in enumerate((k_ref, v_ref, q_ref, o_ref)):
        turned = ref[...].T
        for each in range(HEADS):
            packed[each, part * SIZE : (part + 1) * SIZE, :] = turned[each * SIZE : (each + 1) * SIZE]
    pl.semaphore_wait(barrier, 22)

    def copy_pack(step, which):
        peer = lax.rem(head + step, HEADS)
        land = qo.at[samp] if which else kv_near
        return remote(
            packed.at[peer, pl.ds(which * 96, 96)], land.at[head],
            plane_out.at[which, step], plane_in.at[which, step], samp, half, peer,
        )

    for which in range(2):
        steps(HEADS, lambda step: copy_pack(step, which).start(), 1)
    own_kv = pltpu.make_async_copy(packed.at[head, pl.ds(0, 96)], kv_near.at[head], own_sem.at[0])
    own_qo = pltpu.make_async_copy(packed.at[head, pl.ds(96, 96)], qo.at[samp, head], own_sem.at[1])
    own_kv.start()
    own_qo.start()

    row = lax.broadcasted_iota(jnp.int32, (256, 256), 0)
    lane = lax.broadcasted_iota(jnp.int32, (256, 256), 1)
    averager = jnp.where(row // 128 == lane // 128, 1.0 / 128, 0.0)
    mean_ref[...] = averager.astype(BF16)
    centre_ref[...] = (jnp.where(row == lane, 1.0, 0.0) - averager).astype(BF16)
    gain_row = gain_ref[...]
    gain = jnp.concatenate([gain_row, gain_row], 1)
    weight = weight_ref[...]
    chooser = (
        lax.broadcasted_iota(jnp.int32, (HEADS, 256), 1) // 16 == lax.broadcasted_iota(jnp.int32, (HEADS, 256), 0)
    ).astype(F32).astype(BF16)
    wider = dot(weight, chooser)
    lane_in = lax.rem(lax.broadcasted_iota(jnp.int32, (128, 256), 1), 16)
    for each in range(16):
        weights[each * 128 : (each + 1) * 128, :] = jnp.where(lane_in == each, wider, 0.0).astype(BF16)
    for part in range(4):
        at = pl.ds(pl.multiple_of(samp * 512 + part * 128, 128), 128)
        kept = (mask_ref[0:1, at] > 0).astype(F32)
        keep_ref[part * 128 : (part + 1) * 128, :] = jnp.broadcast_to(kept, (128, 128)).T

    narrow = lax.broadcasted_iota(jnp.int32, (128, 128), 1)

    def norm_block(block):
        slot = min(block, 2)
        load(block).wait()

        def couple(index):
            lanes = pl.ds(pl.multiple_of(index * 256, 256), 256)
            for part in range(4):
                rows = pl.ds(part * 128, 128)
                both = jnp.concatenate(
                    [pairs[slot, 2 * index, rows, :], pairs[slot, 2 * index + 1, rows, :]], 1
                )
                centred = dot(both, centre_ref[...])
                variance = dot((centred * centred).astype(BF16), mean_ref[...])
                inverse = lax.rsqrt(variance + 1e-05)
                standard = centred * inverse
                low = standard.astype(BF16)
                pairs[slot, 2 * index, rows, :] = low[:, :128]
                pairs[slot, 2 * index + 1, rows, :] = low[:, 128:]
                low_ref[rows, lanes] = (standard * gain).astype(BF16)
                old = jnp.where(narrow == 2 * index, inverse[:, :128], inverse_wide[rows, :])
                inverse_wide[rows, :] = jnp.where(narrow == 2 * index + 1, inverse[:, 128:], old)

        steps(8, couple, unroll=2)
        if block == 2:
            spill.start()
        rows = pl.ds(block * 16, 16)
        bias[:, rows, :] = dot(low_ref[...], weights[...]).T.reshape(HEADS, 16, 512).astype(BF16)
        inverse_ref[rows, :] = inverse_wide[...].T[:16]

    def bias_rows(block):
        return pl.ds(pl.multiple_of(block // 2 * 512 + head * 32 + block % 2 * 16, 16), 16)

    def copy_bias(block, step):
        return remote(
            bias.at[lax.rem(head + step, HEADS), pl.ds(block * 16, 16)], all_bias.at[bias_rows(block)],
            bias_out.at[block, step], bias_in.at[block, step], samp, half, lax.rem(head + step, HEADS),
        )

    def keep_bias(block):
        return pltpu.make_async_copy(
            bias.at[head, pl.ds(block * 16, 16)], all_bias.at[bias_rows(block)], own_sem.at[2 + block]
        )

    def start_bias(block):
        steps(HEADS, lambda step: copy_bias(block, step).start(), 1)
        keep_bias(block).start()

    def send_kv(part, across):
        return remote(
            kv_near.at[pl.ds(part * 8, 8)], kv.at[samp],
            group_out.at[4 + part * 2 + across], group_in.at[4 + samp],
            2 * half + part, 1 - half if across else half, head,
        )

    def keep_kv(part):
        return pltpu.make_async_copy(kv_near.at[pl.ds(part * 8, 8)], kv.at[samp], own_sem.at[6])

    def wait_kv(owner):
        here = jnp.logical_and(owner == samp, high == half)

        @pl.when(here)
        def _():
            pltpu.make_async_copy(kv_near.at[pl.ds(0, 8)], kv.at[owner], own_sem.at[6]).wait()

        @pl.when(jnp.logical_not(here))
        def _():
            pltpu.make_async_remote_copy(
                src_ref=kv_near.at[pl.ds(0, 8)],
                dst_ref=kv.at[owner],
                send_sem=group_out.at[4],
                recv_sem=group_in.at[4 + owner],
                device_id=(owner, high * HEADS + head),
                device_id_type=MESH,
            ).wait_recv()

    def send_qo(which):
        slot = kin[2] if which == 3 else samp
        to = kin[1] if which == 3 else kin[which]
        return remote(qo.at[slot], qo.at[slot], group_out.at[which], group_in.at[which], to, half, head)

    def wait_qo(which):
        slot = kin[which]
        remote(
            qo.at[slot], qo.at[slot], group_out.at[which], group_in.at[which],
            kin[1] if which == 3 else kin[which], half, head,
        ).wait_recv()

    norm_block(0)
    start_bias(0)
    steps(HEADS, lambda step: copy_pack(step, 0).wait(), 1)
    own_kv.wait()
    for part in range(2):
        send_kv(part, 1).start()
        mine = samp == 2 * half + part

        @pl.when(mine)
        def _():
            keep_kv(part).start()

        @pl.when(jnp.logical_not(mine))
        def _():
            send_kv(part, 0).start()

    norm_block(1)
    start_bias(1)
    steps(HEADS, lambda step: copy_pack(step, 1).wait(), 1)
    own_qo.wait()
    send_qo(2).start()
    send_qo(1).start()
    norm_block(2)
    start_bias(2)
    spill.wait()
    load(3).start()

    filler = jnp.zeros((32, 128), F32)

    def unpack_qo(owner):
        def body(peer):
            filled = jnp.concatenate([qo[owner, peer].astype(F32), filler], 0).T.astype(BF16)
            for which in range(2):
                for part in range(2):
                    at = pl.ds(pl.multiple_of(part * 512 + peer * 32, 32), 32)
                    start = which * 64 + part * 32
                    qo_rows[2 * owner + which, at, :] = filled[start : start + 32]

        steps(HEADS, body, unroll=2)

    def unpack_kv(owner):
        def body(pair):
            at = pl.ds(pl.multiple_of(pair * 128, 128), 128)
            both = untangle(kv[owner, 2 * pair], kv[owner, 2 * pair + 1])
            for which in range(2):
                filled = jnp.concatenate([both[which], filler], 0)
                kv_t[2 * owner + which, :, at] = filled.astype(BF16)
                kv_rows[2 * owner + which, at, :] = filled.T.astype(BF16)

        steps(4, body, unroll=2)

    unpack_qo(samp)
    norm_block(3)
    start_bias(3)
    wait_qo(2)
    send_qo(3).start()
    wait_kv(samp)
    unpack_kv(samp)

    def turn_bias(part):
        for block in (2 * part, 2 * part + 1):
            keep_bias(block).wait()
            steps(HEADS, lambda step: copy_bias(block, step).wait(), 1)

        def body(block):
            at = pl.ds(pl.multiple_of(part * 512 + block * 128, 128), 128)
            turned = all_bias[at, :].astype(F32).T * LOG2E
            bias_t[:, at] = jnp.where(keep_ref[...] > 0, turned, MASKED)

        steps(4, body)

    def stat_copy(sample, apart):
        return remote(
            stats.at[samp, sample], stats.at[samp, sample],
            stat_out.at[sample, apart], stat_in.at[sample, apart],
            lax.rem(samp + apart, 4), half, head,
        )

    wide = lax.broadcasted_iota(jnp.int32, (512, 128), 1)

    def first_pass(sample, block):
        both = kv_rows[sample]
        kept_ref[...] = jnp.where((wide < SIZE) & (keep_ref[...] > 0), both, 0).astype(BF16)
        vals_ref[...] = jnp.where(wide >= SIZE, both, 0).astype(BF16)
        at = pl.ds(pl.multiple_of(block * 512, 512), 512)
        right = qo_rows[sample, at, :].T
        partial = []
        for part in range(4):
            rows = pl.ds(part * 128, 128)
            score = dot(kept_ref[rows, :], right)
            along = dot(vals_ref[rows, :], right)
            score = score * (inv_root * LOG2E) + bias_t[rows, at]
            top = jnp.max(score, 0, keepdims=True)
            raised = jnp.exp2(score - top)
            raised_ref[sample, rows, at] = raised
            along_ref[sample, rows, at] = along
            tops[sample, part : part + 1, at] = top
            partial.append((top, jnp.sum(raised, 0, keepdims=True), jnp.sum(raised * along, 0, keepdims=True)))
        peak = functools.reduce(jnp.maximum, [p[0] for p in partial])
        scale = [jnp.exp2(p[0] - peak) for p in partial]
        stats[samp, sample, 0:1, at] = peak
        stats[samp, sample, 1:2, at] = sum(p[1] * w for p, w in zip(partial, scale))
        stats[samp, sample, 2:3, at] = sum(p[2] * w for p, w in zip(partial, scale))

    stats[samp] = jnp.zeros((8, 8, 1024), F32)
    for part in range(2):
        turn_bias(part)
        steps(2, lambda which: first_pass(2 * samp + which, part))
    for which in range(2):
        for apart in range(1, 4):
            stat_copy(2 * samp + which, apart).start()

    for which in range(1, 4):
        if which != 2:
            wait_qo(which)
        wait_kv(kin[which])
        unpack_qo(kin[which])
        unpack_kv(kin[which])

        def one(index):
            sample = 2 * kin[which] + index
            steps(2, lambda block: first_pass(sample, block))
            for apart in range(1, 4):
                stat_copy(sample, apart).start()

        steps(2, one)

    for which in range(1, 4):
        send_qo(which).wait_send()
    bias_t[...] = jnp.zeros((512, 1024), F32)

    def second_pass(owner, index, block):
        sample = 2 * owner + index

        def quarter(piece):
            at = pl.ds(pl.multiple_of(block * 512 + piece * 256, 256), 256)
            here = pl.ds(pl.multiple_of(piece * 256, 256), 256)
            after = pl.ds(pl.multiple_of(piece * 256 + 512, 256), 256)
            peaks = [stats[other, sample, 0:1, at] for other in range(4)]
            peak = functools.reduce(jnp.maximum, peaks)
            scale = [jnp.exp2(p - peak) for p in peaks]
            total = sum(stats[other, sample, 1:2, at] * scale[other] for other in range(4))
            blend = sum(stats[other, sample, 2:3, at] * scale[other] for other in range(4))
            share = 1.0 / total
            mean = blend * share
            for part in range(4):
                rows = pl.ds(part * 128, 128)
                factor = jnp.exp2(tops[sample, part : part + 1, at] - peak) * share
                probs = raised_ref[sample, rows, at] * factor
                grad = probs * (along_ref[sample, rows, at] - mean)
                bias_t[rows, at] += grad
                low_ref[rows, here] = probs.astype(BF16)
                low_ref[rows, after] = grad.astype(BF16)

        steps(2, quarter)
        right = qo_rows[sample, block * 512 : block * 512 + 512, :]
        dv = dot(low_ref[:, :512], right)
        dk = dot(low_ref[:, 512:1024], right)
        both = jnp.where(wide < SIZE, dk * inv_root, dv)
        if block == 0:
            raised_ref[sample, :, 0:128] = both
        else:
            turned = (both + raised_ref[sample, :, 0:128]).T
            for piece in range(4):
                packed[2 * sample + piece // 2, piece % 2 * 96 : piece % 2 * 96 + 96, :] = turned[
                    :96, piece * 128 : piece * 128 + 128
                ].astype(BF16)
        dq = (dot(kv_t[sample, :SIZE, :], low_ref[:, 512:1024]) * inv_root).astype(BF16)
        for piece in range(4):
            qo[owner, 2 * (block * 4 + piece) + index, :SIZE, :] = dq[:, piece * 128 : piece * 128 + 128]

    def send_dq(which):
        return remote(
            qo.at[kin[which], :, pl.ds(0, SIZE)], dq_parts.at[which - 1],
            part_out.at[which], part_in.at[which], kin[which], half, head,
        )

    def send_dkv(which):
        return remote(
            packed.at[pl.ds(4 * kin[which], 4)], dkv_parts.at[core, half],
            part_out.at[4 + which], part_in.at[4 + 2 * core + half], kin[which], high, head,
        )

    keep_dkv = pltpu.make_async_copy(packed.at[pl.ds(4 * samp, 4)], dkv_parts.at[core, half], own_sem.at[7])

    def send_back(peer, part):
        at = pl.ds(pl.multiple_of(part * 512 + peer * 32, 32), 32)
        return remote(
            all_bias.at[at], own_bias.at[head, pl.ds(part * 32, 32)],
            back_out.at[part, peer], back_in.at[part, head], samp, half, peer,
        )

    def keep_back(part):
        at = pl.ds(pl.multiple_of(part * 512 + head * 32, 32), 32)
        return pltpu.make_async_copy(
            all_bias.at[at], own_bias.at[head, pl.ds(part * 32, 32)], own_sem.at[8 + part]
        )

    def turn_back(part):
        def body(step):
            block = lax.rem(head // 4 + step, 4)
            at = pl.ds(pl.multiple_of(part * 512 + block * 128, 128), 128)
            all_bias[at, :] = bias_t[:, at].T.astype(BF16)

            def send(index):
                peer = 4 * block + lax.rem(head + index, 4)

                @pl.when(peer == head)
                def _():
                    keep_back(part).start()

                @pl.when(peer != head)
                def _():
                    send_back(peer, part).start()

            steps(4, send)

        steps(4, body)

    def wait_back(part):
        keep_back(part).wait()

        def body(step):
            other = lax.rem(head + step, HEADS)
            at = pl.ds(pl.multiple_of(part * 512 + other * 32, 32), 32)
            remote(
                all_bias.at[at], own_bias.at[other, pl.ds(part * 32, 32)],
                back_out.at[part, other], back_in.at[part, other], samp, half, other,
            ).wait()

        steps(HEADS, body, 1)

    for part in range(2):
        for which in (2, 3, 1, 0):
            def one(index):
                if part == 0:
                    for apart in range(1, 4):
                        stat_copy(2 * kin[which] + index, apart).wait_recv()
                second_pass(kin[which], index, part)

            steps(2, one)
            if part == 1 and which:
                send_dq(which).start()
                send_dkv(which).start()
        turn_back(part)

    @pl.when(high == half)
    def _():
        keep_dkv.start()

    @pl.when(high != half)
    def _():
        send_dkv(0).start()

    scaled_weight = weight.astype(F32).T * gain_row
    scaled_weight = scaled_weight - jnp.mean(scaled_weight, -1, keepdims=True)
    picker = (
        lax.broadcasted_iota(jnp.int32, (256, HEADS), 0) // 16 == lax.broadcasted_iota(jnp.int32, (256, HEADS), 1)
    ).astype(F32).astype(BF16)
    taller = dot(picker, scaled_weight.astype(BF16))
    taller = jnp.concatenate([taller, taller], 1)
    for each in range(8):
        weights[each * 256 : (each + 1) * 256, :] = jnp.where(
            lax.rem(row, 16) == 2 * each + lane // 128, taller, 0.0
        ).astype(BF16)
    mixed_ref[...] = jnp.zeros((32, 256), F32)

    def unload(block):
        slot = 0 if block == 2 else min(block, 2)
        return pltpu.make_async_copy(
            pairs.at[slot], grad_pair.at[pl.ds(block * 16, 16)], load_sem.at[block]
        )

    def pair_block(block):
        slot = 0 if block == 2 else min(block, 2)
        ours = pl.ds(block * 16, 16)
        dbias = own_bias[:, ours, :].reshape(256, 512).astype(F32)
        for part in range(4):
            wide_ref[part] = dbias[:, part * 128 : (part + 1) * 128]
        shrunk = dbias.reshape(HEADS, 16, 512) * inverse_ref[ours, :][None]
        turned_ref[...] = shrunk.reshape(256, 512).T.astype(BF16)

        def couple(index):
            left = jnp.concatenate(
                [
                    jnp.concatenate(
                        [wide_ref[part, pl.ds(2 * index + which, 16, stride=16), :] for part in range(4)], 1
                    )
                    for which in range(2)
                ],
                0,
            ).astype(BF16)
            mixed = mixed_ref[...]
            spread = weights[pl.ds(pl.multiple_of(index * 256, 256), 256), :]
            for part in range(4):
                rows = pl.ds(part * 128, 128)
                low = jnp.concatenate(
                    [pairs[slot, 2 * index, rows, :], pairs[slot, 2 * index + 1, rows, :]], 1
                )
                standard = low.astype(F32)
                scaled = dot(turned_ref[rows, :], spread)
                for which in range(2):
                    lanes = slice(which * 128, which * 128 + 128)
                    mine = standard[:, lanes]
                    along = jnp.sum(scaled[:, lanes] * mine, -1, keepdims=True) * (1.0 / 128)
                    pairs[slot, 2 * index + which, rows, :] = (scaled[:, lanes] - mine * along).astype(BF16)
                mixed = mixed + dot(left[:, part * 128 : (part + 1) * 128], low)
            mixed_ref[...] = mixed

        steps(8, couple)
        unload(block).start()

    wait_back(0)
    pair_block(0)
    pair_block(1)
    unload(0).wait()
    reload.start()
    wait_back(1)
    pair_block(3)

    for which in range(1, 4):
        send_dq(which).wait()
    for block in range(8):
        pieces = []
        for which in range(2):
            total = qo[samp, 2 * block + which, :SIZE, :].astype(F32)
            for other in range(3):
                total = total + dq_parts[other, 2 * block + which].astype(F32)
            pieces.append(total)
        turned = jnp.concatenate(pieces + [filler], 0).T.astype(BF16)
        for each in range(4):
            dq_sum[block % 4 * 4 + each, block // 4 * 32 : block // 4 * 32 + 32, :] = turned[
                each * 32 : each * 32 + 32
            ]

    @pl.when(high == half)
    def _():
        keep_dkv.wait()

    @pl.when(high != half)
    def _():
        send_dkv(0).wait_send()

    for which in range(1, 4):
        send_dkv(which).wait_send()
    for piece in range(2):
        for side in range(2):
            source = 2 * half + piece

            @pl.when(jnp.logical_not((source == samp) & (half == side)))
            def _():
                pltpu.make_async_remote_copy(
                    src_ref=packed.at[pl.ds(0, 4)],
                    dst_ref=dkv_parts.at[piece, side],
                    send_sem=part_out.at[4],
                    recv_sem=part_in.at[4 + 2 * piece + side],
                    device_id=(source, side * HEADS + head),
                    device_id_type=MESH,
                ).wait_recv()

    for piece in range(2):
        for which in range(2):
            for block in range(4):
                spot = (2 * which + block // 2, slice(block % 2 * 96, block % 2 * 96 + 96))
                total = dkv_parts[piece, 0, spot[0], spot[1], :].astype(F32)
                total = total + dkv_parts[piece, 1, spot[0], spot[1], :].astype(F32)
                dkv_sum[piece * 4 + block, which] = total.astype(BF16)

    def last_dq(step):
        peer = lax.rem(head + step, HEADS)
        return remote(
            dq_sum.at[peer], own_dq.at[head], last_out.at[0, step], last_in.at[0, step], samp, half, peer
        )

    def last_dkv(step):
        peer = lax.rem(head + step, HEADS)
        return remote(
            dkv_sum.at[peer // 2], own_dkv.at[head], last_out.at[1, step], last_in.at[1, step], samp, half, peer
        )

    steps(HEADS, lambda step: last_dq(step).start(), 1)
    steps(HEADS, lambda step: last_dkv(step).start(), 1)
    keep_dq = pltpu.make_async_copy(dq_sum.at[head], own_dq.at[head], own_sem.at[10])
    keep_last = pltpu.make_async_copy(dkv_sum.at[head // 2], own_dkv.at[head], own_sem.at[11])
    keep_dq.start()
    keep_last.start()

    reload.wait()
    pair_block(2)

    mine_ref[...] = mixed_ref[:16, :128] + mixed_ref[16:, 128:]

    def share(step):
        return remote(
            mine_ref, plane_parts.at[head], last_out.at[2, step], last_in.at[2, step],
            samp, half, lax.rem(head + step, HEADS),
        )

    steps(HEADS, lambda step: share(step).start(), 1)
    plane_parts[head] = mine_ref[...]
    steps(HEADS, lambda step: share(step).wait(), 1)
    spot = samp * 2 + half
    group_parts[spot] = sum(plane_parts[other] for other in range(HEADS))

    def share_group(apart):
        return remote(
            group_parts.at[spot], group_parts.at[spot], share_out.at[apart], share_in.at[apart],
            lax.rem(samp + apart % 4, 4), half if apart < 4 else 1 - half, head,
        )

    for apart in range(1, 8):
        share_group(apart).start()

    keep_dq.wait()
    keep_last.wait()
    steps(HEADS, lambda step: last_dq(step).wait(), 1)
    steps(HEADS, lambda step: last_dkv(step).wait(), 1)
    odd = lax.rem(head, 2) == 1
    for which in range(2):
        pieces = [own_dq[each, :, which * SIZE : which * SIZE + SIZE].astype(F32) for each in range(HEADS)]
        q_out[which] = jnp.concatenate(pieces, 1).astype(BF16)
        for out, source in ((k_out, own_dkv[:, which, :SIZE]), (v_out, own_dkv[:, which, SIZE:])):
            turned = source.reshape(HEADS * SIZE, 128).astype(F32).T
            out[which] = jnp.where(odd, turned[64:], turned[:64]).astype(BF16)
    for apart in range(1, 8):
        share_group(apart).wait()
    total = sum(group_parts[other] for other in range(8))
    gain_out[...] = jnp.sum(total * weight.astype(F32).T, 0, keepdims=True)
    weight_out[...] = (total * gain_row).T

    for part in range(2):
        send_kv(part, 1).wait_send()

        @pl.when(samp != 2 * half + part)
        def _():
            send_kv(part, 0).wait_send()

    def sent(sample):
        for apart in range(1, 4):
            stat_copy(sample, apart).wait_send()

    steps(8, sent)
    for block in (1, 2, 3):
        unload(block).wait()


def on_device(queries, keys, values, out_grad, pair_repr, norm_gain, bias_weight, token_mask):
    flat = [array.reshape(128, 768) for array in (queries, out_grad, keys, values)]
    sems = pltpu.SemaphoreType.DMA
    outs = pl.pallas_call(
        kernel,
        out_shape=(
            shape((64, 512, 128)),
            shape((2, 64, 768)),
            shape((2, 64, 768)),
            shape((2, 64, 768)),
            shape((128, HEADS), F32),
            shape((1, 128), F32),
            shape((16, 512, 128)),
        ),
        in_specs=[WHOLE] * 4 + [ANY] + [WHOLE] * 3,
        out_specs=[ANY] + [WHOLE] * 5 + [ANY],
        scratch_shapes=[
            pltpu.VMEM((HEADS, 4 * SIZE, 128), BF16),
            pltpu.VMEM((4, HEADS, 96, 128), BF16),
            pltpu.VMEM((4, 8, 96, 128), BF16),
            pltpu.VMEM((HEADS, 96, 128), BF16),
            pltpu.VMEM((1024, 512), BF16),
            pltpu.VMEM((HEADS, 64, 512), BF16),
            pltpu.VMEM((3, 16, 512, 128), BF16),
            pltpu.VMEM((512, 128), F32),
            pltpu.VMEM((64, 512), F32),
            pltpu.VMEM((8, 512, 1024), F32),
            pltpu.VMEM((8, 512, 1024), F32),
            pltpu.VMEM((512, 1024), F32),
            pltpu.VMEM((8, 1024, 128), BF16),
            pltpu.VMEM((8, 128, 512), BF16),
            pltpu.VMEM((8, 512, 128), BF16),
            pltpu.VMEM((512, 128), BF16),
            pltpu.VMEM((512, 128), BF16),
            pltpu.VMEM((512, 2048), BF16),
            pltpu.VMEM((8, 8, 1024), F32),
            pltpu.VMEM((4, 8, 8, 1024), F32),
            pltpu.VMEM((3, HEADS, SIZE, 128), BF16),
            pltpu.VMEM((2, 2, 4, 192, 128), BF16),
            pltpu.VMEM((HEADS, 64, 512), BF16),
            pltpu.VMEM((2048, 256), BF16),
            pltpu.VMEM((512, 256), BF16),
            pltpu.VMEM((4, 256, 128), F32),
            pltpu.VMEM((32, 256), F32),
            pltpu.VMEM((256, 256), BF16),
            pltpu.VMEM((256, 256), BF16),
            pltpu.VMEM((512, 128), F32),
            pltpu.VMEM((HEADS, 64, 128), BF16),
            pltpu.VMEM((8, 2, 96, 128), BF16),
            pltpu.VMEM((HEADS, 64, 128), BF16),
            pltpu.VMEM((HEADS, 2, 96, 128), BF16),
            pltpu.VMEM((HEADS, 128), F32),
            pltpu.VMEM((HEADS, HEADS, 128), F32),
            pltpu.VMEM((8, HEADS, 128), F32),
            sems((4,)),
            sems((2,)),
            sems((12,)),
            sems((2, 16)),
            sems((2, 16)),
            sems((4, 16)),
            sems((4, 16)),
            sems((8,)),
            sems((8,)),
            sems((8, 4)),
            sems((8, 4)),
            sems((8,)),
            sems((8,)),
            sems((2, 16)),
            sems((2, 16)),
            sems((3, 16)),
            sems((3, 16)),
            sems((8,)),
            sems((8,)),
        ],
        compiler_params=pltpu.CompilerParams(
            collective_id=0, has_side_effects=True, vmem_limit_bytes=63 * MIB
        ),
    )(*flat, pair_repr, norm_gain.reshape(1, 128), bias_weight, token_mask.reshape(1, 2048))
    grad_pair, grad_queries, grad_keys, grad_values, grad_weight, grad_gain, _ = outs
    return grad_queries, grad_keys, grad_values, grad_pair, grad_weight, grad_gain.reshape(128)


def solution(mesh):
    tokens = P("samp", "row", None)
    pairs = P("row", "samp", None)
    return jax.shard_map(
        on_device,
        mesh=mesh,
        in_specs=(tokens, tokens, tokens, tokens, pairs, P(), P(), P()),
        out_specs=(tokens, tokens, tokens, pairs, P(), P()),
        check_vma=False,
    )
```

time: 702 us -> 133 us (0.19); the launches traced: 692 us -> 131 us
  waiting for transfers between devices: 416 us -> 0 us
  Pallas kernels: 0 us -> 114 us
  blocking collectives: 71.3 us -> 0 us
  matrix products: 69.4 us -> 0 us
  local copies, waits for them, and re-layouts: 74.7 us -> 16 us
  other arithmetic: 45.9 us -> 0 us
  between operations: 14 us -> 0.64 us
    all_gather x3 -> x0, waiting for transfers between devices: 333 us -> none  [the longest x1 151 us: on_device(): lax.all_gather(keys, 'row', axis=1, tiled=True)]
    pallas_call x0 -> x1, Pallas kernels: none -> 114 us  [on_device(): pl.pallas_call(kernel, out_shape=(shape((64, 512, 128)), shape((2, 64, 76...]
    unnamed x6 -> x0, waiting for transfers between devices: 76.4 us -> none
    psum x1 -> x0, blocking collectives: 71.3 us -> none  [on_device(): grad_weight, grad_gain = lax.psum((grad_weight, grad_gain), ('samp', 'row'))]
    dot_general x7 -> x0, matrix products: 56.6 us -> none  [the longest x1 14.3 us: attend(): jnp.einsum('srhe,sjhe->shrj', grad_heads, value_heads, preferred_element_...]
    reduce_sum x3 -> x0, other arithmetic: 30.4 us -> none  [the longest x1 18.1 us: attend(): return (grad_query, probs_low, score_low, jnp.sum(grad_score, 0))]
    unnamed x21 -> x9, local copies, waits for them, and re-layouts: 42 us -> 16 us
    all_gather x2 -> x0, local copies, waits for them, and re-layouts: 17.3 us -> none  [the longest x1 8.73 us: on_device(): lax.all_gather(keys, 'row', axis=1, tiled=True)]
  transfers between devices with their start and end apart: 5 -> 0, of which waited for: 5 -> 0; matrix products, arithmetic and copies ran while one was open for 17% -> 0% of each run, Pallas kernels for 0% -> 0%
where the time goes in v4:
time: 133 us; the launch traced here: 131 us
  Pallas kernels  114 us (86%)
  local copies, waits for them, and re-layouts  16 us (12%)
    pallas_call x1, Pallas kernels, on_device(): pl.pallas_call(kernel, out_shape=(shape((64, 512, 128)), shape((2, 64, 76...  114 us
    unnamed x9, local copies, waits for them, and re-layouts  16 us

profile of v4, /device:TPU:10, one launch (start us, length us, event | category | flops | bytes accessed | tf_op | source)
XLA Modules:
  0.0 130.6 jit_solution(10893105537308564961)
XLA Ops:
  0.6 1.4 %copy.14.weight_ref = bf16[128,16]{1,0:T(8,128)(2,1)} copy(bf16[128,16]{0,1:T(8,128)(2,1)} %param.14) | data formatting | bytes 8192 | tf_op args[6]
  2.0 113.9 %shard_map.127 = (bf16[64,512,128]{2,1,0:T(8,128)(2,1)}, bf16[2,64,768]{2,1,0:T(8,128)(2,1)}, bf16[2,64,768]{2,1,0:T(8,128)(2,1)}, bf16[2,64,768]{2,1,0:T(8,128)...) custom-call(bf16[128,768]{1,0:T(8,128)(2,1)} %bitcast.7, bf16[128,768]{1,0:T(8,128)(2,1)} %bitcast.8, ...), custom_call_target="tpu_custom_call" | custom-call | tf_op jit(solution)/shard_map/pallas_call | solution.py:681
  116.0 1.5 %copy.15 = f32[128,16]{0,1:T(8,128)} copy(f32[128,16]{1,0:T(8,128)} %get-tuple-element.22) | data formatting | bytes 16384
  117.5 1.6 %copy.21 = bf16[2,64,768]{2,1,0:T(8,128)(2,1)} copy(bf16[2,64,768]{2,1,0:T(8,128)(2,1)} %get-tuple-element.30) | data formatting | bytes 393216
  119.1 1.6 %copy.22 = bf16[2,64,768]{2,1,0:T(8,128)(2,1)} copy(bf16[2,64,768]{2,1,0:T(8,128)(2,1)} %get-tuple-element.31) | data formatting | bytes 393216
  120.7 1.6 %copy.23 = bf16[2,64,768]{2,1,0:T(8,128)(2,1)} copy(bf16[2,64,768]{2,1,0:T(8,128)(2,1)} %get-tuple-element.32) | data formatting | bytes 393216
  122.3 0.0 copy-start
  122.3 7.8 %copy.24 = bf16[64,512,128]{2,1,0:T(8,128)(2,1)} copy(bf16[64,512,128]{2,1,0:T(8,128)(2,1)} %get-tuple-element.33) | data formatting | bytes 16777216
  130.1 0.0 copy-done
  130.1 0.5 copy.25
Async XLA Ops:
  122.3 7.8 %copy-start = (f32[1,128]{1,0:T(1,128)S(1)}, f32[1,128]{1,0:T(1,128)}, u32[]{:S(2)}) copy-start(f32[1,128]{1,0:T(1,128)} %get-tuple-element.17) | copy-start | bytes 1540

commit v5 on v4

--- a/solution.py
+++ b/solution.py
@@ -63,13 +63,13 @@
 
 def kernel(
     q_ref, o_ref, k_ref, v_ref, pair_ref, gain_ref, weight_ref, mask_ref,
-    grad_pair, q_out, k_out, v_out, weight_out, gain_out, spilled,
+    grad_pair, own_dq, own_dkv, weight_out, gain_out, spilled,
     packed, qo, kv, kv_near, all_bias, bias, pairs, inverse_wide, inverse_ref,
     raised_ref, along_ref, bias_t, qo_rows, kv_t, kv_rows, kept_ref, vals_ref,
     low_ref, tops, stats, dq_parts, dkv_parts, own_bias, weights, turned_ref, wide_ref, mixed_ref,
-    centre_ref, mean_ref, keep_ref, dq_sum, dkv_sum, own_dq, own_dkv, mine_ref, plane_parts, group_parts,
+    centre_ref, mean_ref, keep_ref, dq_sum, dkv_sum, mine_ref, plane_parts, group_parts,
     load_sem, store_sem, own_sem, plane_out, plane_in, bias_out, bias_in, group_out, group_in,
-    stat_out, stat_in, part_out, part_in, back_out, back_in, last_out, last_in, share_out, share_in,
+    stat_out, stat_in, dq_out, dq_in, part_out, part_in, back_out, back_in, last_out, last_in, share_out, share_in,
 ):
     samp, half, head = place()
     core, high = lax.rem(samp, 2), samp // 2
@@ -400,10 +400,11 @@
         for piece in range(4):
             qo[owner, 2 * (block * 4 + piece) + index, :SIZE, :] = dq[:, piece * 128 : piece * 128 + 128]
 
-    def send_dq(which):
-        return remote(
-            qo.at[kin[which], :, pl.ds(0, SIZE)], dq_parts.at[which - 1],
-            part_out.at[which], part_in.at[which], kin[which], half, head,
+    def send_dq(which, part):
+        some = pl.ds(part * 8, 8)
+        return remote(
+            qo.at[kin[which], some, pl.ds(0, SIZE)], dq_parts.at[which - 1, some],
+            dq_out.at[part, which], dq_in.at[part, which], kin[which], half, head,
         )
 
     def send_dkv(which):
@@ -470,9 +471,10 @@
                 second_pass(kin[which], index, part)
 
             steps(2, one)
-            if part == 1 and which:
-                send_dq(which).start()
-                send_dkv(which).start()
+            if which:
+                if part == 1:
+                    send_dkv(which).start()
+                send_dq(which, part).start()
         turn_back(part)
 
     @pl.when(high == half)
@@ -548,9 +550,23 @@
     reload.start()
     wait_back(1)
     pair_block(3)
-
-    for which in range(1, 4):
-        send_dq(which).wait()
+    reload.wait()
+    pair_block(2)
+
+    mine_ref[...] = mixed_ref[:16, :128] + mixed_ref[16:, 128:]
+
+    def share(step):
+        return remote(
+            mine_ref, plane_parts.at[head], last_out.at[2, step], last_in.at[2, step],
+            samp, half, lax.rem(head + step, HEADS),
+        )
+
+    steps(HEADS, lambda step: share(step).start(), 1)
+    plane_parts[head] = mine_ref[...]
+
+    for part in range(2):
+        for which in range(1, 4):
+            send_dq(which, part).wait()
     for block in range(8):
         pieces = []
         for which in range(2):
@@ -616,19 +632,6 @@
     keep_dq.start()
     keep_last.start()
 
-    reload.wait()
-    pair_block(2)
-
-    mine_ref[...] = mixed_ref[:16, :128] + mixed_ref[16:, 128:]
-
-    def share(step):
-        return remote(
-            mine_ref, plane_parts.at[head], last_out.at[2, step], last_in.at[2, step],
-            samp, half, lax.rem(head + step, HEADS),
-        )
-
-    steps(HEADS, lambda step: share(step).start(), 1)
-    plane_parts[head] = mine_ref[...]
     steps(HEADS, lambda step: share(step).wait(), 1)
     spot = samp * 2 + half
     group_parts[spot] = sum(plane_parts[other] for other in range(HEADS))
@@ -642,23 +645,15 @@
     for apart in range(1, 8):
         share_group(apart).start()
 
-    keep_dq.wait()
-    keep_last.wait()
-    steps(HEADS, lambda step: last_dq(step).wait(), 1)
-    steps(HEADS, lambda step: last_dkv(step).wait(), 1)
-    odd = lax.rem(head, 2) == 1
-    for which in range(2):
-        pieces = [own_dq[each, :, which * SIZE : which * SIZE + SIZE].astype(F32) for each in range(HEADS)]
-        q_out[which] = jnp.concatenate(pieces, 1).astype(BF16)
-        for out, source in ((k_out, own_dkv[:, which, :SIZE]), (v_out, own_dkv[:, which, SIZE:])):
-            turned = source.reshape(HEADS * SIZE, 128).astype(F32).T
-            out[which] = jnp.where(odd, turned[64:], turned[:64]).astype(BF16)
     for apart in range(1, 8):
         share_group(apart).wait()
     total = sum(group_parts[other] for other in range(8))
     gain_out[...] = jnp.sum(total * weight.astype(F32).T, 0, keepdims=True)
     weight_out[...] = (total * gain_row).T
-
+    keep_dq.wait()
+    keep_last.wait()
+    steps(HEADS, lambda step: last_dq(step).wait(), 1)
+    steps(HEADS, lambda step: last_dkv(step).wait(), 1)
     for part in range(2):
         send_kv(part, 1).wait_send()
 
@@ -673,6 +668,31 @@
     steps(8, sent)
     for block in (1, 2, 3):
         unload(block).wait()
+
+
+def deliver_kernel(
+    pair_ref, dq_ref, dkv_ref, weight_ref, gain_ref, pair_out, q_out, k_out, v_out, weight_out, gain_out
+):
+    pair_out[...] = pair_ref[...]
+    step = pl.program_id(0)
+
+    @pl.when(step == 0)
+    def _():
+        weight_out[...] = weight_ref[...]
+        gain_out[...] = gain_ref[...]
+
+    for which in range(2):
+        @pl.when(step == which + 1)
+        def _():
+            pieces = [dq_ref[each, :, which * SIZE : which * SIZE + SIZE].astype(F32) for each in range(HEADS)]
+            q_out[which] = jnp.concatenate(pieces, 1).astype(BF16)
+
+        for at, (out, rows) in enumerate(((k_out, slice(0, SIZE)), (v_out, slice(SIZE, 2 * SIZE)))):
+            @pl.when(step == 3 + 2 * at + which)
+            def _():
+                odd = lax.rem(lax.axis_index("row"), 2) == 1
+                turned = dkv_ref[:, which, rows].reshape(HEADS * SIZE, 128).astype(F32).T
+                out[which] = jnp.where(odd, turned[64:], turned[:64]).astype(BF16)
 
 
 def on_device(queries, keys, values, out_grad, pair_repr, norm_gain, bias_weight, token_mask):
@@ -682,15 +702,14 @@
         kernel,
         out_shape=(
             shape((64, 512, 128)),
-            shape((2, 64, 768)),
-            shape((2, 64, 768)),
-            shape((2, 64, 768)),
+            shape((HEADS, 64, 128)),
+            shape((HEADS, 2, 96, 128)),
             shape((128, HEADS), F32),
             shape((1, 128), F32),
             shape((16, 512, 128)),
         ),
         in_specs=[WHOLE] * 4 + [ANY] + [WHOLE] * 3,
-        out_specs=[ANY] + [WHOLE] * 5 + [ANY],
+        out_specs=[ANY] * 3 + [WHOLE] * 2 + [ANY],
         scratch_shapes=[
             pltpu.VMEM((HEADS, 4 * SIZE, 128), BF16),
             pltpu.VMEM((4, HEADS, 96, 128), BF16),
@@ -724,8 +743,6 @@
             pltpu.VMEM((512, 128), F32),
             pltpu.VMEM((HEADS, 64, 128), BF16),
             pltpu.VMEM((8, 2, 96, 128), BF16),
-            pltpu.VMEM((HEADS, 64, 128), BF16),
-            pltpu.VMEM((HEADS, 2, 96, 128), BF16),
             pltpu.VMEM((HEADS, 128), F32),
             pltpu.VMEM((HEADS, HEADS, 128), F32),
             pltpu.VMEM((8, HEADS, 128), F32),
@@ -740,6 +757,8 @@
             sems((8,)),
             sems((8, 4)),
             sems((8, 4)),
+            sems((2, 4)),
+            sems((2, 4)),
             sems((8,)),
             sems((8,)),
             sems((2, 16)),
@@ -753,7 +772,31 @@
             collective_id=0, has_side_effects=True, vmem_limit_bytes=63 * MIB
         ),
     )(*flat, pair_repr, norm_gain.reshape(1, 128), bias_weight, token_mask.reshape(1, 2048))
-    grad_pair, grad_queries, grad_keys, grad_values, grad_weight, grad_gain, _ = outs
+    near_pair, near_dq, near_dkv, near_weight, near_gain, _ = outs
+    fixed = lambda *dims: pl.BlockSpec(dims, lambda i: (0,) * len(dims))
+    grad_pair, grad_queries, grad_keys, grad_values, grad_weight, grad_gain = pl.pallas_call(
+        deliver_kernel,
+        grid=(8,),
+        out_shape=(
+            shape((64, 512, 128)),
+            shape((2, 64, 768)),
+            shape((2, 64, 768)),
+            shape((2, 64, 768)),
+            shape((128, HEADS), F32),
+            shape((1, 128), F32),
+        ),
+        in_specs=[
+            pl.BlockSpec((8, 512, 128), lambda i: (i, 0, 0)),
+            fixed(HEADS, 64, 128),
+            fixed(HEADS, 2, 96, 128),
+            fixed(128, HEADS),
+            fixed(1, 128),
+        ],
+        out_specs=[pl.BlockSpec((8, 512, 128), lambda i: (i, 0, 0))]
+        + [fixed(2, 64, 768)] * 3
+        + [fixed(128, HEADS), fixed(1, 128)],
+        compiler_params=pltpu.CompilerParams(vmem_limit_bytes=60 * MIB),
+    )(near_pair, near_dq, near_dkv, near_weight, near_gain)
     return grad_queries, grad_keys, grad_values, grad_pair, grad_weight, grad_gain.reshape(128)
 
 

time: 133 us -> 118 us (0.89)
  the two profiles are of different devices: /device:TPU:10 before, /device:TPU:24 now
where the time goes in v5:
time: 118 us
  Pallas kernels  114 us (97%)
  local copies, waits for them, and re-layouts  2.91 us (2%)
    pallas_call x1, Pallas kernels, on_device(): pl.pallas_call(kernel, out_shape=(shape((64, 512, 128)), shape((HEADS, 64...  104 us
    pallas_call x1, Pallas kernels, on_device(): pl.pallas_call(deliver_kernel, grid=(8,), out_shape=(shape((64, 512, 128)...  9.94 us
    unnamed x2, local copies, waits for them, and re-layouts  2.91 us

profile of v5, /device:TPU:24, one launch (start us, length us, event | category | flops | bytes accessed | tf_op | source)
XLA Modules:
  0.0 117.6 jit_solution(14892154602744691223)
XLA Ops:
  0.6 1.4 %copy.14.weight_ref = bf16[128,16]{1,0:T(8,128)(2,1)} copy(bf16[128,16]{0,1:T(8,128)(2,1)} %param.14) | data formatting | bytes 8192 | tf_op args[6]
  2.0 104.1 %shard_map.127 = (bf16[64,512,128]{2,1,0:T(8,128)(2,1)}, bf16[16,64,128]{2,1,0:T(8,128)(2,1)}, bf16[16,2,96,128]{3,2,1,0:T(8,128)(2,1)}, f32[128,16]{1,0:T(8,128...) custom-call(bf16[128,768]{1,0:T(8,128)(2,1)} %bitcast.7, bf16[128,768]{1,0:T(8,128)(2,1)} %bitcast.8, ...), custom_call_target="tpu_custom_call" | custom-call | tf_op jit(solution)/shard_map/pallas_call | solution.py:701
  106.2 9.9 %shard_map.128 = (bf16[64,512,128]{2,1,0:T(8,128)(2,1)}, bf16[2,64,768]{2,1,0:T(8,128)(2,1)}, bf16[2,64,768]{2,1,0:T(8,128)(2,1)}, bf16[2,64,768]{2,1,0:T(8,128)...) custom-call(bf16[64,512,128]{2,1,0:T(8,128)(2,1)} %get-tuple-element.17.pair_ref, ...), custom_call_target="tpu_custom_call" | custom-call | tf_op jit(solution)/shard_map/pallas_call | solution.py:777
  116.1 1.5 %copy.15 = f32[128,16]{0,1:T(8,128)} copy(f32[128,16]{1,0:T(8,128)} %get-tuple-element.32) | data formatting | bytes 16384

commit v6 on v5

--- a/solution.py
+++ b/solution.py
@@ -127,11 +127,11 @@
     centre_ref[...] = (jnp.where(row == lane, 1.0, 0.0) - averager).astype(BF16)
     gain_row = gain_ref[...]
     gain = jnp.concatenate([gain_row, gain_row], 1)
-    weight = weight_ref[...]
+    weight = weight_ref[...].astype(F32)
     chooser = (
         lax.broadcasted_iota(jnp.int32, (HEADS, 256), 1) // 16 == lax.broadcasted_iota(jnp.int32, (HEADS, 256), 0)
     ).astype(F32).astype(BF16)
-    wider = dot(weight, chooser)
+    wider = dot(weight.T.astype(BF16), chooser)
     lane_in = lax.rem(lax.broadcasted_iota(jnp.int32, (128, 256), 1), 16)
     for each in range(16):
         weights[each * 128 : (each + 1) * 128, :] = jnp.where(lane_in == each, wider, 0.0).astype(BF16)
@@ -360,57 +360,74 @@
         send_qo(which).wait_send()
     bias_t[...] = jnp.zeros((512, 1024), F32)
 
-    def second_pass(owner, index, block):
-        sample = 2 * owner + index
-
-        def quarter(piece):
-            at = pl.ds(pl.multiple_of(block * 512 + piece * 256, 256), 256)
-            here = pl.ds(pl.multiple_of(piece * 256, 256), 256)
-            after = pl.ds(pl.multiple_of(piece * 256 + 512, 256), 256)
-            peaks = [stats[other, sample, 0:1, at] for other in range(4)]
-            peak = functools.reduce(jnp.maximum, peaks)
-            scale = [jnp.exp2(p - peak) for p in peaks]
-            total = sum(stats[other, sample, 1:2, at] * scale[other] for other in range(4))
-            blend = sum(stats[other, sample, 2:3, at] * scale[other] for other in range(4))
-            share = 1.0 / total
-            mean = blend * share
+    def kin_of(which):
+        across, over = lax.rem(which, 2), which // 2
+        return (high + over - 2 * high * over) * 2 + core + across - 2 * core * across
+
+    def second_pass(owner, block):
+        both = [None, None]
+        for piece in range(2):
+            start = block * 512 + piece * 256
+            at = slice(start, start + 256)
+            scales = []
+            for index in range(2):
+                sample = 2 * owner + index
+                peaks = [stats[other, sample, 0:1, at] for other in range(4)]
+                peak = functools.reduce(jnp.maximum, peaks)
+                scale = [jnp.exp2(p - peak) for p in peaks]
+                total = sum(stats[other, sample, 1:2, at] * scale[other] for other in range(4))
+                blend = sum(stats[other, sample, 2:3, at] * scale[other] for other in range(4))
+                share = 1.0 / total
+                scales.append((peak, share, blend * share))
             for part in range(4):
                 rows = pl.ds(part * 128, 128)
-                factor = jnp.exp2(tops[sample, part : part + 1, at] - peak) * share
-                probs = raised_ref[sample, rows, at] * factor
-                grad = probs * (along_ref[sample, rows, at] - mean)
-                bias_t[rows, at] += grad
-                low_ref[rows, here] = probs.astype(BF16)
-                low_ref[rows, after] = grad.astype(BF16)
-
-        steps(2, quarter)
-        right = qo_rows[sample, block * 512 : block * 512 + 512, :]
-        dv = dot(low_ref[:, :512], right)
-        dk = dot(low_ref[:, 512:1024], right)
-        both = jnp.where(wide < SIZE, dk * inv_root, dv)
-        if block == 0:
-            raised_ref[sample, :, 0:128] = both
-        else:
-            turned = (both + raised_ref[sample, :, 0:128]).T
-            for piece in range(4):
-                packed[2 * sample + piece // 2, piece % 2 * 96 : piece % 2 * 96 + 96, :] = turned[
-                    :96, piece * 128 : piece * 128 + 128
-                ].astype(BF16)
-        dq = (dot(kv_t[sample, :SIZE, :], low_ref[:, 512:1024]) * inv_root).astype(BF16)
-        for piece in range(4):
-            qo[owner, 2 * (block * 4 + piece) + index, :SIZE, :] = dq[:, piece * 128 : piece * 128 + 128]
+                grads = []
+                for index in range(2):
+                    sample = 2 * owner + index
+                    peak, share, mean = scales[index]
+                    factor = jnp.exp2(tops[sample, part : part + 1, at] - peak) * share
+                    probs = raised_ref[sample, rows, at] * factor
+                    grad = probs * (along_ref[sample, rows, at] - mean)
+                    grads.append(grad)
+                    spot = index * 1024 + piece * 256
+                    low_ref[rows, spot : spot + 256] = probs.astype(BF16)
+                    low_ref[rows, spot + 512 : spot + 768] = grad.astype(BF16)
+                bias_t[rows, at] += grads[0] + grads[1]
+            for index in range(2):
+                sample = 2 * owner + index
+                spot = index * 1024 + piece * 256
+                right = qo_rows[sample, at, :]
+                dv = dot(low_ref[:, spot : spot + 256], right)
+                dk = dot(low_ref[:, spot + 512 : spot + 768], right)
+                here = jnp.where(wide < SIZE, dk * inv_root, dv)
+                both[index] = here if piece == 0 else both[index] + here
+                dq = (dot(kv_t[sample, :SIZE, :], low_ref[:, spot + 512 : spot + 768]) * inv_root).astype(BF16)
+                for side in range(2):
+                    qo[owner, 2 * (block * 4 + piece * 2 + side) + index, :SIZE, :] = dq[
+                        :, side * 128 : side * 128 + 128
+                    ]
+        for index in range(2):
+            sample = 2 * owner + index
+            if block == 0:
+                raised_ref[sample, :, 0:128] = both[index]
+            else:
+                turned = (both[index] + raised_ref[sample, :, 0:128]).T
+                for piece in range(4):
+                    packed[2 * sample + piece // 2, piece % 2 * 96 : piece % 2 * 96 + 96, :] = turned[
+                        :96, piece * 128 : piece * 128 + 128
+                    ].astype(BF16)
 
     def send_dq(which, part):
         some = pl.ds(part * 8, 8)
         return remote(
-            qo.at[kin[which], some, pl.ds(0, SIZE)], dq_parts.at[which - 1, some],
-            dq_out.at[part, which], dq_in.at[part, which], kin[which], half, head,
+            qo.at[kin_of(which), some, pl.ds(0, SIZE)], dq_parts.at[which - 1, some],
+            dq_out.at[part, which], dq_in.at[part, which], kin_of(which), half, head,
         )
 
     def send_dkv(which):
         return remote(
-            packed.at[pl.ds(4 * kin[which], 4)], dkv_parts.at[core, half],
-            part_out.at[4 + which], part_in.at[4 + 2 * core + half], kin[which], high, head,
+            packed.at[pl.ds(4 * kin_of(which), 4)], dkv_parts.at[core, half],
+            part_out.at[4 + which], part_in.at[4 + 2 * core + half], kin_of(which), high, head,
         )
 
     keep_dkv = pltpu.make_async_copy(packed.at[pl.ds(4 * samp, 4)], dkv_parts.at[core, half], own_sem.at[7])
@@ -463,18 +480,22 @@
         steps(HEADS, body, 1)
 
     for part in range(2):
-        for which in (2, 3, 1, 0):
-            def one(index):
-                if part == 0:
+        def pair_body(step):
+            which = 3 - step
+            owner = kin_of(which)
+            if part == 0:
+                for index in range(2):
                     for apart in range(1, 4):
-                        stat_copy(2 * kin[which] + index, apart).wait_recv()
-                second_pass(kin[which], index, part)
-
-            steps(2, one)
-            if which:
+                        stat_copy(2 * owner + index, apart).wait_recv()
+            second_pass(owner, part)
+
+            @pl.when(which > 0)
+            def _():
                 if part == 1:
                     send_dkv(which).start()
                 send_dq(which, part).start()
+
+        steps(4, pair_body)
         turn_back(part)
 
     @pl.when(high == half)
@@ -485,7 +506,7 @@
     def _():
         send_dkv(0).start()
 
-    scaled_weight = weight.astype(F32).T * gain_row
+    scaled_weight = weight * gain_row
     scaled_weight = scaled_weight - jnp.mean(scaled_weight, -1, keepdims=True)
     picker = (
         lax.broadcasted_iota(jnp.int32, (256, HEADS), 0) // 16 == lax.broadcasted_iota(jnp.int32, (256, HEADS), 1)
@@ -648,8 +669,8 @@
     for apart in range(1, 8):
         share_group(apart).wait()
     total = sum(group_parts[other] for other in range(8))
-    gain_out[...] = jnp.sum(total * weight.astype(F32).T, 0, keepdims=True)
-    weight_out[...] = (total * gain_row).T
+    gain_out[...] = jnp.sum(total * weight, 0, keepdims=True)
+    weight_out[...] = total * gain_row
     keep_dq.wait()
     keep_last.wait()
     steps(HEADS, lambda step: last_dq(step).wait(), 1)
@@ -671,28 +692,35 @@
 
 
 def deliver_kernel(
-    pair_ref, dq_ref, dkv_ref, weight_ref, gain_ref, pair_out, q_out, k_out, v_out, weight_out, gain_out
+    pair_ref, dq_ref, dkv_ref, weight_ref, gain_ref, pair_out, q_out, k_out, v_out, weight_out, gain_out,
+    held, load_sem, store_sem,
 ):
-    pair_out[...] = pair_ref[...]
-    step = pl.program_id(0)
-
-    @pl.when(step == 0)
-    def _():
-        weight_out[...] = weight_ref[...]
-        gain_out[...] = gain_ref[...]
-
-    for which in range(2):
-        @pl.when(step == which + 1)
-        def _():
+    def load(block):
+        at = pl.ds(block * 8, 8)
+        return pltpu.make_async_copy(pair_ref.at[at], held.at[at], load_sem.at[block])
+
+    def store(block):
+        at = pl.ds(block * 8, 8)
+        return pltpu.make_async_copy(held.at[at], pair_out.at[at], store_sem.at[block])
+
+    for block in range(8):
+        load(block).start()
+    weight_out[...] = weight_ref[...]
+    gain_out[...] = gain_ref[...]
+    odd = lax.rem(lax.axis_index("row"), 2) == 1
+    for block in range(8):
+        load(block).wait()
+        store(block).start()
+        which = block % 2
+        if block // 2 == 0:
             pieces = [dq_ref[each, :, which * SIZE : which * SIZE + SIZE].astype(F32) for each in range(HEADS)]
             q_out[which] = jnp.concatenate(pieces, 1).astype(BF16)
-
-        for at, (out, rows) in enumerate(((k_out, slice(0, SIZE)), (v_out, slice(SIZE, 2 * SIZE)))):
-            @pl.when(step == 3 + 2 * at + which)
-            def _():
-                odd = lax.rem(lax.axis_index("row"), 2) == 1
-                turned = dkv_ref[:, which, rows].reshape(HEADS * SIZE, 128).astype(F32).T
-                out[which] = jnp.where(odd, turned[64:], turned[:64]).astype(BF16)
+        elif block // 2 < 3:
+            out, rows = ((k_out, slice(0, SIZE)), (v_out, slice(SIZE, 2 * SIZE)))[block // 2 - 1]
+            turned = dkv_ref[:, which, rows].reshape(HEADS * SIZE, 128).astype(F32).T
+            out[which] = jnp.where(odd, turned[64:], turned[:64]).astype(BF16)
+    for block in range(8):
+        store(block).wait()
 
 
 def on_device(queries, keys, values, out_grad, pair_repr, norm_gain, bias_weight, token_mask):
@@ -704,7 +732,7 @@
             shape((64, 512, 128)),
             shape((HEADS, 64, 128)),
             shape((HEADS, 2, 96, 128)),
-            shape((128, HEADS), F32),
+            shape((HEADS, 128), F32),
             shape((1, 128), F32),
             shape((16, 512, 128)),
         ),
@@ -771,33 +799,34 @@
         compiler_params=pltpu.CompilerParams(
             collective_id=0, has_side_effects=True, vmem_limit_bytes=63 * MIB
         ),
-    )(*flat, pair_repr, norm_gain.reshape(1, 128), bias_weight, token_mask.reshape(1, 2048))
+    )(*flat, pair_repr, norm_gain.reshape(1, 128), bias_weight.T, token_mask.reshape(1, 2048))
     near_pair, near_dq, near_dkv, near_weight, near_gain, _ = outs
     fixed = lambda *dims: pl.BlockSpec(dims, lambda i: (0,) * len(dims))
     grad_pair, grad_queries, grad_keys, grad_values, grad_weight, grad_gain = pl.pallas_call(
         deliver_kernel,
-        grid=(8,),
+        grid=(1,),
         out_shape=(
             shape((64, 512, 128)),
             shape((2, 64, 768)),
             shape((2, 64, 768)),
             shape((2, 64, 768)),
-            shape((128, HEADS), F32),
+            shape((HEADS, 128), F32),
             shape((1, 128), F32),
         ),
         in_specs=[
-            pl.BlockSpec((8, 512, 128), lambda i: (i, 0, 0)),
+            ANY,
             fixed(HEADS, 64, 128),
             fixed(HEADS, 2, 96, 128),
-            fixed(128, HEADS),
+            fixed(HEADS, 128),
             fixed(1, 128),
         ],
-        out_specs=[pl.BlockSpec((8, 512, 128), lambda i: (i, 0, 0))]
+        out_specs=[ANY]
         + [fixed(2, 64, 768)] * 3
-        + [fixed(128, HEADS), fixed(1, 128)],
+        + [fixed(HEADS, 128), fixed(1, 128)],
+        scratch_shapes=[pltpu.VMEM((64, 512, 128), BF16), sems((8,)), sems((8,))],
         compiler_params=pltpu.CompilerParams(vmem_limit_bytes=60 * MIB),
     )(near_pair, near_dq, near_dkv, near_weight, near_gain)
-    return grad_queries, grad_keys, grad_values, grad_pair, grad_weight, grad_gain.reshape(128)
+    return grad_queries, grad_keys, grad_values, grad_pair, grad_weight.T, grad_gain.reshape(128)
 
 
 def solution(mesh):

time: 118 us -> 112 us (0.949)
  the two profiles are of different devices: /device:TPU:24 before, /device:TPU:10 now
where the time goes in v6:
time: 112 us; the launch traced here: 110 us
  Pallas kernels  109 us (97%)
    pallas_call x1, Pallas kernels, on_device(): pl.pallas_call(kernel, out_shape=(shape((64, 512, 128)), shape((HEADS, 64...  101 us
    pallas_call x1, Pallas kernels, on_device(): pl.pallas_call(deliver_kernel, grid=(1,), out_shape=(shape((64, 512, 128)...  8.43 us

profile of v6, /device:TPU:10, one launch (start us, length us, event | category | flops | bytes accessed | tf_op | source)
XLA Modules:
  0.0 109.9 jit_solution(3456813296044033382)
XLA Ops:
  0.6 100.6 %shard_map.127 = (bf16[64,512,128]{2,1,0:T(8,128)(2,1)}, bf16[16,64,128]{2,1,0:T(8,128)(2,1)}, bf16[16,2,96,128]{3,2,1,0:T(8,128)(2,1)}, f32[16,128]{1,0:T(8,128...) custom-call(bf16[128,768]{1,0:T(8,128)(2,1)} %bitcast.9, bf16[128,768]{1,0:T(8,128)(2,1)} %bitcast.10, ...), custom_call_target="tpu_custom_call" | custom-call | tf_op jit(solution)/shard_map/pallas_call | solution.py:729
  101.3 8.4 %shard_map.128 = (bf16[64,512,128]{2,1,0:T(8,128)(2,1)}, bf16[2,64,768]{2,1,0:T(8,128)(2,1)}, bf16[2,64,768]{2,1,0:T(8,128)(2,1)}, bf16[2,64,768]{2,1,0:T(8,128)...) custom-call(bf16[64,512,128]{2,1,0:T(8,128)(2,1)} %get-tuple-element.17.pair_ref, ...), custom_call_target="tpu_custom_call" | custom-call | tf_op jit(solution)/shard_map/pallas_call | solution.py:805

commit v7 on v6

--- a/solution.py
+++ b/solution.py
@@ -164,7 +164,7 @@
                 old = jnp.where(narrow == 2 * index, inverse[:, :128], inverse_wide[rows, :])
                 inverse_wide[rows, :] = jnp.where(narrow == 2 * index + 1, inverse[:, 128:], old)
 
-        steps(8, couple, unroll=2)
+        steps(8, couple, unroll=4)
         if block == 2:
             spill.start()
         rows = pl.ds(block * 16, 16)
@@ -334,27 +334,31 @@
         stats[samp, sample, 2:3, at] = sum(p[2] * w for p, w in zip(partial, scale))
 
     stats[samp] = jnp.zeros((8, 8, 1024), F32)
-    for part in range(2):
-        turn_bias(part)
-        steps(2, lambda which: first_pass(2 * samp + which, part))
-    for which in range(2):
-        for apart in range(1, 4):
-            stat_copy(2 * samp + which, apart).start()
-
-    for which in range(1, 4):
-        if which != 2:
-            wait_qo(which)
+    def send_stats(owner):
+        for index in range(2):
+            for apart in range(1, 4):
+                stat_copy(2 * owner + index, apart).start()
+
+    turn_bias(0)
+    steps(2, lambda index: first_pass(2 * samp + index, 0))
+    wait_qo(1)
+    wait_kv(kin[1])
+    unpack_qo(kin[1])
+    unpack_kv(kin[1])
+    steps(2, lambda index: first_pass(2 * kin[1] + index, 0))
+    turn_bias(1)
+    steps(2, lambda index: first_pass(2 * samp + index, 1))
+    send_stats(samp)
+    steps(2, lambda index: first_pass(2 * kin[1] + index, 1))
+    send_stats(kin[1])
+    for which in range(2, 4):
+        if which == 3:
+            wait_qo(3)
         wait_kv(kin[which])
         unpack_qo(kin[which])
         unpack_kv(kin[which])
-
-        def one(index):
-            sample = 2 * kin[which] + index
-            steps(2, lambda block: first_pass(sample, block))
-            for apart in range(1, 4):
-                stat_copy(sample, apart).start()
-
-        steps(2, one)
+        steps(4, lambda index: first_pass(2 * kin[which] + index // 2, lax.rem(index, 2)))
+        send_stats(kin[which])
 
     for which in range(1, 4):
         send_qo(which).wait_send()
@@ -481,7 +485,7 @@
 
     for part in range(2):
         def pair_body(step):
-            which = 3 - step
+            which = lax.rem(step + 1, 4) if part == 0 else 3 - step
             owner = kin_of(which)
             if part == 0:
                 for index in range(2):
@@ -561,11 +565,41 @@
                 mixed = mixed + dot(left[:, part * 128 : (part + 1) * 128], low)
             mixed_ref[...] = mixed
 
-        steps(8, couple)
+        steps(8, couple, unroll=2)
         unload(block).start()
+
+    def last_dq(part, step):
+        peer = lax.rem(head + step, HEADS)
+        some = pl.ds(part * 32, 32)
+        return remote(
+            dq_sum.at[peer, some], own_dq.at[head, some],
+            last_out.at[part, step], last_in.at[part, step], samp, half, peer,
+        )
+
+    def keep_dq(part):
+        some = pl.ds(part * 32, 32)
+        return pltpu.make_async_copy(dq_sum.at[head, some], own_dq.at[head, some], own_sem.at[10 + part])
+
+    def sum_dq(part):
+        for which in range(1, 4):
+            send_dq(which, part).wait()
+        for block in range(4):
+            pieces = []
+            for which in range(2):
+                spot = part * 8 + 2 * block + which
+                total = qo[samp, spot, :SIZE, :].astype(F32)
+                for other in range(3):
+                    total = total + dq_parts[other, spot].astype(F32)
+                pieces.append(total)
+            turned = jnp.concatenate(pieces + [filler], 0).T.astype(BF16)
+            for each in range(4):
+                dq_sum[block * 4 + each, part * 32 : part * 32 + 32, :] = turned[each * 32 : each * 32 + 32]
+        steps(HEADS, lambda step: last_dq(part, step).start(), 1)
+        keep_dq(part).start()
 
     wait_back(0)
     pair_block(0)
+    sum_dq(0)
     pair_block(1)
     unload(0).wait()
     reload.start()
@@ -578,28 +612,12 @@
 
     def share(step):
         return remote(
-            mine_ref, plane_parts.at[head], last_out.at[2, step], last_in.at[2, step],
+            mine_ref, plane_parts.at[head], last_out.at[3, step], last_in.at[3, step],
             samp, half, lax.rem(head + step, HEADS),
         )
 
     steps(HEADS, lambda step: share(step).start(), 1)
     plane_parts[head] = mine_ref[...]
-
-    for part in range(2):
-        for which in range(1, 4):
-            send_dq(which, part).wait()
-    for block in range(8):
-        pieces = []
-        for which in range(2):
-            total = qo[samp, 2 * block + which, :SIZE, :].astype(F32)
-            for other in range(3):
-                total = total + dq_parts[other, 2 * block + which].astype(F32)
-            pieces.append(total)
-        turned = jnp.concatenate(pieces + [filler], 0).T.astype(BF16)
-        for each in range(4):
-            dq_sum[block % 4 * 4 + each, block // 4 * 32 : block // 4 * 32 + 32, :] = turned[
-                each * 32 : each * 32 + 32
-            ]
 
     @pl.when(high == half)
     def _():
@@ -634,24 +652,16 @@
                 total = total + dkv_parts[piece, 1, spot[0], spot[1], :].astype(F32)
                 dkv_sum[piece * 4 + block, which] = total.astype(BF16)
 
-    def last_dq(step):
-        peer = lax.rem(head + step, HEADS)
-        return remote(
-            dq_sum.at[peer], own_dq.at[head], last_out.at[0, step], last_in.at[0, step], samp, half, peer
-        )
-
     def last_dkv(step):
         peer = lax.rem(head + step, HEADS)
         return remote(
-            dkv_sum.at[peer // 2], own_dkv.at[head], last_out.at[1, step], last_in.at[1, step], samp, half, peer
-        )
-
-    steps(HEADS, lambda step: last_dq(step).start(), 1)
+            dkv_sum.at[peer // 2], own_dkv.at[head], last_out.at[2, step], last_in.at[2, step], samp, half, peer
+        )
+
     steps(HEADS, lambda step: last_dkv(step).start(), 1)
-    keep_dq = pltpu.make_async_copy(dq_sum.at[head], own_dq.at[head], own_sem.at[10])
-    keep_last = pltpu.make_async_copy(dkv_sum.at[head // 2], own_dkv.at[head], own_sem.at[11])
-    keep_dq.start()
+    keep_last = pltpu.make_async_copy(dkv_sum.at[head // 2], own_dkv.at[head], own_sem.at[12])
     keep_last.start()
+    sum_dq(1)
 
     steps(HEADS, lambda step: share(step).wait(), 1)
     spot = samp * 2 + half
@@ -671,9 +681,10 @@
     total = sum(group_parts[other] for other in range(8))
     gain_out[...] = jnp.sum(total * weight, 0, keepdims=True)
     weight_out[...] = total * gain_row
-    keep_dq.wait()
     keep_last.wait()
-    steps(HEADS, lambda step: last_dq(step).wait(), 1)
+    for part in range(2):
+        keep_dq(part).wait()
+        steps(HEADS, lambda step: last_dq(part, step).wait(), 1)
     steps(HEADS, lambda step: last_dkv(step).wait(), 1)
     for part in range(2):
         send_kv(part, 1).wait_send()
@@ -776,7 +787,7 @@
             pltpu.VMEM((8, HEADS, 128), F32),
             sems((4,)),
             sems((2,)),
-            sems((12,)),
+            sems((13,)),
             sems((2, 16)),
             sems((2, 16)),
             sems((4, 16)),
@@ -791,8 +802,8 @@
             sems((8,)),
             sems((2, 16)),
             sems((2, 16)),
-            sems((3, 16)),
-            sems((3, 16)),
+            sems((4, 16)),
+            sems((4, 16)),
             sems((8,)),
             sems((8,)),
         ],

time: 112 us -> 113 us (level); the launches traced: 110 us -> 112 us
  Pallas kernels: 109 us -> 112 us
    pallas_call x1, Pallas kernels: 101 us -> 103 us  [on_device(): pl.pallas_call(kernel, out_shape=(shape((64, 512, 128)), shape((HEADS, 64...]
where the time goes in v7:
time: 113 us; the launch traced here: 112 us
  Pallas kernels  112 us (99%)
    pallas_call x1, Pallas kernels, on_device(): pl.pallas_call(kernel, out_shape=(shape((64, 512, 128)), shape((HEADS, 64...  103 us
    pallas_call x1, Pallas kernels, on_device(): pl.pallas_call(deliver_kernel, grid=(1,), out_shape=(shape((64, 512, 128)...  8.43 us

profile of v7, /device:TPU:10, one launch (start us, length us, event | category | flops | bytes accessed | tf_op | source)
XLA Modules:
  0.0 112.5 jit_solution(17971274651419499564)
XLA Ops:
  0.6 103.3 %shard_map.127 = (bf16[64,512,128]{2,1,0:T(8,128)(2,1)}, bf16[16,64,128]{2,1,0:T(8,128)(2,1)}, bf16[16,2,96,128]{3,2,1,0:T(8,128)(2,1)}, f32[16,128]{1,0:T(8,128...) custom-call(bf16[128,768]{1,0:T(8,128)(2,1)} %bitcast.9, bf16[128,768]{1,0:T(8,128)(2,1)} %bitcast.10, ...), custom_call_target="tpu_custom_call" | custom-call | tf_op jit(solution)/shard_map/pallas_call | solution.py:740
  103.9 8.4 %shard_map.128 = (bf16[64,512,128]{2,1,0:T(8,128)(2,1)}, bf16[2,64,768]{2,1,0:T(8,128)(2,1)}, bf16[2,64,768]{2,1,0:T(8,128)(2,1)}, bf16[2,64,768]{2,1,0:T(8,128)...) custom-call(bf16[64,512,128]{2,1,0:T(8,128)(2,1)} %get-tuple-element.17.pair_ref, ...), custom_call_target="tpu_custom_call" | custom-call | tf_op jit(solution)/shard_map/pallas_call | solution.py:816

commit v8 on v7

--- a/solution.py
+++ b/solution.py
@@ -171,23 +171,23 @@
         bias[:, rows, :] = dot(low_ref[...], weights[...]).T.reshape(HEADS, 16, 512).astype(BF16)
         inverse_ref[rows, :] = inverse_wide[...].T[:16]
 
-    def bias_rows(block):
-        return pl.ds(pl.multiple_of(block // 2 * 512 + head * 32 + block % 2 * 16, 16), 16)
-
-    def copy_bias(block, step):
-        return remote(
-            bias.at[lax.rem(head + step, HEADS), pl.ds(block * 16, 16)], all_bias.at[bias_rows(block)],
-            bias_out.at[block, step], bias_in.at[block, step], samp, half, lax.rem(head + step, HEADS),
-        )
-
-    def keep_bias(block):
+    def bias_rows(part):
+        return pl.ds(pl.multiple_of(part * 512 + head * 32, 32), 32)
+
+    def copy_bias(part, step):
+        return remote(
+            bias.at[lax.rem(head + step, HEADS), pl.ds(part * 32, 32)], all_bias.at[bias_rows(part)],
+            bias_out.at[part, step], bias_in.at[part, step], samp, half, lax.rem(head + step, HEADS),
+        )
+
+    def keep_bias(part):
         return pltpu.make_async_copy(
-            bias.at[head, pl.ds(block * 16, 16)], all_bias.at[bias_rows(block)], own_sem.at[2 + block]
-        )
-
-    def start_bias(block):
-        steps(HEADS, lambda step: copy_bias(block, step).start(), 1)
-        keep_bias(block).start()
+            bias.at[head, pl.ds(part * 32, 32)], all_bias.at[bias_rows(part)], own_sem.at[2 + part]
+        )
+
+    def start_bias(part):
+        steps(HEADS, lambda step: copy_bias(part, step).start(), 1)
+        keep_bias(part).start()
 
     def send_kv(part, across):
         return remote(
@@ -230,7 +230,6 @@
         ).wait_recv()
 
     norm_block(0)
-    start_bias(0)
     steps(HEADS, lambda step: copy_pack(step, 0).wait(), 1)
     own_kv.wait()
     for part in range(2):
@@ -246,13 +245,12 @@
             send_kv(part, 0).start()
 
     norm_block(1)
-    start_bias(1)
+    start_bias(0)
     steps(HEADS, lambda step: copy_pack(step, 1).wait(), 1)
     own_qo.wait()
     send_qo(2).start()
     send_qo(1).start()
     norm_block(2)
-    start_bias(2)
     spill.wait()
     load(3).start()
 
@@ -267,7 +265,7 @@
                     start = which * 64 + part * 32
                     qo_rows[2 * owner + which, at, :] = filled[start : start + 32]
 
-        steps(HEADS, body, unroll=2)
+        steps(HEADS, body, unroll=8)
 
     def unpack_kv(owner):
         def body(pair):
@@ -278,27 +276,26 @@
                 kv_t[2 * owner + which, :, at] = filled.astype(BF16)
                 kv_rows[2 * owner + which, at, :] = filled.T.astype(BF16)
 
-        steps(4, body, unroll=2)
+        steps(4, body, unroll=4)
 
     unpack_qo(samp)
     norm_block(3)
-    start_bias(3)
+    start_bias(1)
     wait_qo(2)
     send_qo(3).start()
     wait_kv(samp)
     unpack_kv(samp)
 
     def turn_bias(part):
-        for block in (2 * part, 2 * part + 1):
-            keep_bias(block).wait()
-            steps(HEADS, lambda step: copy_bias(block, step).wait(), 1)
+        keep_bias(part).wait()
+        steps(HEADS, lambda step: copy_bias(part, step).wait(), 1)
 
         def body(block):
             at = pl.ds(pl.multiple_of(part * 512 + block * 128, 128), 128)
             turned = all_bias[at, :].astype(F32).T * LOG2E
             bias_t[:, at] = jnp.where(keep_ref[...] > 0, turned, MASKED)
 
-        steps(4, body)
+        steps(4, body, unroll=4)
 
     def stat_copy(sample, apart):
         return remote(
@@ -424,9 +421,16 @@
     def send_dq(which, part):
         some = pl.ds(part * 8, 8)
         return remote(
-            qo.at[kin_of(which), some, pl.ds(0, SIZE)], dq_parts.at[which - 1, some],
-            dq_out.at[part, which], dq_in.at[part, which], kin_of(which), half, head,
-        )
+            qo.at[kin[which], some, pl.ds(0, SIZE)], dq_parts.at[which - 1, some],
+            dq_out.at[part, which], dq_in.at[part, which], kin[2 if which == 2 else 1], half, head,
+        )
+
+    def merge_dq(part):
+        send_dq(3, part).wait_recv()
+        for spot in range(part * 8, part * 8 + 8):
+            total = qo[kin[2], spot, :SIZE, :].astype(F32) + dq_parts[2, spot].astype(F32)
+            qo[kin[2], spot, :SIZE, :] = total.astype(BF16)
+        send_dq(2, part).start()
 
     def send_dkv(which):
         return remote(
@@ -493,11 +497,19 @@
                         stat_copy(2 * owner + index, apart).wait_recv()
             second_pass(owner, part)
 
-            @pl.when(which > 0)
+            for side in (1, 3):
+                @pl.when(which == side)
+                def _():
+                    send_dq(side, part).start()
+
+            if part == 1:
+                @pl.when(which > 0)
+                def _():
+                    send_dkv(which).start()
+
+            @pl.when(step == 3 - part)
             def _():
-                if part == 1:
-                    send_dkv(which).start()
-                send_dq(which, part).start()
+                merge_dq(part)
 
         steps(4, pair_body)
         turn_back(part)
@@ -581,14 +593,15 @@
         return pltpu.make_async_copy(dq_sum.at[head, some], own_dq.at[head, some], own_sem.at[10 + part])
 
     def sum_dq(part):
-        for which in range(1, 4):
+        for which in range(1, 3):
             send_dq(which, part).wait()
+        send_dq(3, part).wait_send()
         for block in range(4):
             pieces = []
             for which in range(2):
                 spot = part * 8 + 2 * block + which
                 total = qo[samp, spot, :SIZE, :].astype(F32)
-                for other in range(3):
+                for other in range(2):
                     total = total + dq_parts[other, spot].astype(F32)
                 pieces.append(total)
             turned = jnp.concatenate(pieces + [filler], 0).T.astype(BF16)
@@ -703,8 +716,8 @@
 
 
 def deliver_kernel(
-    pair_ref, dq_ref, dkv_ref, weight_ref, gain_ref, pair_out, q_out, k_out, v_out, weight_out, gain_out,
-    held, load_sem, store_sem,
+    pair_ref, near_dq, near_dkv, weight_ref, gain_ref, pair_out, q_out, k_out, v_out, weight_out, gain_out,
+    held, dq_ref, dkv_ref, load_sem, store_sem, token_sem,
 ):
     def load(block):
         at = pl.ds(block * 8, 8)
@@ -714,7 +727,12 @@
         at = pl.ds(block * 8, 8)
         return pltpu.make_async_copy(held.at[at], pair_out.at[at], store_sem.at[block])
 
-    for block in range(8):
+    load_dq = pltpu.make_async_copy(near_dq, dq_ref, token_sem.at[0])
+    load_dkv = pltpu.make_async_copy(near_dkv, dkv_ref, token_sem.at[1])
+    load(0).start()
+    load_dq.start()
+    load_dkv.start()
+    for block in range(1, 8):
         load(block).start()
     weight_out[...] = weight_ref[...]
     gain_out[...] = gain_ref[...]
@@ -723,6 +741,10 @@
         load(block).wait()
         store(block).start()
         which = block % 2
+        if block == 0:
+            load_dq.wait()
+        if block == 2:
+            load_dkv.wait()
         if block // 2 == 0:
             pieces = [dq_ref[each, :, which * SIZE : which * SIZE + SIZE].astype(F32) for each in range(HEADS)]
             q_out[which] = jnp.concatenate(pieces, 1).astype(BF16)
@@ -790,8 +812,8 @@
             sems((13,)),
             sems((2, 16)),
             sems((2, 16)),
-            sems((4, 16)),
-            sems((4, 16)),
+            sems((2, 16)),
+            sems((2, 16)),
             sems((8,)),
             sems((8,)),
             sems((8, 4)),
@@ -826,15 +848,22 @@
         ),
         in_specs=[
             ANY,
-            fixed(HEADS, 64, 128),
-            fixed(HEADS, 2, 96, 128),
+            ANY,
+            ANY,
             fixed(HEADS, 128),
             fixed(1, 128),
         ],
         out_specs=[ANY]
         + [fixed(2, 64, 768)] * 3
         + [fixed(HEADS, 128), fixed(1, 128)],
-        scratch_shapes=[pltpu.VMEM((64, 512, 128), BF16), sems((8,)), sems((8,))],
+        scratch_shapes=[
+            pltpu.VMEM((64, 512, 128), BF16),
+            pltpu.VMEM((HEADS, 64, 128), BF16),
+            pltpu.VMEM((HEADS, 2, 96, 128), BF16),
+            sems((8,)),
+            sems((8,)),
+            sems((2,)),
+        ],
         compiler_params=pltpu.CompilerParams(vmem_limit_bytes=60 * MIB),
     )(near_pair, near_dq, near_dkv, near_weight, near_gain)
     return grad_queries, grad_keys, grad_values, grad_pair, grad_weight.T, grad_gain.reshape(128)

time: 113 us -> 110 us (0.973)
  Pallas kernels: 112 us -> 109 us
    pallas_call x1, Pallas kernels: 103 us -> 101 us  [on_device(): pl.pallas_call(kernel, out_shape=(shape((64, 512, 128)), shape((HEADS, 64...]
where the time goes in v8:
time: 110 us; the launch traced here: 109 us
  Pallas kernels  109 us (99%)
    pallas_call x1, Pallas kernels, on_device(): pl.pallas_call(kernel, out_shape=(shape((64, 512, 128)), shape((HEADS, 64...  101 us
    pallas_call x1, Pallas kernels, on_device(): pl.pallas_call(deliver_kernel, grid=(1,), out_shape=(shape((64, 512, 128)...  7.99 us

profile of v8, /device:TPU:10, one launch (start us, length us, event | category | flops | bytes accessed | tf_op | source)
XLA Modules:
  0.0 109.4 jit_solution(13835105925011120650)
XLA Ops:
  0.6 100.7 %shard_map.127 = (bf16[64,512,128]{2,1,0:T(8,128)(2,1)}, bf16[16,64,128]{2,1,0:T(8,128)(2,1)}, bf16[16,2,96,128]{3,2,1,0:T(8,128)(2,1)}, f32[16,128]{1,0:T(8,128...) custom-call(bf16[128,768]{1,0:T(8,128)(2,1)} %bitcast.9, bf16[128,768]{1,0:T(8,128)(2,1)} %bitcast.10, ...), custom_call_target="tpu_custom_call" | custom-call | tf_op jit(solution)/shard_map/pallas_call | solution.py:762
  101.3 8.0 %shard_map.128 = (bf16[64,512,128]{2,1,0:T(8,128)(2,1)}, bf16[2,64,768]{2,1,0:T(8,128)(2,1)}, bf16[2,64,768]{2,1,0:T(8,128)(2,1)}, bf16[2,64,768]{2,1,0:T(8,128)...) custom-call(bf16[64,512,128]{2,1,0:T(8,128)(2,1)} %get-tuple-element.17.pair_ref, ...), custom_call_target="tpu_custom_call" | custom-call | tf_op jit(solution)/shard_map/pallas_call | solution.py:838
